TPU v7x, 32 devices: a whole 2x2x4 slice. The times are simulated.
32 devices in a mesh: mem: 8 (over y, x, core), lat: 4 (over z).
Axes of the slice: x: 2, y: 2, z: 4, core: 2. Of those that a mesh axis runs over, the one named last changes fastest.
Arguments:
- ensemble: float32 [256, 4, 16, 1024], P('mem', None, 'lat'), may hold values from -6 to 6
- obs_value: float32 [1, 32, 16], P(None, ('mem', 'lat')), may hold values from -9 to 9
- obs_var: float32 [1, 32, 16], P(None, ('mem', 'lat')), may hold values from 0.5 to 4
- obs_cell: int32 [1, 32, 16], P(None, ('mem', 'lat')), may hold values from 0 to 2047
- obs_loop: int32 [1, 32, 16], P(None, ('mem', 'lat')), may hold values from 0 to 3
- obs_count: int32 [1, 32], P(None, ('mem', 'lat')), may hold values from 8 to 16, as said below
Outputs:
- analysis: float32 [256, 4, 16, 1024], P('mem', None, 'lat')
Inputs may be any that keep to these rules, and one draw needn't show every extreme that they name: `obs_count`: at least 8 and at most 16 slots live per patch; in each cycle some patch has all 16 slots live and another exactly 8.
All inputs are finite; a program needn't handle non-finite values.
Results may differ from a plain program's by a relative error of at most 0.0003.
Values sent between devices are 32-bit elements; how exact they have to be, the bound alone decides.
No kernel may reach another device: no remote copies, remote signals or barrier semaphores. Data moves between devices by JAX's collectives and lax.ppermute only.
A program may use at most 64 MiB of HBM per device.

v0:
```python
import jax
import jax.numpy as jnp
from jax import lax
from jax.sharding import PartitionSpec as P

NSI = 5


time_step = 0.15
viscosity = 0.1
third_part = 1.0 / 3.0
two_thirds = 2.0 / 3.0


def with_halo(cells, sides, width):
    for axis, dim in sides:
        count = lax.axis_size(axis)
        ends = count - 1
        head = lax.slice_in_dim(cells, 0, width, axis=dim)
        tail = lax.slice_in_dim(cells, cells.shape[dim] - width, cells.shape[dim], axis=dim)
        cells = jnp.concatenate(
            [
                lax.ppermute(tail, axis, [(i, (i + 1) % count) for i in range(ends)]),
                cells,
                lax.ppermute(head, axis, [((i + 1) % count, i) for i in range(ends)]),
            ],
            axis=dim,
        )
    return cells


def tendency(padded):
    centre = padded[:, :, 1:-1, 1:-1]
    to_north = padded[:, :, 2:, 1:-1]
    to_south = padded[:, :, :-2, 1:-1]
    to_east = padded[:, :, 1:-1, 2:]
    to_west = padded[:, :, 1:-1, :-2]
    zonal_wind = centre[:, 0:1]
    meridional = centre[:, 1:2]
    moved = zonal_wind * (to_east - to_west) * 0.5 + meridional * (to_north - to_south) * 0.5
    return -moved + viscosity * (to_north + to_south + to_east + to_west - 4.0 * centre)


def widen(state, width):
    widened = with_halo(state, (("lat", 2),), width)
    return jnp.concatenate([widened[..., -width:], widened, widened[..., :width]], axis=3)


def advance_single(state):
    first = state + time_step * tendency(widen(state, 1))
    second = 0.75 * state + 0.25 * (first + time_step * tendency(widen(first, 1)))
    return third_part * state + two_thirds * (second + time_step * tendency(widen(second, 1)))


def analyse(cells, values, variance, slot_cell, slot_loop, count):
    members = cells.shape[0]
    highest = lax.Precision.HIGHEST
    centre_mean = jnp.mean(cells, axis=0)
    perturb = cells - centre_mean
    seen = jnp.take(cells, slot_cell, axis=1)
    seen_mean = jnp.mean(seen, axis=0)
    seen_pert = seen - seen_mean
    slots = jnp.arange(slot_cell.shape[0], dtype=jnp.int32)
    weight = jnp.where(
        slots < count, jnp.exp(-0.35 * slot_loop.astype(cells.dtype)) / variance, 0.0
    )
    scaled = seen_pert * weight
    gram = jnp.dot(scaled, seen_pert.T, precision=highest)
    drive = jnp.dot(scaled, values - seen_mean, precision=highest)
    identity = jnp.eye(members, dtype=cells.dtype)
    bound = members - 1.0 + 0.5 * jnp.trace(gram)
    root_up = ((members - 1.0) * identity + gram) / bound
    root_down = identity
    for repeat in range(NSI):
        factor = 1.5 * identity - 0.5 * jnp.dot(root_down, root_up, precision=highest)
        root_up = jnp.dot(root_up, factor, precision=highest)
        root_down = jnp.dot(factor, root_down, precision=highest)
    spread = root_down * jnp.sqrt((members - 1.0) / bound)
    centre_shift = (
        jnp.dot(root_down, jnp.dot(root_down, drive, precision=highest), precision=highest) / bound
    )
    transform = spread + centre_shift[:, None]
    return centre_mean + jnp.dot(transform.T, perturb, precision=highest)


def per_device(ensemble, obs_value, obs_var, obs_cell, obs_loop, obs_count):
    state = ensemble
    state = advance_single(state)
    state = lax.all_to_all(state, "mem", split_axis=3, concat_axis=0, tiled=True)
    members, fields, band_rows, lon_part = state.shape
    cells = state.reshape(members, fields * band_rows * lon_part)
    updated = analyse(
        cells, obs_value[0, 0], obs_var[0, 0], obs_cell[0, 0], obs_loop[0, 0], obs_count[0, 0]
    )
    state = updated.reshape(members, fields, band_rows, lon_part)
    state = lax.all_to_all(state, "mem", split_axis=0, concat_axis=3, tiled=True)
    return state


def solution(mesh):
    placed = (
        P("mem", None, "lat", None),
        P(None, ("mem", "lat"), None),
        P(None, ("mem", "lat"), None),
        P(None, ("mem", "lat"), None),
        P(None, ("mem", "lat"), None),
        P(None, ("mem", "lat")),
    )
    return jax.shard_map(
        per_device,
        mesh=mesh,
        in_specs=placed,
        out_specs=P("mem", None, "lat", None),
        check_vma=False,
    )
```

profile of v0, /device:TPU:0, one launch (start us, length us, event | category | flops | bytes accessed | tf_op | source)
XLA Modules:
  0.0 189.7 jit_solution(7955677220711514687)
XLA Ops:
  0.0 2.8 %copy.25 = f32[32,4,4,1024]{3,0,2,1:T(8,128)S(1)} copy(f32[32,4,4,1024]{3,2,1,0:T(4,128)} %param.6) | data formatting | bytes 4194304 | tf_op args[0]
  2.9 5.1 %collective-permute-start = (f32[32,4,1,1024]{3,0,2,1:T(8,128)S(1)}, f32[32,4,1,1024]{3,0,2,1:T(8,128)S(1)}, u32[]{:S(2)}, u32[]{:S(2)}) collective-permute-start(f32[32,4,1,1024]{3,0,2,1:T(8,128)S(1)} %get-tuple-element.17), channel_id=1, source_target_pairs={{0,1},{1,2},{2,3},{4,5},{5,6},{6,7},{8,9},{9,10},{10,11},{12,13},{... | collective-permute-start | bytes 1572872 | tf_op jit(solution)/shard_map/ppermute | solution.py:23
  8.0 1.3 collective-permute-start.1
  10.0 9.1 %collective-permute-done = f32[32,4,1,1024]{3,0,2,1:T(8,128)S(1)} collective-permute-done((f32[32,4,1,1024]{3,0,2,1:T(8,128)S(1)}, f32[32,4,1,1024]{3,0,2,1:T(8,128)S(1)}, u32[]{:S(2)}, u32[]{:S(2)}) %collective-permute-start) | collective-permute-done | bytes 524320 | tf_op jit(solution)/shard_map/ppermute | solution.py:23
  19.2 1.2 constant_dynamic-update-slice_fusion.1
  20.4 2.9 %collective-permute-done.1 = f32[32,4,1,1024]{3,0,2,1:T(8,128)S(1)} collective-permute-done((f32[32,4,1,1024]{3,0,2,1:T(8,128)S(1)}, f32[32,4,1,1024]{3,0,2,1:T(8,128)S(1)}, u32[]{:S(2)}, u32[]{:S(2)}) %collective-permute-start.1) | collective-permute-done | bytes 524320 | tf_op jit(solution)/shard_map/ppermute | solution.py:25
  23.5 1.8 multiply_add_fusion.2
  25.4 3.5 %collective-permute-start.2 = (f32[32,4,1,1024]{3,0,2,1:T(8,128)S(1)}, f32[32,4,1,1024]{3,0,2,1:T(8,128)S(1)}, u32[]{:S(2)}, u32[]{:S(2)}) collective-permute-start(f32[32,4,1,1024]{3,0,2,1:T(8,128)S(1)} %get-tuple-element.13), channel_id=1, source_target_pairs={{0,1},{1,2},{2,3},{4,5},{5,6},{6,7},{8,9},{9,10},{10,11},{12,13},{... | collective-permute-start | bytes 1572872 | tf_op jit(solution)/shard_map/ppermute | solution.py:23
  28.9 1.3 collective-permute-start.3
  30.3 8.5 %collective-permute-done.2 = f32[32,4,1,1024]{3,0,2,1:T(8,128)S(1)} collective-permute-done((f32[32,4,1,1024]{3,0,2,1:T(8,128)S(1)}, f32[32,4,1,1024]{3,0,2,1:T(8,128)S(1)}, u32[]{:S(2)}, u32[]{:S(2)}) %collective-permute-start.2) | collective-permute-done | bytes 524320 | tf_op jit(solution)/shard_map/ppermute | solution.py:23
  38.9 4.1 %collective-permute-done.3 = f32[32,4,1,1024]{3,0,2,1:T(8,128)S(1)} collective-permute-done((f32[32,4,1,1024]{3,0,2,1:T(8,128)S(1)}, f32[32,4,1,1024]{3,0,2,1:T(8,128)S(1)}, u32[]{:S(2)}, u32[]{:S(2)}) %collective-permute-start.3) | collective-permute-done | bytes 524320 | tf_op jit(solution)/shard_map/ppermute | solution.py:25
  43.0 3.1 %multiply_add_fusion.1 = f32[32,4,4,1024]{3,0,2,1:T(8,128)S(1)} fusion(f32[32,4,4,1024]{3,0,2,1:T(8,128)S(1)} %multiply_add_fusion.2, f32[32,4,1,1024]{3,0,2,1:T(8,128)S(1)} %collective-permute-done.3, f32[32,4,1,1024]{3,0,2,1:T(8,128)S(1)} %collective-permute-done.2, f32[32,4,1024]{2,0,1:T(8,128)S(1)} %get-tuple-element.12, ...), kind=kLoop, calls=%fused_computation.33 | loop fusion | flops 16252928 | bytes 8388608 | tf_op jit(solution)/shard_map/add | solution.py:51
  46.2 3.5 %collective-permute-start.4 = (f32[32,4,1,1024]{3,0,2,1:T(8,128)S(1)}, f32[32,4,1,1024]{3,0,2,1:T(8,128)S(1)}, u32[]{:S(2)}, u32[]{:S(2)}) collective-permute-start(f32[32,4,1,1024]{3,0,2,1:T(8,128)S(1)} %get-tuple-element.9), channel_id=1, source_target_pairs={{0,1},{1,2},{2,3},{4,5},{5,6},{6,7},{8,9},{9,10},{10,11},{12,13},{... | collective-permute-start | bytes 1572872 | tf_op jit(solution)/shard_map/ppermute | solution.py:23
  49.7 1.3 collective-permute-start.5
  51.2 7.3 %collective-permute-done.4 = f32[32,4,1,1024]{3,0,2,1:T(8,128)S(1)} collective-permute-done((f32[32,4,1,1024]{3,0,2,1:T(8,128)S(1)}, f32[32,4,1,1024]{3,0,2,1:T(8,128)S(1)}, u32[]{:S(2)}, u32[]{:S(2)}) %collective-permute-start.4) | collective-permute-done | bytes 524320 | tf_op jit(solution)/shard_map/ppermute | solution.py:23
  58.5 4.1 %collective-permute-done.5 = f32[32,4,1,1024]{3,0,2,1:T(8,128)S(1)} collective-permute-done((f32[32,4,1,1024]{3,0,2,1:T(8,128)S(1)}, f32[32,4,1,1024]{3,0,2,1:T(8,128)S(1)}, u32[]{:S(2)}, u32[]{:S(2)}) %collective-permute-start.5) | collective-permute-done | bytes 524320 | tf_op jit(solution)/shard_map/ppermute | solution.py:25
  62.6 3.1 %multiply_add_fusion = f32[32,4,4,1024]{3,0,2,1:T(8,128)S(1)} fusion(f32[32,4,4,1024]{3,0,2,1:T(8,128)S(1)} %multiply_add_fusion.1, f32[32,4,1,1024]{3,0,2,1:T(8,128)S(1)} %collective-permute-done.5, f32[32,4,1,1024]{3,0,2,1:T(8,128)S(1)} %collective-permute-done.4, f32[32,4,1024]{2,0,1:T(8,128)S(1)} %get-tuple-element.8, ...), kind=kLoop, calls=%fused_computation.32 | loop fusion | flops 16252928 | bytes 8388608 | tf_op jit(solution)/shard_map/add | solution.py:52
  65.8 6.2 %copy.36 = f32[32,4,4,1024]{0,2,1,3:T(4,128)} copy(f32[32,4,4,1024]{3,0,2,1:T(8,128)S(1)} %multiply_add_fusion) | data formatting | bytes 4194304 | tf_op jit(solution)/shard_map/add | solution.py:52
  72.0 9.5 %reshape.92 = f32[8,1,65536]{2,1,0:T(1,128)} reshape(f32[1024,4,4,32]{3,2,1,0:T(4,128)} %bitcast.80) | data formatting | bytes 4194304
  81.4 3.9 %all-to-all-start = ((f32[8,1,65536]{2,1,0:T(1,128)}), f32[8,1,65536]{2,1,0:T(1,128)S(1)}, u32[]{:S(2)}, u32[]{:S(2)}) async-start(f32[8,1,65536]{2,1,0:T(1,128)} %reshape.92), calls=%async_computation | async-start | bytes 4194304 | tf_op jit(solution)/shard_map/all_to_all | solution.py:89
  86.1 25.9 %all-to-all-done = f32[8,1,65536]{2,1,0:T(1,128)S(1)} async-done(((f32[8,1,65536]{2,1,0:T(1,128)}), f32[8,1,65536]{2,1,0:T(1,128)S(1)}, u32[]{:S(2)}, u32[]{:S(2)}) %all-to-all-start) | async-done | bytes 2097184 | tf_op jit(solution)/shard_map/all_to_all | solution.py:89
  111.9 1.3 copy-done.2
  113.3 0.5 broadcast.192
  113.8 7.2 %reduce.2 = f32[8,65536]{1,0:T(8,128)S(1)} reduce(f32[8,1,65536]{2,1,0:T(1,128)} %copy-done.2, f32[]{:T(128)} %broadcast.192), dimensions={1}, to_apply=%all_to_all.24.reduce_sub_computation | reduce | bytes 4194308 | tf_op jit(solution)/shard_map/all_to_all | solution.py:89
  121.0 7.6 %reshape.93 = f32[1024,4,4,32]{3,2,1,0:T(4,128)} reshape(f32[8,65536]{1,0:T(8,128)S(1)} %reduce.2) | data formatting | bytes 4194304
  128.6 7.5 %copy.37 = f32[32,4,4,8,128]{4,2,1,0,3:T(4,128)S(1)} copy(f32[32,4,4,8,128]{0,2,1,4,3:T(4,128)} %bitcast.81) | data formatting | bytes 4194304 | tf_op jit(solution)/shard_map/all_to_all | solution.py:89
  136.1 1.8 reshape.76
  138.0 2.9 %copy.38 = f32[256,2048]{0,1:T(8,128)} copy(f32[256,2048]{1,0:T(8,128)} %reshape.76) | data formatting | bytes 4194304 | tf_op jit(solution)/shard_map/reshape | solution.py:91
  140.9 2.2 %gather_fusion = f32[16,256]{1,0:T(8,128)S(1)} fusion(f32[256,2048]{0,1:T(8,128)} %copy.38, s32[1024]{0:T(1024)S(1)} %pad_clamp_fusion), kind=kCustom, calls=%fused_computation | custom fusion | bytes 32832 | tf_op jit(solution)/shard_map/jit(_take)/gather | solution.py:60
  143.3 1.1 select_reduce_fusion
  145.0 0.3 fusion.9
  145.4 0.4 fusion.16
  146.1 0.4 fusion.8
  146.5 0.4 fusion.44
  146.8 0.4 fusion.43
  147.2 0.4 fusion.7
  147.6 0.4 fusion.46
  148.0 0.4 fusion.45
  148.4 0.4 fusion.6
  148.8 0.4 fusion.48
  149.2 0.4 fusion.47
  150.2 0.4 fusion.5
  150.6 0.4 fusion.49
  151.7 3.3 %convolution_add_fusion = f32[256,2048]{1,0:T(8,128)} fusion(f32[256,2048]{1,0:T(8,128)S(1)} %copy-done.1, f32[2048]{0:T(1024)S(1)} %bitcast.85, f32[256,256]{1,0:T(8,128)S(1)} %fusion.49, f32[256]{0:T(256)S(1)} %broadcast_divide_fusion, f32[]{:T(128)S(6)} %sqrt.3), kind=kOutput, calls=%fused_computation.1 | convolution fusion | flops 1611792384 | bytes 4465668 | tf_op jit(solution)/shard_map/dot_general | solution.py:83
  155.0 2.7 %reshape.77 = f32[256,4,4,128]{3,2,1,0:T(4,128)S(1)} reshape(f32[256,2048]{1,0:T(8,128)} %convolution_add_fusion) | data formatting | bytes 4194304 | tf_op jit(solution)/shard_map/reshape | solution.py:95
  157.7 29.0 %all_to_all.33 = f32[256,4,4,128]{3,2,1,0:T(4,128)S(1)} all-to-all(f32[256,4,4,128]{3,2,1,0:T(4,128)S(1)} %reshape.77), channel_id=1, replica_groups=mesh['mem'=8,'lat'=4] {'mem'}, dimensions={0} | all-to-all | bytes 4194304 | tf_op jit(solution)/shard_map/all_to_all | solution.py:96
  186.7 1.2 copy.44
  187.9 1.7 all_to_all.30
  (36 shorter events, 3.1 us)
Async XLA Ops:
  2.8 6.5 %copy-start = (f32[32,4,4,1024]{3,2,1,0:T(4,128)S(1)}, f32[32,4,4,1024]{3,2,1,0:T(4,128)}, u32[]{:S(2)}) copy-start(f32[32,4,4,1024]{3,2,1,0:T(4,128)} %param.6) | copy-start | bytes 6291460
  2.9 16.2 %collective-permute-start = (f32[32,4,1,1024]{3,0,2,1:T(8,128)S(1)}, f32[32,4,1,1024]{3,0,2,1:T(8,128)S(1)}, u32[]{:S(2)}, u32[]{:S(2)}) collective-permute-start(f32[32,4,1,1024]{3,0,2,1:T(8,128)S(1)} %get-tuple-element.17), channel_id=1, source_target_pairs={{0,1},{1,2},{2,3},{4,5},{5,6},{6,7},{8,9},{9,10},{10,11},{12,13},{... | collective-permute-start | bytes 1572872 | tf_op jit(solution)/shard_map/ppermute | solution.py:23
  8.0 15.3 %collective-permute-start.1 = (f32[32,4,1,1024]{3,0,2,1:T(8,128)S(1)}, f32[32,4,1,1024]{3,0,2,1:T(8,128)S(1)}, u32[]{:S(2)}, u32[]{:S(2)}) collective-permute-start(f32[32,4,1,1024]{3,0,2,1:T(8,128)S(1)} %get-tuple-element.18), channel_id=1, source_target_pairs={{1,0},{2,1},{3,2},{5,4},{6,5},{7,6},{9,8},{10,9},{11,10},{13,12},{... | collective-permute-start | bytes 1572872 | tf_op jit(solution)/shard_map/ppermute | solution.py:25
  25.4 13.4 %collective-permute-start.2 = (f32[32,4,1,1024]{3,0,2,1:T(8,128)S(1)}, f32[32,4,1,1024]{3,0,2,1:T(8,128)S(1)}, u32[]{:S(2)}, u32[]{:S(2)}) collective-permute-start(f32[32,4,1,1024]{3,0,2,1:T(8,128)S(1)} %get-tuple-element.13), channel_id=1, source_target_pairs={{0,1},{1,2},{2,3},{4,5},{5,6},{6,7},{8,9},{9,10},{10,11},{12,13},{... | collective-permute-start | bytes 1572872 | tf_op jit(solution)/shard_map/ppermute | solution.py:23
  28.9 14.1 %collective-permute-start.3 = (f32[32,4,1,1024]{3,0,2,1:T(8,128)S(1)}, f32[32,4,1,1024]{3,0,2,1:T(8,128)S(1)}, u32[]{:S(2)}, u32[]{:S(2)}) collective-permute-start(f32[32,4,1,1024]{3,0,2,1:T(8,128)S(1)} %get-tuple-element.14), channel_id=1, source_target_pairs={{1,0},{2,1},{3,2},{5,4},{6,5},{7,6},{9,8},{10,9},{11,10},{13,12},{... | collective-permute-start | bytes 1572872 | tf_op jit(solution)/shard_map/ppermute | solution.py:25
  46.2 12.2 %collective-permute-start.4 = (f32[32,4,1,1024]{3,0,2,1:T(8,128)S(1)}, f32[32,4,1,1024]{3,0,2,1:T(8,128)S(1)}, u32[]{:S(2)}, u32[]{:S(2)}) collective-permute-start(f32[32,4,1,1024]{3,0,2,1:T(8,128)S(1)} %get-tuple-element.9), channel_id=1, source_target_pairs={{0,1},{1,2},{2,3},{4,5},{5,6},{6,7},{8,9},{9,10},{10,11},{12,13},{... | collective-permute-start | bytes 1572872 | tf_op jit(solution)/shard_map/ppermute | solution.py:23
  49.7 12.9 %collective-permute-start.5 = (f32[32,4,1,1024]{3,0,2,1:T(8,128)S(1)}, f32[32,4,1,1024]{3,0,2,1:T(8,128)S(1)}, u32[]{:S(2)}, u32[]{:S(2)}) collective-permute-start(f32[32,4,1,1024]{3,0,2,1:T(8,128)S(1)} %get-tuple-element.10), channel_id=1, source_target_pairs={{1,0},{2,1},{3,2},{5,4},{6,5},{7,6},{9,8},{10,9},{11,10},{13,12},{... | collective-permute-start | bytes 1572872 | tf_op jit(solution)/shard_map/ppermute | solution.py:25
  81.4 4.6 %copy-start.5 = (s32[1,1,16]{2,1,0:T(1,128)S(1)}, s32[1,1,16]{2,1,0:T(1,128)}, u32[]{:S(2)}) copy-start(s32[1,1,16]{2,1,0:T(1,128)} %param.9) | copy-start | bytes 196
  81.4 30.5 %all-to-all-start = ((f32[8,1,65536]{2,1,0:T(1,128)}), f32[8,1,65536]{2,1,0:T(1,128)S(1)}, u32[]{:S(2)}, u32[]{:S(2)}) async-start(f32[8,1,65536]{2,1,0:T(1,128)} %reshape.92), calls=%async_computation | async-start | bytes 4194304 | tf_op jit(solution)/shard_map/all_to_all | solution.py:89
  111.9 1.3 copy-start.2
  138.0 5.3 %copy-start.3 = (f32[1,1,16]{2,1,0:T(1,128)S(1)}, f32[1,1,16]{2,1,0:T(1,128)}, u32[]{:S(2)}) copy-start(f32[1,1,16]{2,1,0:T(1,128)} %param.8) | copy-start | bytes 196
  138.0 5.3 %copy-start.4 = (s32[1,1,16]{2,1,0:T(1,128)S(1)}, s32[1,1,16]{2,1,0:T(1,128)}, u32[]{:S(2)}) copy-start(s32[1,1,16]{2,1,0:T(1,128)} %param.10) | copy-start | bytes 196
  148.4 1.6 copy-start.6
  150.0 1.7 copy-start.1
where the time goes:
time: 190 us
  waiting for transfers between devices  62 us (33%)
  local copies, waits for them, and re-layouts  50.6 us (27%)
  blocking collectives  29 us (15%)
  starting transfers between devices  19.9 us (10%)
  other arithmetic  15.8 us (8%)
  matrix products  10.4 us (5%)
    all_to_all x1, blocking collectives, per_device(): lax.all_to_all(state, 'mem', split_axis=0, concat_axis=3, tiled=True)  29 us
    all_to_all x1, waiting for transfers between devices, per_device(): lax.all_to_all(state, 'mem', split_axis=3, concat_axis=0, tiled=True)  25.9 us
    ppermute x3, waiting for transfers between devices, with_halo(): lax.ppermute(tail, axis, [(i, (i + 1) % count) for i in range(ends)])  25 us
    unnamed x19, local copies, waits for them, and re-layouts  22.5 us
    ppermute x3, starting transfers between devices, with_halo(): lax.ppermute(tail, axis, [(i, (i + 1) % count) for i in range(ends)])  12.1 us
    ppermute x3, waiting for transfers between devices, with_halo(): lax.ppermute(head, axis, [((i + 1) % count, i) for i in range(ends)])  11.2 us
    all_to_all x2, local copies, waits for them, and re-layouts, per_device(): lax.all_to_all(state, 'mem', split_axis=3, concat_axis=0, tiled=True)  8.07 us
    all_to_all x1, other arithmetic, per_device(): lax.all_to_all(state, 'mem', split_axis=3, concat_axis=0, tiled=True)  7.21 us
  transfers between devices with their start and end apart: 7, of which 7 were waited for; matrix products, arithmetic and copies ran while one was open for 1% of the time, Pallas kernels for 0%

commit v1 on v0

v1 whole, which is shorter than its diff:
```python
import functools

import jax
import jax.numpy as jnp
from jax import lax
from jax.experimental import pallas as pl
from jax.experimental.pallas import tpu as pltpu
from jax.sharding import PartitionSpec as P

NSI = 5
HALO = 3
LANES = 128
SUB = 8

time_step = 0.15
viscosity = 0.1
third_part = 1.0 / 3.0
two_thirds = 2.0 / 3.0

HIGHEST = lax.Precision.HIGHEST
VMEM = pl.BlockSpec(memory_space=pltpu.VMEM)
SMEM = pl.BlockSpec(memory_space=pltpu.SMEM)
KERNEL_VMEM = 24 << 20


def call(kernel, out_shape, in_specs, scratch=(), cost=(1 << 20, 1 << 20), name=None):
    flops, nbytes = cost
    return pl.pallas_call(
        kernel,
        out_shape=out_shape,
        in_specs=in_specs,
        out_specs=jax.tree.map(lambda _: VMEM, out_shape),
        scratch_shapes=list(scratch),
        compiler_params=pltpu.CompilerParams(vmem_limit_bytes=KERNEL_VMEM),
        cost_estimate=pl.CostEstimate(flops=flops, bytes_accessed=nbytes, transcendentals=0),
        name=name,
    )


class Plan:
    def __init__(self, ensemble, slots, groups):
        self.members, self.fields, self.rows, self.columns = ensemble.shape
        self.total = self.members * groups
        self.slots = slots
        self.groups = groups
        self.width = self.columns // groups
        self.tiles = self.columns // LANES
        chunks = min(4, self.tiles)
        while self.tiles % chunks or (self.columns // chunks) % self.width:
            chunks -= 1
        self.chunks = chunks
        self.nt = self.tiles // chunks
        self.np = self.columns // chunks // self.width
        self.halves = 2
        self.hrows = self.rows // self.halves
        self.hrf = self.hrows * self.fields
        self.edge_groups = HALO * self.fields
        self.per_edge = LANES // (2 * HALO)
        self.edge_tiles = -(-self.edge_groups // self.per_edge)
        self.message = self.nt * self.edge_groups + self.edge_tiles
        self.q = max(1, LANES // self.width)
        self.plain = -(-self.hrf // SUB) * SUB
        self.block = self.hrf * slots + self.plain
        self.total_rows = self.nt * self.block

    def patches_of(self, tile):
        if self.width >= LANES:
            return [(tile * LANES // self.width, 0, LANES)]
        return [(tile * self.q + i, i * self.width, (i + 1) * self.width) for i in range(self.q)]


def lane_ids(shape):
    return lax.broadcasted_iota(jnp.int32, shape, len(shape) - 1)


def pack_kernel(plan, raw, state, *messages):
    p = plan
    lane = lane_ids((SUB, LANES))

    def body(kk, carry):
        mem = pl.ds(pl.multiple_of(kk * SUB, SUB), SUB)
        for t in range(p.tiles):
            c, i = divmod(t, p.nt)
            up, down = messages[2 * c], messages[2 * c + 1]
            for f in range(p.fields):
                for r in range(p.rows):
                    x = raw[mem, f, r, t * LANES : (t + 1) * LANES]
                    state[t, r, f, mem, :] = x
                    if r >= p.rows - HALO:
                        up[(i * HALO + r - (p.rows - HALO)) * p.fields + f, mem, :] = x
                    if r < HALO:
                        down[(i * HALO + r) * p.fields + f, mem, :] = x
        for c in range(p.chunks):
            after = (c + 1) * p.nt % p.tiles
            before = (c * p.nt - 1) % p.tiles
            for d in range(2):
                out = messages[2 * c + d]
                for e in range(p.edge_tiles):
                    packed = jnp.zeros((SUB, LANES), jnp.float32)
                    for g in range(e * p.per_edge, min((e + 1) * p.per_edge, p.edge_groups)):
                        i, f = divmod(g, p.fields)
                        r = i + (p.rows - HALO if d == 0 else 0)
                        edge = jnp.where(lane < LANES // 2, state[after, r, f, mem, :], state[before, r, f, mem, :])
                        place = (g - e * p.per_edge) * 2 * HALO
                        inside = (lane >= place) & (lane < place + 2 * HALO)
                        packed = jnp.where(inside, pltpu.roll(edge, place + HALO, 1), packed)
                    out[p.nt * p.edge_groups + e, mem, :] = packed
        return carry

    lax.fori_loop(0, p.members // SUB, body, 0)


def step_once(p, rows_in, load, store, last):
    lane = lane_ids((SUB, LANES))
    ring = p.nt + 1
    out_tiles = p.nt if last else ring
    for row in range(1, rows_in - 1):
        coef = []
        for t in range(out_tiles):
            u = load(row, 0, t) * (time_step * 0.5)
            v = load(row, 1, t) * (time_step * 0.5)
            k = time_step * viscosity
            coef.append((k - u, k + u, k - v, k + v))
        for f in range(p.fields):
            x = [load(row, f, t) for t in range(ring)]
            right = [pltpu.roll(a, 1, 1) for a in x]
            left = [pltpu.roll(a, LANES - 1, 1) for a in x]
            for t in range(out_tiles):
                west = jnp.where(lane == 0, right[(t - 1) % ring], right[t])
                east = jnp.where(lane == LANES - 1, left[(t + 1) % ring], left[t])
                ce, cw, cn, cs = coef[t]
                moved = (ce * east + cw * west) + (cn * load(row + 1, f, t) + cs * load(row - 1, f, t))
                store(row, f, t, x[t], (1.0 - 4.0 * time_step * viscosity) * x[t] + moved)


def forecast_kernel(plan, chunk, obs_cell, flags, state, low, high, ahead, seen, keep, send, s0, s1, s2):
    p = plan
    ring = p.nt + 1
    full = p.rows + 2 * HALO
    after = (chunk + 1) * p.nt % p.tiles
    before = (chunk * p.nt - 1) % p.tiles
    has_low = flags[0].astype(jnp.float32)
    has_high = flags[1].astype(jnp.float32)
    core = flags[2]
    lane = lane_ids((SUB, LANES))

    def body(kk, carry):
        mem = pl.ds(pl.multiple_of(kk * SUB, SUB), SUB)

        def edge_of(source, g):
            e, place = divmod(g, p.per_edge)
            return pltpu.roll(source[p.nt * p.edge_groups + e, mem, :], (LANES - HALO - place * 2 * HALO) % LANES, 1)

        for f in range(p.fields):
            for r in range(p.rows):
                s0[r + HALO, f, p.nt] = jnp.where(lane < LANES // 2, state[after, r, f, mem, :], state[before, r, f, mem, :])
            for i in range(HALO):
                s0[i, f, p.nt] = edge_of(low, i * p.fields + f)
                s0[HALO + p.rows + i, f, p.nt] = edge_of(high, i * p.fields + f)

        def load0(row, f, t):
            if t == p.nt:
                return s0[row, f, t]
            if row < HALO:
                return low[(t * HALO + row) * p.fields + f, mem, :]
            if row >= HALO + p.rows:
                return high[(t * HALO + row - HALO - p.rows) * p.fields + f, mem, :]
            return state[chunk * p.nt + t, row - HALO, f, mem, :]

        def keep_zero(row, value):
            if row < HALO:
                return value * has_low
            if row >= HALO + p.rows:
                return value * has_high
            return value

        def load1(row, f, t):
            return s1[row, f, t]

        def load2(row, f, t):
            return s2[row, f, t]

        def store1(row, f, t, x, stepped):
            s1[row, f, t] = keep_zero(row, stepped)

        def store2(row, f, t, x, stepped):
            row = row + 1
            s2[row, f, t] = keep_zero(row, 0.75 * load0(row, f, t) + 0.25 * stepped)

        def store3(row, f, t, x, stepped):
            row = row + 2
            ahead[t, row - HALO, f, mem, :] = third_part * load0(row, f, t) + two_thirds * stepped

        step_once(p, full, load0, store1, False)
        step_once(p, full - 2, lambda row, f, t: s1[row + 1, f, t], store2, False)
        step_once(p, full - 4, lambda row, f, t: s2[row + 2, f, t], store3, True)
        return carry

    lax.fori_loop(0, p.members // SUB, body, 0)

    wide = lane_ids((p.members, LANES))
    for j in range(p.np):
        found = jnp.zeros((p.members, LANES), jnp.float32)
        for o in range(p.slots):
            cell = obs_cell[(chunk * p.np + j) * p.slots + o]
            f = cell // (p.rows * p.width)
            r = cell // p.width % p.rows
            column = cell % p.width + j * p.width
            tile = ahead[column // LANES, r, f]
            shift = (o - column % LANES + LANES) % LANES
            found = jnp.where(wide == o, pltpu.roll(tile, shift, 1), found)
        seen[j] = found

    last = lax.broadcasted_iota(jnp.int32, (SUB, p.members), 0)
    ones = jnp.where(last == 0, 1.0, 0.0).astype(jnp.float32)
    sides = [jnp.concatenate([jnp.transpose(seen[j])[: p.slots], ones], axis=0) for j in range(p.np)]
    for side in range(p.halves):
        out = keep if side == 0 else send
        half = core if side == 0 else 1 - core
        for t in range(p.nt):
            base = t * p.block
            tiles = [ahead[t, half * p.hrows + i // p.fields, i % p.fields] for i in range(p.hrf)]
            joined = jnp.concatenate(tiles, axis=1)
            result = None
            for j, first, stop in p.patches_of(t):
                part = jnp.dot(sides[j], joined, precision=HIGHEST, preferred_element_type=jnp.float32)
                if result is None:
                    result = part
                else:
                    at = lane_ids(part.shape) % LANES
                    result = jnp.where((at >= first) & (at < stop), part, result)
            for i in range(p.hrf):
                piece = result[:, i * LANES : (i + 1) * LANES]
                out[pl.ds(base + i * p.slots, p.slots), :] = piece[: p.slots]
                out[pl.ds(base + p.hrf * p.slots + i, 1), :] = piece[p.slots : p.slots + 1]
            for i in range(p.hrf, p.plain):
                out[pl.ds(base + p.hrf * p.slots + i, 1), :] = jnp.zeros((1, LANES), jnp.float32)


def finish_kernel(plan, chunk, obs_cell, flags, obs, ahead, seen, own, other, new):
    p = plan
    n = p.slots
    core = flags[2]
    free = p.total - 1.0
    row_of = lax.broadcasted_iota(jnp.int32, (n, n), 0)
    col_of = lax.broadcasted_iota(jnp.int32, (n, n), 1)
    eye = jnp.where(row_of == col_of, 1.0, 0.0).astype(jnp.float32)
    lane_row = lane_ids((1, LANES))
    lane_mat = lane_ids((n, LANES))

    def column(row):
        return jnp.sum(eye * row, axis=1, keepdims=True)

    def dot(a, b):
        return jnp.dot(a, b, precision=HIGHEST, preferred_element_type=jnp.float32)

    factors = []
    for j in range(p.np):
        moments = jnp.zeros((n, LANES), jnp.float32)
        sums = jnp.zeros((1, LANES), jnp.float32)
        for o in range(n):
            cell = obs_cell[(chunk * p.np + j) * n + o]
            f = cell // (p.rows * p.width)
            r = cell // p.width % p.rows
            col = cell % p.width + j * p.width
            base = col // LANES * p.block
            index = r % p.hrows * p.fields + f
            half = r // p.hrows
            shift = (o - col % LANES + LANES) % LANES
            at = pl.multiple_of(base + index * n, SUB)
            a = own[pl.ds(at, n), :]
            b = other[pl.ds(at, n), :]
            value = jnp.where(half == core, a, b)
            moments = jnp.where(lane_mat == o, pltpu.roll(value, shift, 1), moments)
            plain = base + p.hrf * n + index
            value = jnp.where(half == core, own[pl.ds(plain, 1), :], other[pl.ds(plain, 1), :])
            sums = jnp.where(lane_row == o, pltpu.roll(jnp.broadcast_to(value, (SUB, LANES)), shift, 1)[:1], sums)
        mean = sums[:, :n] * (1.0 / p.total)
        mean_col = column(mean)
        gram = moments[:, :n] - p.total * mean_col * mean
        patch = chunk * p.np + j
        value, variance, loop, count = (obs[patch, i : i + 1, :n] for i in range(4))
        slot = lax.broadcasted_iota(jnp.int32, (1, n), 1).astype(jnp.float32)
        weight = jnp.where(slot < count, jnp.exp(-0.35 * loop) / variance, 0.0)
        root = jnp.sqrt(weight)
        root_col = column(root)
        scaled = root_col * gram * root
        bound = free + 0.5 * jnp.sum(jnp.sum(scaled * eye, axis=1, keepdims=True), axis=0, keepdims=True)
        inverse = 1.0 / bound
        y0 = free * inverse
        yg = eye * inverse
        yf = y0 * eye + scaled * inverse
        z0 = jnp.ones((1, 1), jnp.float32)
        zg = jnp.zeros((n, n), jnp.float32)
        zf = eye
        for repeat in range(NSI):
            if repeat == 0:
                tf, tg = yf, yg
            else:
                both = dot(jnp.concatenate([zf, zg], axis=0), yf)
                tf, tg = both[:n], z0 * yg + both[n:]
            f0 = 1.5 - 0.5 * z0 * y0
            fg = -0.5 * tg
            ff = 1.5 * eye - 0.5 * tf
            if repeat == 0:
                both = dot(jnp.concatenate([yf, yg], axis=0), ff)
                yf, yg = both[:n], y0 * fg + both[n:]
                zf, zg = ff, fg
            elif repeat < NSI - 1:
                both = dot(jnp.concatenate([yf, yg, zf, zg], axis=0), ff)
                yf, yg = both[:n], y0 * fg + both[n : 2 * n]
                zf, zg = both[2 * n : 3 * n], z0 * fg + both[3 * n :]
            else:
                both = dot(jnp.concatenate([zf, zg], axis=0), ff)
                zf, zg = both[:n], z0 * fg + both[n:]
            y0 = y0 * f0
            z0 = z0 * f0
        scale = jnp.sqrt(free * inverse)
        spread = scale * root_col * zg * root
        drive = root * (value - mean)
        down = jnp.sum(zf * column(drive), axis=0, keepdims=True)
        down = jnp.sum(zf * column(down), axis=0, keepdims=True)
        shift_row = root * down * inverse
        pert = seen[j][:, :n] - mean
        weights = dot(pert, spread) + shift_row
        factors.append((weights, mean_col, scale * z0))

    for t in range(p.nt):
        for half in range(p.halves):
            at_own = half == core
            pieces = []
            for i in range(p.hrf):
                at = t * p.block + i * n
                pieces.append(jnp.where(at_own, own[at : at + n, :], other[at : at + n, :]))
            base = t * p.block + p.hrf * n
            plain = jnp.where(at_own, own[base : base + p.plain, :], other[base : base + p.plain, :])
            results = []
            for j, first, stop in p.patches_of(t):
                weights, mean_col, spread0 = factors[j]
                centred = [pieces[i] - mean_col * plain[i : i + 1, :] for i in range(p.hrf)]
                update = dot(weights, jnp.concatenate(centred, axis=1))
                results.append((update, spread0, first, stop))
            for i in range(p.hrf):
                r, f = half * p.hrows + i // p.fields, i % p.fields
                x = ahead[t, r, f]
                mean = plain[i : i + 1, :] * (1.0 / p.total)
                final = None
                for update, spread0, first, stop in results:
                    part = mean + spread0 * (x - mean) + update[:, i * LANES : (i + 1) * LANES]
                    if final is None:
                        final = part
                    else:
                        at = lane_ids(part.shape)
                        final = jnp.where((at >= first) & (at < stop), part, final)
                new[t, r, f] = final


def total_over_members(plan, keep, send):
    p = plan
    pairs = [(i, i ^ 1) for i in range(p.groups)]
    chip = keep + lax.ppermute(send, "mem", pairs)
    chips = p.groups // 2
    if chips <= 4 and chips & (chips - 1) == 0:
        total = chip
        for step in range(chips - 1, 0, -1):
            total = total + lax.ppermute(chip, "mem", [(i, i ^ (2 * step)) for i in range(p.groups)])
    else:
        same = [[2 * i + core for i in range(chips)] for core in range(2)]
        total = lax.psum(chip, "mem", axis_index_groups=same)
    return total, lax.ppermute(total, "mem", pairs)


def per_device(ensemble, obs_value, obs_var, obs_cell, obs_loop, obs_count):
    groups = lax.axis_size("mem")
    bands = lax.axis_size("lat")
    slots = obs_cell.shape[-1]
    p = Plan(ensemble, slots, groups)
    f32 = jnp.float32
    shape = jax.ShapeDtypeStruct

    out = call(
        functools.partial(pack_kernel, p),
        [shape((p.tiles, p.rows, p.fields, p.members, LANES), f32)]
        + [shape((p.message, p.members, LANES), f32)] * (2 * p.chunks),
        [VMEM],
        name="pack",
    )(ensemble)
    state, messages = out[0], out[1:]
    up = [(i, i + 1) for i in range(bands - 1)]
    down = [(i + 1, i) for i in range(bands - 1)]
    low, high = [], []
    for c in range(p.chunks):
        low.append(lax.ppermute(messages[2 * c], "lat", up))
        high.append(lax.ppermute(messages[2 * c + 1], "lat", down))

    mine = jnp.concatenate(
        [
            obs_value[0],
            obs_var[0],
            obs_loop[0].astype(f32),
            jnp.broadcast_to(obs_count[0][:, None].astype(f32), (1, slots)),
            obs_cell[0].astype(f32),
        ],
        axis=1,
    )
    every = lax.all_gather(mine, "mem", axis=0, tiled=True).reshape(groups, 5, slots)
    cells = every[:, 4].astype(jnp.int32).reshape(groups * slots)
    obs = jnp.pad(every[:, :4], ((0, 0), (0, SUB - 4), (0, LANES - slots)))

    band = lax.axis_index("lat")
    core = lax.rem(lax.axis_index("mem"), 2)
    flags = jnp.stack([(band > 0).astype(jnp.int32), (band < bands - 1).astype(jnp.int32), core.astype(jnp.int32)])

    new = []
    for c in range(p.chunks):
        stage = (p.rows + 2 * HALO, p.fields, p.nt + 1, SUB, LANES)
        ahead, seen, keep, send = call(
            functools.partial(forecast_kernel, p, c),
            [
                shape((p.nt, p.rows, p.fields, p.members, LANES), f32),
                shape((p.np, p.members, LANES), f32),
                shape((p.total_rows, LANES), f32),
                shape((p.total_rows, LANES), f32),
            ],
            [SMEM, SMEM, VMEM, VMEM, VMEM],
            [pltpu.VMEM(stage, f32)] * 3,
            name="forecast",
        )(cells, flags, state, low[c], high[c])
        own, other = total_over_members(p, keep, send)
        new.append(
            call(
                functools.partial(finish_kernel, p, c),
                shape((p.nt, p.rows, p.fields, p.members, LANES), f32),
                [SMEM, SMEM, VMEM, VMEM, VMEM, VMEM, VMEM],
                name="finish",
            )(cells, flags, obs, ahead, seen, own, other)
        )
    joined = jnp.concatenate(new, axis=0)
    return joined.transpose(3, 2, 1, 0, 4).reshape(p.members, p.fields, p.rows, p.columns)


def solution(mesh):
    placed = (
        P("mem", None, "lat", None),
        P(None, ("mem", "lat"), None),
        P(None, ("mem", "lat"), None),
        P(None, ("mem", "lat"), None),
        P(None, ("mem", "lat"), None),
        P(None, ("mem", "lat")),
    )
    return jax.shard_map(
        per_device,
        mesh=mesh,
        in_specs=placed,
        out_specs=P("mem", None, "lat", None),
        check_vma=False,
    )
```

time: 190 us -> 116 us (0.61)
  the two profiles are of different devices: /device:TPU:0 before, /device:TPU:19 now
where the time goes in v1:
time: 116 us; the launch traced here: 114 us
  starting transfers between devices  41.3 us (36%)
  Pallas kernels  40.1 us (35%)
  blocking collectives  11.2 us (10%)
  local copies, waits for them, and re-layouts  9.61 us (8%)
  waiting for transfers between devices  9.53 us (8%)
  other arithmetic  1.19 us (1%)
    pallas_call x4, Pallas kernels, per_device(): call(functools.partial(finish_kernel, p, c), shape((p.nt, p.rows, p.field...  19.2 us
    pallas_call x4, Pallas kernels, per_device(): call(functools.partial(forecast_kernel, p, c), [shape((p.nt, p.rows, p.fi...  17.8 us
    ppermute x4, starting transfers between devices, per_device(): low.append(lax.ppermute(messages[2 * c], 'lat', up))  14.5 us
    ppermute x12, starting transfers between devices, total_over_members(): lax.ppermute(chip, 'mem', [(i, i ^ 2 * step) for i in range(p.groups)])  11.4 us
    all_gather x1, blocking collectives, per_device(): lax.all_gather(mine, 'mem', axis=0, tiled=True).reshape(groups, 5, slots)  11.2 us
    ppermute x12, waiting for transfers between devices, total_over_members(): lax.ppermute(chip, 'mem', [(i, i ^ 2 * step) for i in range(p.groups)])  9.49 us
    ppermute x4, starting transfers between devices, per_device(): high.append(lax.ppermute(messages[2 * c + 1], 'lat', down))  7.95 us
    ppermute x4, starting transfers between devices, total_over_members(): return (total, lax.ppermute(total, 'mem', pairs))  6.26 us
  transfers between devices with their start and end apart: 28, of which 7 were waited for; matrix products, arithmetic and copies ran while one was open for 1% of the time, Pallas kernels for 28%

profile of v1, /device:TPU:19, one launch (start us, length us, event | category | flops | bytes accessed | tf_op | source)
XLA Modules:
  0.0 113.9 jit_solution(18223192222096661811)
XLA Ops:
  0.0 1.6 %copy-done = f32[32,4,4,1024]{3,2,1,0:T(4,128)S(1)} copy-done((f32[32,4,4,1024]{3,2,1,0:T(4,128)S(1)}, f32[32,4,4,1024]{3,2,1,0:T(4,128)}, u32[]{:S(2)}) %copy-start) | copy-done | bytes 2097176
  1.6 3.1 %pack.1 = (f32[8,4,4,32,128]{4,3,2,1,0:T(8,128)S(1)}, f32[25,32,128]{2,1,0:T(8,128)S(1)}, f32[25,32,128]{2,1,0:T(8,128)S(1)}, f32[25,32,128]{2,1,0:T(8,128)S(1)}...) custom-call(f32[32,4,4,1024]{3,2,1,0:T(4,128)S(1)} %copy-done), custom_call_target="tpu_custom_call" | custom-call | flops 1048576 | bytes 1048576 | tf_op jit(solution)/shard_map/pack/pallas_call | solution.py:381
  4.7 3.2 %collective-permute-start = (f32[25,32,128]{2,1,0:T(8,128)S(1)}, f32[25,32,128]{2,1,0:T(8,128)S(1)}, u32[]{:S(2)}, u32[]{:S(2)}) collective-permute-start(f32[25,32,128]{2,1,0:T(8,128)S(1)} %get-tuple-element.31), channel_id=1, source_target_pairs={{0,1},{1,2},{2,3},{4,5},{5,6},{6,7},{8,9},{9,10},{10,11},{12,13},{... | collective-permute-start | bytes 1228808 | tf_op jit(solution)/shard_map/ppermute | solution.py:393
  7.9 2.1 %collective-permute-start.1 = (f32[25,32,128]{2,1,0:T(8,128)S(1)}, f32[25,32,128]{2,1,0:T(8,128)S(1)}, u32[]{:S(2)}, u32[]{:S(2)}) collective-permute-start(f32[25,32,128]{2,1,0:T(8,128)S(1)} %get-tuple-element.32), channel_id=1, source_target_pairs={{1,0},{2,1},{3,2},{5,4},{6,5},{7,6},{9,8},{10,9},{11,10},{13,12},{... | collective-permute-start | bytes 1228808 | tf_op jit(solution)/shard_map/ppermute | solution.py:394
  10.0 3.2 %collective-permute-start.7 = (f32[25,32,128]{2,1,0:T(8,128)S(1)}, f32[25,32,128]{2,1,0:T(8,128)S(1)}, u32[]{:S(2)}, u32[]{:S(2)}) collective-permute-start(f32[25,32,128]{2,1,0:T(8,128)S(1)} %get-tuple-element.37), channel_id=1, source_target_pairs={{0,1},{1,2},{2,3},{4,5},{5,6},{6,7},{8,9},{9,10},{10,11},{12,13},{... | collective-permute-start | bytes 1228808 | tf_op jit(solution)/shard_map/ppermute | solution.py:393
  13.2 2.1 %collective-permute-start.8 = (f32[25,32,128]{2,1,0:T(8,128)}, f32[25,32,128]{2,1,0:T(8,128)}, u32[]{:S(2)}, u32[]{:S(2)}) collective-permute-start(f32[25,32,128]{2,1,0:T(8,128)} %get-tuple-element.38), channel_id=1, source_target_pairs={{1,0},{2,1},{3,2},{5,4},{6,5},{7,6},{9,8},{10,9},{11,10},{13,12},{... | collective-permute-start | bytes 1228808 | tf_op jit(solution)/shard_map/ppermute | solution.py:394
  15.3 4.0 %collective-permute-start.14 = (f32[25,32,128]{2,1,0:T(8,128)}, f32[25,32,128]{2,1,0:T(8,128)S(1)}, u32[]{:S(2)}, u32[]{:S(2)}) collective-permute-start(f32[25,32,128]{2,1,0:T(8,128)} %get-tuple-element.43), channel_id=1, source_target_pairs={{0,1},{1,2},{2,3},{4,5},{5,6},{6,7},{8,9},{9,10},{10,11},{12,13},{... | collective-permute-start | bytes 1228808 | tf_op jit(solution)/shard_map/ppermute | solution.py:393
  19.3 0.7 copy-done.3
  20.0 1.9 %collective-permute-start.15 = (f32[25,32,128]{2,1,0:T(8,128)}, f32[25,32,128]{2,1,0:T(8,128)}, u32[]{:S(2)}, u32[]{:S(2)}) collective-permute-start(f32[25,32,128]{2,1,0:T(8,128)} %get-tuple-element.44), channel_id=1, source_target_pairs={{1,0},{2,1},{3,2},{5,4},{6,5},{7,6},{9,8},{10,9},{11,10},{13,12},{... | collective-permute-start | bytes 1228808 | tf_op jit(solution)/shard_map/ppermute | solution.py:394
  22.0 0.7 copy-done.5
  22.7 4.1 %collective-permute-start.21 = (f32[25,32,128]{2,1,0:T(8,128)}, f32[25,32,128]{2,1,0:T(8,128)S(1)}, u32[]{:S(2)}, u32[]{:S(2)}) collective-permute-start(f32[25,32,128]{2,1,0:T(8,128)} %get-tuple-element.49), channel_id=1, source_target_pairs={{0,1},{1,2},{2,3},{4,5},{5,6},{6,7},{8,9},{9,10},{10,11},{12,13},{... | collective-permute-start | bytes 1228808 | tf_op jit(solution)/shard_map/ppermute | solution.py:393
  26.8 0.7 copy-done.1
  27.6 1.9 %collective-permute-start.22 = (f32[25,32,128]{2,1,0:T(8,128)}, f32[25,32,128]{2,1,0:T(8,128)S(1)}, u32[]{:S(2)}, u32[]{:S(2)}) collective-permute-start(f32[25,32,128]{2,1,0:T(8,128)} %get-tuple-element.50), channel_id=1, source_target_pairs={{1,0},{2,1},{3,2},{5,4},{6,5},{7,6},{9,8},{10,9},{11,10},{13,12},{... | collective-permute-start | bytes 1228808 | tf_op jit(solution)/shard_map/ppermute | solution.py:394
  30.3 11.2 %all-gather = f32[8,1,80]{2,1,0:T(1,128)S(1)} all-gather(f32[1,1,80]{2,1,0:T(1,128)S(1)} %bitcast.15), channel_id=1, replica_groups=mesh['mem'=8,'lat'=4] {'mem'}, dimensions={0}, use_global_device_ids=true | all-gather | bytes 2880 | tf_op jit(solution)/shard_map/all_gather | solution.py:406
  41.5 0.5 broadcast.10
  42.0 0.6 reduce.7
  42.9 1.0 copy-done.4
  43.9 1.0 copy-done.6
  44.9 4.2 %forecast.4 = (f32[2,4,4,32,128]{4,3,2,1,0:T(8,128)S(1)}, f32[2,32,128]{2,1,0:T(8,128)S(1)}, f32[272,128]{1,0:T(8,128)S(1)}, f32[272,128]{1,0:T(8,128)S(1)}) custom-call(s32[128]{0:T(128)S(1)} %convert_element_type.48.obs_cell, s32[3]{0:T(128)S(1)} %pad_add_fusion.flags, f32[8,4,4,32,128]{4,3,2,1,0:T(8,128)S(1)} %get-tuple-element.30.state, ...), custom_call_target="tpu_custom_call" | custom-call | flops 1048576 | bytes 1048576 | tf_op jit(solution)/shard_map/forecast/pallas_call | solution.py:417
  49.3 4.6 %forecast.5 = (f32[2,4,4,32,128]{4,3,2,1,0:T(8,128)S(1)}, f32[2,32,128]{2,1,0:T(8,128)S(1)}, f32[272,128]{1,0:T(8,128)S(1)}, f32[272,128]{1,0:T(8,128)S(1)}) custom-call(s32[128]{0:T(128)S(1)} %convert_element_type.48.obs_cell, s32[3]{0:T(128)S(1)} %pad_add_fusion.flags, f32[8,4,4,32,128]{4,3,2,1,0:T(8,128)S(1)} %get-tuple-element.30.state, ...), custom_call_target="tpu_custom_call" | custom-call | flops 1048576 | bytes 1048576 | tf_op jit(solution)/shard_map/forecast/pallas_call | solution.py:417
  54.0 0.4 collective-permute-start.9
  54.4 4.6 %forecast.6 = (f32[2,4,4,32,128]{4,3,2,1,0:T(8,128)S(1)}, f32[2,32,128]{2,1,0:T(8,128)S(1)}, f32[272,128]{1,0:T(8,128)S(1)}, f32[272,128]{1,0:T(8,128)S(1)}) custom-call(s32[128]{0:T(128)S(1)} %convert_element_type.48.obs_cell, s32[3]{0:T(128)S(1)} %pad_add_fusion.flags, f32[8,4,4,32,128]{4,3,2,1,0:T(8,128)S(1)} %get-tuple-element.30.state, ...), custom_call_target="tpu_custom_call" | custom-call | flops 1048576 | bytes 1048576 | tf_op jit(solution)/shard_map/forecast/pallas_call | solution.py:417
  59.2 4.4 %forecast.7 = (f32[2,4,4,32,128]{4,3,2,1,0:T(8,128)S(1)}, f32[2,32,128]{2,1,0:T(8,128)S(1)}, f32[272,128]{1,0:T(8,128)S(1)}, f32[272,128]{1,0:T(8,128)S(1)}) custom-call(s32[128]{0:T(128)S(1)} %convert_element_type.48.obs_cell, s32[3]{0:T(128)S(1)} %pad_add_fusion.flags, f32[8,4,4,32,128]{4,3,2,1,0:T(8,128)S(1)} %get-tuple-element.30.state, ...), custom_call_target="tpu_custom_call" | custom-call | flops 1048576 | bytes 1048576 | tf_op jit(solution)/shard_map/forecast/pallas_call | solution.py:417
  64.3 1.2 %collective-permute-start.4 = (f32[272,128]{1,0:T(8,128)S(1)}, f32[272,128]{1,0:T(8,128)S(1)}, u32[]{:S(2)}, u32[]{:S(2)}) collective-permute-start(f32[272,128]{1,0:T(8,128)S(1)} %add.50), channel_id=1, source_target_pairs={{0,16},{4,20},{8,24},{12,28},{16,0},{20,4},{24,8},{28,12},{1,17},{... | collective-permute-start | bytes 417800 | tf_op jit(solution)/shard_map/ppermute | solution.py:366
  65.5 1.2 %collective-permute-start.3 = (f32[272,128]{1,0:T(8,128)S(1)}, f32[272,128]{1,0:T(8,128)S(1)}, u32[]{:S(2)}, u32[]{:S(2)}) collective-permute-start(f32[272,128]{1,0:T(8,128)S(1)} %add.50), channel_id=1, source_target_pairs={{0,24},{4,28},{8,16},{12,20},{16,8},{20,12},{24,0},{28,4},{1,25},{... | collective-permute-start | bytes 417800 | tf_op jit(solution)/shard_map/ppermute | solution.py:366
  67.1 1.3 %collective-permute-start.11 = (f32[272,128]{1,0:T(8,128)S(1)}, f32[272,128]{1,0:T(8,128)S(1)}, u32[]{:S(2)}, u32[]{:S(2)}) collective-permute-start(f32[272,128]{1,0:T(8,128)S(1)} %add.54), channel_id=1, source_target_pairs={{0,16},{4,20},{8,24},{12,28},{16,0},{20,4},{24,8},{28,12},{1,17},{... | collective-permute-start | bytes 417800 | tf_op jit(solution)/shard_map/ppermute | solution.py:366
  68.4 0.8 collective-permute-done.5
  69.1 1.2 %collective-permute-start.10 = (f32[272,128]{1,0:T(8,128)S(1)}, f32[272,128]{1,0:T(8,128)S(1)}, u32[]{:S(2)}, u32[]{:S(2)}) collective-permute-start(f32[272,128]{1,0:T(8,128)S(1)} %add.54), channel_id=1, source_target_pairs={{0,24},{4,28},{8,16},{12,20},{16,8},{20,12},{24,0},{28,4},{1,25},{... | collective-permute-start | bytes 417800 | tf_op jit(solution)/shard_map/ppermute | solution.py:366
  70.6 1.5 %collective-permute-done.3 = f32[272,128]{1,0:T(8,128)S(1)} collective-permute-done((f32[272,128]{1,0:T(8,128)S(1)}, f32[272,128]{1,0:T(8,128)S(1)}, u32[]{:S(2)}, u32[]{:S(2)}) %collective-permute-start.3) | collective-permute-done | bytes 139296 | tf_op jit(solution)/shard_map/ppermute | solution.py:366
  72.1 1.3 %collective-permute-start.18 = (f32[272,128]{1,0:T(8,128)S(1)}, f32[272,128]{1,0:T(8,128)S(1)}, u32[]{:S(2)}, u32[]{:S(2)}) collective-permute-start(f32[272,128]{1,0:T(8,128)S(1)} %add.58), channel_id=1, source_target_pairs={{0,16},{4,20},{8,24},{12,28},{16,0},{20,4},{24,8},{28,12},{1,17},{... | collective-permute-start | bytes 417800 | tf_op jit(solution)/shard_map/ppermute | solution.py:366
  73.4 1.8 %collective-permute-done.12 = f32[272,128]{1,0:T(8,128)S(1)} collective-permute-done((f32[272,128]{1,0:T(8,128)S(1)}, f32[272,128]{1,0:T(8,128)S(1)}, u32[]{:S(2)}, u32[]{:S(2)}) %collective-permute-start.12) | collective-permute-done | bytes 139296 | tf_op jit(solution)/shard_map/ppermute | solution.py:366
  75.1 1.2 %collective-permute-start.17 = (f32[272,128]{1,0:T(8,128)S(1)}, f32[272,128]{1,0:T(8,128)S(1)}, u32[]{:S(2)}, u32[]{:S(2)}) collective-permute-start(f32[272,128]{1,0:T(8,128)S(1)} %add.58), channel_id=1, source_target_pairs={{0,24},{4,28},{8,16},{12,20},{16,8},{20,12},{24,0},{28,4},{1,25},{... | collective-permute-start | bytes 417800 | tf_op jit(solution)/shard_map/ppermute | solution.py:366
  76.3 0.8 collective-permute-start.26
  77.1 1.0 collective-permute-done.10
  78.1 1.3 %collective-permute-start.25 = (f32[272,128]{1,0:T(8,128)S(1)}, f32[272,128]{1,0:T(8,128)S(1)}, u32[]{:S(2)}, u32[]{:S(2)}) collective-permute-start(f32[272,128]{1,0:T(8,128)S(1)} %add.62), channel_id=1, source_target_pairs={{0,16},{4,20},{8,24},{12,28},{16,0},{20,4},{24,8},{28,12},{1,17},{... | collective-permute-start | bytes 417800 | tf_op jit(solution)/shard_map/ppermute | solution.py:366
  79.4 1.8 %collective-permute-done.19 = f32[272,128]{1,0:T(8,128)S(1)} collective-permute-done((f32[272,128]{1,0:T(8,128)S(1)}, f32[272,128]{1,0:T(8,128)S(1)}, u32[]{:S(2)}, u32[]{:S(2)}) %collective-permute-start.19) | collective-permute-done | bytes 139296 | tf_op jit(solution)/shard_map/ppermute | solution.py:366
  81.2 1.2 %collective-permute-start.24 = (f32[272,128]{1,0:T(8,128)S(1)}, f32[272,128]{1,0:T(8,128)S(1)}, u32[]{:S(2)}, u32[]{:S(2)}) collective-permute-start(f32[272,128]{1,0:T(8,128)S(1)} %add.62), channel_id=1, source_target_pairs={{0,24},{4,28},{8,16},{12,20},{16,8},{20,12},{24,0},{28,4},{1,25},{... | collective-permute-start | bytes 417800 | tf_op jit(solution)/shard_map/ppermute | solution.py:366
  82.4 3.3 %collective-permute-start.6 = (f32[272,128]{1,0:T(8,128)S(1)}, f32[272,128]{1,0:T(8,128)S(1)}, u32[]{:S(2)}, u32[]{:S(2)}) collective-permute-start(f32[272,128]{1,0:T(8,128)S(1)} %add_add_fusion.3.own), channel_id=1, source_target_pairs={{0,4},{4,0},{8,12},{12,8},{16,20},{20,16},{24,28},{28,24},{1,5},{5... | collective-permute-start | bytes 417800 | tf_op jit(solution)/shard_map/ppermute | solution.py:370
  85.9 1.3 %collective-permute-done.26 = f32[272,128]{1,0:T(8,128)S(1)} collective-permute-done((f32[272,128]{1,0:T(8,128)S(1)}, f32[272,128]{1,0:T(8,128)S(1)}, u32[]{:S(2)}, u32[]{:S(2)}) %collective-permute-start.26) | collective-permute-done | bytes 139296 | tf_op jit(solution)/shard_map/ppermute | solution.py:366
  87.2 1.6 %collective-permute-start.20 = (f32[272,128]{1,0:T(8,128)S(1)}, f32[272,128]{1,0:T(8,128)S(1)}, u32[]{:S(2)}, u32[]{:S(2)}) collective-permute-start(f32[272,128]{1,0:T(8,128)S(1)} %add_add_fusion.1.own), channel_id=1, source_target_pairs={{0,4},{4,0},{8,12},{12,8},{16,20},{20,16},{24,28},{28,24},{1,5},{5... | collective-permute-start | bytes 417800 | tf_op jit(solution)/shard_map/ppermute | solution.py:370
  88.8 1.4 %collective-permute-done.24 = f32[272,128]{1,0:T(8,128)S(1)} collective-permute-done((f32[272,128]{1,0:T(8,128)S(1)}, f32[272,128]{1,0:T(8,128)S(1)}, u32[]{:S(2)}, u32[]{:S(2)}) %collective-permute-start.24) | collective-permute-done | bytes 139296 | tf_op jit(solution)/shard_map/ppermute | solution.py:366
  90.2 1.2 %collective-permute-start.27 = (f32[272,128]{1,0:T(8,128)S(1)}, f32[272,128]{1,0:T(8,128)S(1)}, u32[]{:S(2)}, u32[]{:S(2)}) collective-permute-start(f32[272,128]{1,0:T(8,128)S(1)} %add_add_fusion.own), channel_id=1, source_target_pairs={{0,4},{4,0},{8,12},{12,8},{16,20},{20,16},{24,28},{28,24},{1,5},{5... | collective-permute-start | bytes 417800 | tf_op jit(solution)/shard_map/ppermute | solution.py:370
  91.4 4.8 %finish.4 = f32[2,4,4,32,128]{4,3,2,1,0:T(8,128)S(1)} custom-call(s32[128]{0:T(128)S(1)} %convert_element_type.48.obs_cell, s32[3]{0:T(128)S(1)} %pad_add_fusion.flags, f32[8,8,128]{2,1,0:T(8,128)S(1)} %pad.4.obs, f32[2,4,4,32,128]{4,3,2,1,0:T(8,128)S(1)} %get-tuple-element.33.ahead, f32[2,32,128]{2,1,0:T(8,128)S(1)} %get-tuple-element.34.seen, ...), custom_call_target="tpu_custom_call" | custom-call | flops 1048576 | bytes 1048576 | tf_op jit(solution)/shard_map/finish/pallas_call | solution.py:431
  96.2 4.8 %finish.5 = f32[2,4,4,32,128]{4,3,2,1,0:T(8,128)S(1)} custom-call(s32[128]{0:T(128)S(1)} %convert_element_type.48.obs_cell, s32[3]{0:T(128)S(1)} %pad_add_fusion.flags, f32[8,8,128]{2,1,0:T(8,128)S(1)} %pad.4.obs, f32[2,4,4,32,128]{4,3,2,1,0:T(8,128)S(1)} %get-tuple-element.39.ahead, f32[2,32,128]{2,1,0:T(8,128)S(1)} %get-tuple-element.40.seen, ...), custom_call_target="tpu_custom_call" | custom-call | flops 1048576 | bytes 1048576 | tf_op jit(solution)/shard_map/finish/pallas_call | solution.py:431
  101.0 4.8 %finish.6 = f32[2,4,4,32,128]{4,3,2,1,0:T(8,128)S(1)} custom-call(s32[128]{0:T(128)S(1)} %convert_element_type.48.obs_cell, s32[3]{0:T(128)S(1)} %pad_add_fusion.flags, f32[8,8,128]{2,1,0:T(8,128)S(1)} %pad.4.obs, f32[2,4,4,32,128]{4,3,2,1,0:T(8,128)S(1)} %get-tuple-element.45.ahead, f32[2,32,128]{2,1,0:T(8,128)S(1)} %get-tuple-element.46.seen, ...), custom_call_target="tpu_custom_call" | custom-call | flops 1048576 | bytes 1048576 | tf_op jit(solution)/shard_map/finish/pallas_call | solution.py:431
  105.8 4.8 %finish.7 = f32[2,4,4,32,128]{4,3,2,1,0:T(8,128)S(1)} custom-call(s32[128]{0:T(128)S(1)} %convert_element_type.48.obs_cell, s32[3]{0:T(128)S(1)} %pad_add_fusion.flags, f32[8,8,128]{2,1,0:T(8,128)S(1)} %pad.4.obs, f32[2,4,4,32,128]{4,3,2,1,0:T(8,128)S(1)} %get-tuple-element.51.ahead, f32[2,32,128]{2,1,0:T(8,128)S(1)} %get-tuple-element.52.seen, ...), custom_call_target="tpu_custom_call" | custom-call | flops 1048576 | bytes 1048576 | tf_op jit(solution)/shard_map/finish/pallas_call | solution.py:431
  110.9 1.2 %copy.11 = f32[32,4,4,8,128]{4,3,2,1,0:T(8,128)S(1)} copy(f32[32,4,4,8,128]{4,0,1,2,3:T(8,128)S(1)} %maximum_bitcast_fusion) | data formatting | bytes 4194304 | tf_op jit(solution)/shard_map/reshape | solution.py:439
  112.1 1.7 %reshape.44 = f32[32,4,4,1024]{3,2,1,0:T(4,128)} reshape(f32[32,4,4,8,128]{4,3,2,1,0:T(8,128)S(1)} %copy.11) | data formatting | bytes 4194304 | tf_op jit(solution)/shard_map/reshape | solution.py:439
  (62 shorter events, 2.8 us)
Async XLA Ops:
  0.0 1.6 %copy-start = (f32[32,4,4,1024]{3,2,1,0:T(4,128)S(1)}, f32[32,4,4,1024]{3,2,1,0:T(4,128)}, u32[]{:S(2)}) copy-start(f32[32,4,4,1024]{3,2,1,0:T(4,128)} %raw.1) | copy-start | bytes 6291460
  1.6 27.9 %copy-start.7 = (s32[1,1,16]{2,1,0:T(1,128)S(1)}, s32[1,1,16]{2,1,0:T(1,128)}, u32[]{:S(2)}) copy-start(s32[1,1,16]{2,1,0:T(1,128)} %param.9) | copy-start | bytes 196
  1.6 27.9 %copy-start.8 = (s32[1,1,16]{2,1,0:T(1,128)S(1)}, s32[1,1,16]{2,1,0:T(1,128)}, u32[]{:S(2)}) copy-start(s32[1,1,16]{2,1,0:T(1,128)} %param.10) | copy-start | bytes 196
  1.6 28.6 %copy-start.9 = (f32[1,1,16]{2,1,0:T(1,128)S(1)}, f32[1,1,16]{2,1,0:T(1,128)}, u32[]{:S(2)}) copy-start(f32[1,1,16]{2,1,0:T(1,128)} %param.7) | copy-start | bytes 196
  1.6 28.6 %copy-start.10 = (f32[1,1,16]{2,1,0:T(1,128)S(1)}, f32[1,1,16]{2,1,0:T(1,128)}, u32[]{:S(2)}) copy-start(f32[1,1,16]{2,1,0:T(1,128)} %param.8) | copy-start | bytes 196
  4.7 14.6 %collective-permute-start = (f32[25,32,128]{2,1,0:T(8,128)S(1)}, f32[25,32,128]{2,1,0:T(8,128)S(1)}, u32[]{:S(2)}, u32[]{:S(2)}) collective-permute-start(f32[25,32,128]{2,1,0:T(8,128)S(1)} %get-tuple-element.31), channel_id=1, source_target_pairs={{0,1},{1,2},{2,3},{4,5},{5,6},{6,7},{8,9},{9,10},{10,11},{12,13},{... | collective-permute-start | bytes 1228808 | tf_op jit(solution)/shard_map/ppermute | solution.py:393
  7.9 14.1 %collective-permute-start.1 = (f32[25,32,128]{2,1,0:T(8,128)S(1)}, f32[25,32,128]{2,1,0:T(8,128)S(1)}, u32[]{:S(2)}, u32[]{:S(2)}) collective-permute-start(f32[25,32,128]{2,1,0:T(8,128)S(1)} %get-tuple-element.32), channel_id=1, source_target_pairs={{1,0},{2,1},{3,2},{5,4},{6,5},{7,6},{9,8},{10,9},{11,10},{13,12},{... | collective-permute-start | bytes 1228808 | tf_op jit(solution)/shard_map/ppermute | solution.py:394
  10.0 16.8 %collective-permute-start.7 = (f32[25,32,128]{2,1,0:T(8,128)S(1)}, f32[25,32,128]{2,1,0:T(8,128)S(1)}, u32[]{:S(2)}, u32[]{:S(2)}) collective-permute-start(f32[25,32,128]{2,1,0:T(8,128)S(1)} %get-tuple-element.37), channel_id=1, source_target_pairs={{0,1},{1,2},{2,3},{4,5},{5,6},{6,7},{8,9},{9,10},{10,11},{12,13},{... | collective-permute-start | bytes 1228808 | tf_op jit(solution)/shard_map/ppermute | solution.py:393
  13.2 35.9 %collective-permute-start.8 = (f32[25,32,128]{2,1,0:T(8,128)}, f32[25,32,128]{2,1,0:T(8,128)}, u32[]{:S(2)}, u32[]{:S(2)}) collective-permute-start(f32[25,32,128]{2,1,0:T(8,128)} %get-tuple-element.38), channel_id=1, source_target_pairs={{1,0},{2,1},{3,2},{5,4},{6,5},{7,6},{9,8},{10,9},{11,10},{13,12},{... | collective-permute-start | bytes 1228808 | tf_op jit(solution)/shard_map/ppermute | solution.py:394
  15.3 38.7 %collective-permute-start.14 = (f32[25,32,128]{2,1,0:T(8,128)}, f32[25,32,128]{2,1,0:T(8,128)S(1)}, u32[]{:S(2)}, u32[]{:S(2)}) collective-permute-start(f32[25,32,128]{2,1,0:T(8,128)} %get-tuple-element.43), channel_id=1, source_target_pairs={{0,1},{1,2},{2,3},{4,5},{5,6},{6,7},{8,9},{9,10},{10,11},{12,13},{... | collective-permute-start | bytes 1228808 | tf_op jit(solution)/shard_map/ppermute | solution.py:393
  19.3 0.8 copy-start.3
  20.0 34.4 %collective-permute-start.15 = (f32[25,32,128]{2,1,0:T(8,128)}, f32[25,32,128]{2,1,0:T(8,128)}, u32[]{:S(2)}, u32[]{:S(2)}) collective-permute-start(f32[25,32,128]{2,1,0:T(8,128)} %get-tuple-element.44), channel_id=1, source_target_pairs={{1,0},{2,1},{3,2},{5,4},{6,5},{7,6},{9,8},{10,9},{11,10},{13,12},{... | collective-permute-start | bytes 1228808 | tf_op jit(solution)/shard_map/ppermute | solution.py:394
  22.0 0.7 copy-start.5
  22.7 36.5 %collective-permute-start.21 = (f32[25,32,128]{2,1,0:T(8,128)}, f32[25,32,128]{2,1,0:T(8,128)S(1)}, u32[]{:S(2)}, u32[]{:S(2)}) collective-permute-start(f32[25,32,128]{2,1,0:T(8,128)} %get-tuple-element.49), channel_id=1, source_target_pairs={{0,1},{1,2},{2,3},{4,5},{5,6},{6,7},{8,9},{9,10},{10,11},{12,13},{... | collective-permute-start | bytes 1228808 | tf_op jit(solution)/shard_map/ppermute | solution.py:393
  26.8 0.8 copy-start.1
  27.6 31.7 %collective-permute-start.22 = (f32[25,32,128]{2,1,0:T(8,128)}, f32[25,32,128]{2,1,0:T(8,128)S(1)}, u32[]{:S(2)}, u32[]{:S(2)}) collective-permute-start(f32[25,32,128]{2,1,0:T(8,128)} %get-tuple-element.50), channel_id=1, source_target_pairs={{1,0},{2,1},{3,2},{5,4},{6,5},{7,6},{9,8},{10,9},{11,10},{13,12},{... | collective-permute-start | bytes 1228808 | tf_op jit(solution)/shard_map/ppermute | solution.py:394
  42.8 6.6 %copy-start.2 = (f32[25,32,128]{2,1,0:T(8,128)S(1)}, f32[25,32,128]{2,1,0:T(8,128)}, u32[]{:S(2)}) copy-start(f32[25,32,128]{2,1,0:T(8,128)} %copy-done.1) | copy-start | bytes 1228804
  42.9 1.1 copy-start.4
  43.9 1.0 copy-start.6
  49.1 14.9 %collective-permute-start.2 = (f32[272,128]{1,0:T(8,128)S(1)}, f32[272,128]{1,0:T(8,128)S(1)}, u32[]{:S(2)}, u32[]{:S(2)}) collective-permute-start(f32[272,128]{1,0:T(8,128)S(1)} %get-tuple-element.36), channel_id=1, source_target_pairs={{0,4},{4,0},{8,12},{12,8},{16,20},{20,16},{24,28},{28,24},{1,5},{5... | collective-permute-start | bytes 417800 | tf_op jit(solution)/shard_map/ppermute | solution.py:361
  54.0 11.5 %collective-permute-start.9 = (f32[272,128]{1,0:T(8,128)S(1)}, f32[272,128]{1,0:T(8,128)S(1)}, u32[]{:S(2)}, u32[]{:S(2)}) collective-permute-start(f32[272,128]{1,0:T(8,128)S(1)} %get-tuple-element.42), channel_id=1, source_target_pairs={{0,4},{4,0},{8,12},{12,8},{16,20},{20,16},{24,28},{28,24},{1,5},{5... | collective-permute-start | bytes 417800 | tf_op jit(solution)/shard_map/ppermute | solution.py:361
  59.0 7.7 %collective-permute-start.16 = (f32[272,128]{1,0:T(8,128)S(1)}, f32[272,128]{1,0:T(8,128)S(1)}, u32[]{:S(2)}, u32[]{:S(2)}) collective-permute-start(f32[272,128]{1,0:T(8,128)S(1)} %get-tuple-element.48), channel_id=1, source_target_pairs={{0,4},{4,0},{8,12},{12,8},{16,20},{20,16},{24,28},{28,24},{1,5},{5... | collective-permute-start | bytes 417800 | tf_op jit(solution)/shard_map/ppermute | solution.py:361
  63.6 3.5 %collective-permute-start.23 = (f32[272,128]{1,0:T(8,128)S(1)}, f32[272,128]{1,0:T(8,128)S(1)}, u32[]{:S(2)}, u32[]{:S(2)}) collective-permute-start(f32[272,128]{1,0:T(8,128)S(1)} %get-tuple-element.54), channel_id=1, source_target_pairs={{0,4},{4,0},{8,12},{12,8},{16,20},{20,16},{24,28},{28,24},{1,5},{5... | collective-permute-start | bytes 417800 | tf_op jit(solution)/shard_map/ppermute | solution.py:361
  64.0 5.2 %collective-permute-start.5 = (f32[272,128]{1,0:T(8,128)S(1)}, f32[272,128]{1,0:T(8,128)S(1)}, u32[]{:S(2)}, u32[]{:S(2)}) collective-permute-start(f32[272,128]{1,0:T(8,128)S(1)} %add.50), channel_id=1, source_target_pairs={{0,8},{4,12},{8,0},{12,4},{16,24},{20,28},{24,16},{28,20},{1,9},{5... | collective-permute-start | bytes 417800 | tf_op jit(solution)/shard_map/ppermute | solution.py:366
  64.3 6.0 %collective-permute-start.4 = (f32[272,128]{1,0:T(8,128)S(1)}, f32[272,128]{1,0:T(8,128)S(1)}, u32[]{:S(2)}, u32[]{:S(2)}) collective-permute-start(f32[272,128]{1,0:T(8,128)S(1)} %add.50), channel_id=1, source_target_pairs={{0,16},{4,20},{8,24},{12,28},{16,0},{20,4},{24,8},{28,12},{1,17},{... | collective-permute-start | bytes 417800 | tf_op jit(solution)/shard_map/ppermute | solution.py:366
  65.5 6.6 %collective-permute-start.3 = (f32[272,128]{1,0:T(8,128)S(1)}, f32[272,128]{1,0:T(8,128)S(1)}, u32[]{:S(2)}, u32[]{:S(2)}) collective-permute-start(f32[272,128]{1,0:T(8,128)S(1)} %add.50), channel_id=1, source_target_pairs={{0,24},{4,28},{8,16},{12,20},{16,8},{20,12},{24,0},{28,4},{1,25},{... | collective-permute-start | bytes 417800 | tf_op jit(solution)/shard_map/ppermute | solution.py:366
  66.7 8.4 %collective-permute-start.12 = (f32[272,128]{1,0:T(8,128)S(1)}, f32[272,128]{1,0:T(8,128)S(1)}, u32[]{:S(2)}, u32[]{:S(2)}) collective-permute-start(f32[272,128]{1,0:T(8,128)S(1)} %add.54), channel_id=1, source_target_pairs={{0,8},{4,12},{8,0},{12,4},{16,24},{20,28},{24,16},{28,20},{1,9},{5... | collective-permute-start | bytes 417800 | tf_op jit(solution)/shard_map/ppermute | solution.py:366
  67.1 9.3 %collective-permute-start.11 = (f32[272,128]{1,0:T(8,128)S(1)}, f32[272,128]{1,0:T(8,128)S(1)}, u32[]{:S(2)}, u32[]{:S(2)}) collective-permute-start(f32[272,128]{1,0:T(8,128)S(1)} %add.54), channel_id=1, source_target_pairs={{0,16},{4,20},{8,24},{12,28},{16,0},{20,4},{24,8},{28,12},{1,17},{... | collective-permute-start | bytes 417800 | tf_op jit(solution)/shard_map/ppermute | solution.py:366
  69.1 9.0 %collective-permute-start.10 = (f32[272,128]{1,0:T(8,128)S(1)}, f32[272,128]{1,0:T(8,128)S(1)}, u32[]{:S(2)}, u32[]{:S(2)}) collective-permute-start(f32[272,128]{1,0:T(8,128)S(1)} %add.54), channel_id=1, source_target_pairs={{0,24},{4,28},{8,16},{12,20},{16,8},{20,12},{24,0},{28,4},{1,25},{... | collective-permute-start | bytes 417800 | tf_op jit(solution)/shard_map/ppermute | solution.py:366
  70.3 10.8 %collective-permute-start.19 = (f32[272,128]{1,0:T(8,128)S(1)}, f32[272,128]{1,0:T(8,128)S(1)}, u32[]{:S(2)}, u32[]{:S(2)}) collective-permute-start(f32[272,128]{1,0:T(8,128)S(1)} %add.58), channel_id=1, source_target_pairs={{0,8},{4,12},{8,0},{12,4},{16,24},{20,28},{24,16},{28,20},{1,9},{5... | collective-permute-start | bytes 417800 | tf_op jit(solution)/shard_map/ppermute | solution.py:366
  72.1 10.3 %collective-permute-start.18 = (f32[272,128]{1,0:T(8,128)S(1)}, f32[272,128]{1,0:T(8,128)S(1)}, u32[]{:S(2)}, u32[]{:S(2)}) collective-permute-start(f32[272,128]{1,0:T(8,128)S(1)} %add.58), channel_id=1, source_target_pairs={{0,16},{4,20},{8,24},{12,28},{16,0},{20,4},{24,8},{28,12},{1,17},{... | collective-permute-start | bytes 417800 | tf_op jit(solution)/shard_map/ppermute | solution.py:366
  75.1 10.5 %collective-permute-start.17 = (f32[272,128]{1,0:T(8,128)S(1)}, f32[272,128]{1,0:T(8,128)S(1)}, u32[]{:S(2)}, u32[]{:S(2)}) collective-permute-start(f32[272,128]{1,0:T(8,128)S(1)} %add.58), channel_id=1, source_target_pairs={{0,24},{4,28},{8,16},{12,20},{16,8},{20,12},{24,0},{28,4},{1,25},{... | collective-permute-start | bytes 417800 | tf_op jit(solution)/shard_map/ppermute | solution.py:366
  76.3 10.8 %collective-permute-start.26 = (f32[272,128]{1,0:T(8,128)S(1)}, f32[272,128]{1,0:T(8,128)S(1)}, u32[]{:S(2)}, u32[]{:S(2)}) collective-permute-start(f32[272,128]{1,0:T(8,128)S(1)} %add.62), channel_id=1, source_target_pairs={{0,8},{4,12},{8,0},{12,4},{16,24},{20,28},{24,16},{28,20},{1,9},{5... | collective-permute-start | bytes 417800 | tf_op jit(solution)/shard_map/ppermute | solution.py:366
  78.1 10.7 %collective-permute-start.25 = (f32[272,128]{1,0:T(8,128)S(1)}, f32[272,128]{1,0:T(8,128)S(1)}, u32[]{:S(2)}, u32[]{:S(2)}) collective-permute-start(f32[272,128]{1,0:T(8,128)S(1)} %add.62), channel_id=1, source_target_pairs={{0,16},{4,20},{8,24},{12,28},{16,0},{20,4},{24,8},{28,12},{1,17},{... | collective-permute-start | bytes 417800 | tf_op jit(solution)/shard_map/ppermute | solution.py:366
  81.2 9.0 %collective-permute-start.24 = (f32[272,128]{1,0:T(8,128)S(1)}, f32[272,128]{1,0:T(8,128)S(1)}, u32[]{:S(2)}, u32[]{:S(2)}) collective-permute-start(f32[272,128]{1,0:T(8,128)S(1)} %add.62), channel_id=1, source_target_pairs={{0,24},{4,28},{8,16},{12,20},{16,8},{20,12},{24,0},{28,4},{1,25},{... | collective-permute-start | bytes 417800 | tf_op jit(solution)/shard_map/ppermute | solution.py:366
  82.4 9.1 %collective-permute-start.6 = (f32[272,128]{1,0:T(8,128)S(1)}, f32[272,128]{1,0:T(8,128)S(1)}, u32[]{:S(2)}, u32[]{:S(2)}) collective-permute-start(f32[272,128]{1,0:T(8,128)S(1)} %add_add_fusion.3.own), channel_id=1, source_target_pairs={{0,4},{4,0},{8,12},{12,8},{16,20},{20,16},{24,28},{28,24},{1,5},{5... | collective-permute-start | bytes 417800 | tf_op jit(solution)/shard_map/ppermute | solution.py:370
  85.6 10.6 %collective-permute-start.13 = (f32[272,128]{1,0:T(8,128)S(1)}, f32[272,128]{1,0:T(8,128)S(1)}, u32[]{:S(2)}, u32[]{:S(2)}) collective-permute-start(f32[272,128]{1,0:T(8,128)S(1)} %add_add_fusion.2.own), channel_id=1, source_target_pairs={{0,4},{4,0},{8,12},{12,8},{16,20},{20,16},{24,28},{28,24},{1,5},{5... | collective-permute-start | bytes 417800 | tf_op jit(solution)/shard_map/ppermute | solution.py:370
  87.2 13.9 %collective-permute-start.20 = (f32[272,128]{1,0:T(8,128)S(1)}, f32[272,128]{1,0:T(8,128)S(1)}, u32[]{:S(2)}, u32[]{:S(2)}) collective-permute-start(f32[272,128]{1,0:T(8,128)S(1)} %add_add_fusion.1.own), channel_id=1, source_target_pairs={{0,4},{4,0},{8,12},{12,8},{16,20},{20,16},{24,28},{28,24},{1,5},{5... | collective-permute-start | bytes 417800 | tf_op jit(solution)/shard_map/ppermute | solution.py:370
  90.2 15.7 %collective-permute-start.27 = (f32[272,128]{1,0:T(8,128)S(1)}, f32[272,128]{1,0:T(8,128)S(1)}, u32[]{:S(2)}, u32[]{:S(2)}) collective-permute-start(f32[272,128]{1,0:T(8,128)S(1)} %add_add_fusion.own), channel_id=1, source_target_pairs={{0,4},{4,0},{8,12},{12,8},{16,20},{20,16},{24,28},{28,24},{1,5},{5... | collective-permute-start | bytes 417800 | tf_op jit(solution)/shard_map/ppermute | solution.py:370

commit v2 on v1

v2 whole, which is shorter than its diff:
```python
import copy
import functools

import jax
import jax.numpy as jnp
from jax import lax
from jax.experimental import pallas as pl
from jax.experimental.pallas import tpu as pltpu
from jax.sharding import PartitionSpec as P

NSI = 5
HALO = 3
LANES = 128
SUB = 8

time_step = 0.15
viscosity = 0.1
third_part = 1.0 / 3.0
two_thirds = 2.0 / 3.0

HIGHEST = lax.Precision.HIGHEST
VMEM = pl.BlockSpec(memory_space=pltpu.VMEM)
SMEM = pl.BlockSpec(memory_space=pltpu.SMEM)
HBM = pl.BlockSpec(memory_space=pltpu.HBM)
KERNEL_VMEM = 10 << 20


def call(kernel, out_shape, in_specs, scratch=(), cost=(1 << 20, 1 << 20), name=None, out_spec=VMEM, alias={}):
    flops, nbytes = cost
    return pl.pallas_call(
        kernel,
        out_shape=out_shape,
        in_specs=in_specs,
        out_specs=jax.tree.map(lambda _: out_spec, out_shape),
        scratch_shapes=list(scratch),
        input_output_aliases=alias,
        compiler_params=pltpu.CompilerParams(vmem_limit_bytes=KERNEL_VMEM),
        cost_estimate=pl.CostEstimate(flops=flops, bytes_accessed=nbytes, transcendentals=0),
        name=name,
    )


def chunk_tiles(tiles, most, step):
    most = max(step, most // step * step)
    count = -(-tiles // most)
    units = tiles // step
    return [(units // count + (1 if i < units % count else 0)) * step for i in range(count)]


class Plan:
    def __init__(self, ensemble, slots, groups):
        self.members, self.fields, self.rows, self.columns = ensemble.shape
        self.total = self.members * groups
        self.slots = slots
        self.groups = groups
        self.width = self.columns // groups
        self.tiles = self.columns // LANES
        self.q = max(1, LANES // self.width)
        most = LANES // (slots * self.q)
        self.counts = chunk_tiles(self.tiles, min(most, -(-self.tiles // 2)), max(1, self.width // LANES))
        self.starts = [sum(self.counts[:i]) for i in range(len(self.counts))]
        self.halves = 2
        self.hrows = self.rows // self.halves
        self.hrf = self.hrows * self.fields
        self.edge_groups = HALO * self.fields
        self.per_edge = LANES // (2 * HALO)
        self.edge_tiles = -(-self.edge_groups // self.per_edge)
        self.plain = -(-self.hrf // SUB) * SUB
        self.block = self.hrf * slots + self.plain

    def chunk(self, c):
        p = copy.copy(self)
        p.nt = self.counts[c]
        p.first = self.starts[c]
        p.after = (p.first + p.nt) % self.tiles
        p.before = (p.first - 1) % self.tiles
        p.np = p.nt * LANES // self.width
        p.first_patch = p.first * LANES // self.width
        p.message = p.nt * self.edge_groups + self.edge_tiles
        p.total_rows = p.nt * self.block
        return p

    def patches_of(self, tile):
        if self.width >= LANES:
            return [(tile * LANES // self.width, 0, LANES)]
        return [(tile * self.q + i, i * self.width, (i + 1) * self.width) for i in range(self.q)]


def lane_ids(shape):
    return lax.broadcasted_iota(jnp.int32, shape, len(shape) - 1)


def pack_kernel(plan, raw, state, *messages):
    p = plan
    lane = lane_ids((SUB, LANES))
    chunks = [p.chunk(c) for c in range(len(p.counts))]

    def body(kk, carry):
        mem = pl.ds(pl.multiple_of(kk * SUB, SUB), SUB)
        for c, h in enumerate(chunks):
            up, down = messages[2 * c], messages[2 * c + 1]
            for i in range(h.nt):
                t = h.first + i
                for f in range(p.fields):
                    for r in range(p.rows):
                        x = raw[mem, f, r, t * LANES : (t + 1) * LANES]
                        state[t, r, f, mem, :] = x
                        if r >= p.rows - HALO:
                            up[(i * HALO + r - (p.rows - HALO)) * p.fields + f, mem, :] = x
                        if r < HALO:
                            down[(i * HALO + r) * p.fields + f, mem, :] = x
        for c, h in enumerate(chunks):
            for d in range(2):
                out = messages[2 * c + d]
                for e in range(p.edge_tiles):
                    packed = jnp.zeros((SUB, LANES), jnp.float32)
                    for g in range(e * p.per_edge, min((e + 1) * p.per_edge, p.edge_groups)):
                        i, f = divmod(g, p.fields)
                        r = i + (p.rows - HALO if d == 0 else 0)
                        edge = jnp.where(lane < LANES // 2, state[h.after, r, f, mem, :], state[h.before, r, f, mem, :])
                        place = (g - e * p.per_edge) * 2 * HALO
                        inside = (lane >= place) & (lane < place + 2 * HALO)
                        packed = jnp.where(inside, pltpu.roll(edge, place + HALO, 1), packed)
                    out[h.nt * p.edge_groups + e, mem, :] = packed
        return carry

    lax.fori_loop(0, p.members // SUB, body, 0)


def step_once(p, rows_in, load, store, last):
    lane = lane_ids((SUB, LANES))
    ring = p.nt + 1
    out_tiles = p.nt if last else ring
    for row in range(1, rows_in - 1):
        coef = []
        for t in range(out_tiles):
            u = load(row, 0, t) * (time_step * 0.5)
            v = load(row, 1, t) * (time_step * 0.5)
            k = time_step * viscosity
            coef.append((k - u, k + u, k - v, k + v))
        for f in range(p.fields):
            x = [load(row, f, t) for t in range(ring)]
            right = [pltpu.roll(a, 1, 1) for a in x]
            left = [pltpu.roll(a, LANES - 1, 1) for a in x]
            for t in range(out_tiles):
                west = jnp.where(lane == 0, right[(t - 1) % ring], right[t])
                east = jnp.where(lane == LANES - 1, left[(t + 1) % ring], left[t])
                ce, cw, cn, cs = coef[t]
                moved = (ce * east + cw * west) + (cn * load(row + 1, f, t) + cs * load(row - 1, f, t))
                store(row, f, t, (1.0 - 4.0 * time_step * viscosity) * x[t] + moved)


def place_of(p, cell, patch):
    column = lax.rem(cell, p.width) + patch * p.width
    line = lax.div(cell, p.width)
    return lax.rem(line, p.rows), lax.div(line, p.rows), lax.div(column, LANES), lax.rem(column, LANES)


def forecast_kernel(plan, obs_cell, flags, state, low, high, ahead, seen, keep, send, s0, s1, s2):
    p = plan
    full = p.rows + 2 * HALO
    has_low = flags[0].astype(jnp.float32)
    has_high = flags[1].astype(jnp.float32)
    core = flags[2]
    me = flags[3]
    lane = lane_ids((SUB, LANES))

    def body(kk, carry):
        mem = pl.ds(pl.multiple_of(kk * SUB, SUB), SUB)

        def edge_of(source, g):
            e, place = divmod(g, p.per_edge)
            return pltpu.roll(source[p.nt * p.edge_groups + e, mem, :], (LANES - HALO - place * 2 * HALO) % LANES, 1)

        for f in range(p.fields):
            for r in range(p.rows):
                s0[r + HALO, f] = jnp.where(lane < LANES // 2, state[p.after, r, f, mem, :], state[p.before, r, f, mem, :])
            for i in range(HALO):
                s0[i, f] = edge_of(low, i * p.fields + f)
                s0[HALO + p.rows + i, f] = edge_of(high, i * p.fields + f)

        def load0(row, f, t):
            if t == p.nt:
                return s0[row, f]
            if row < HALO:
                return low[(t * HALO + row) * p.fields + f, mem, :]
            if row >= HALO + p.rows:
                return high[(t * HALO + row - HALO - p.rows) * p.fields + f, mem, :]
            return state[p.first + t, row - HALO, f, mem, :]

        def keep_zero(row, value):
            if row < HALO:
                return value * has_low
            if row >= HALO + p.rows:
                return value * has_high
            return value

        def store1(row, f, t, stepped):
            s1[row, f, t] = keep_zero(row, stepped)

        def store2(row, f, t, stepped):
            row = row + 1
            s2[row, f, t] = keep_zero(row, 0.75 * load0(row, f, t) + 0.25 * stepped)

        def store3(row, f, t, stepped):
            row = row + 2
            ahead[t, row - HALO, f, mem, :] = third_part * load0(row, f, t) + two_thirds * stepped

        step_once(p, full, load0, store1, False)
        step_once(p, full - 2, lambda row, f, t: s1[row + 1, f, t], store2, False)
        step_once(p, full - 4, lambda row, f, t: s2[row + 2, f, t], store3, True)
        return carry

    lax.fori_loop(0, p.members // SUB, body, 0)

    wide = lane_ids((p.members, LANES))
    found = jnp.zeros((p.members, LANES), jnp.float32)
    for j in range(p.np):
        at = ((p.first_patch + j) ^ me) * p.slots
        for o in range(p.slots):
            r, f, t, column = place_of(p, obs_cell[at + o], j)
            to = j * p.slots + o
            found = jnp.where(wide == to, pltpu.roll(ahead[t, r, f], lax.rem(to + LANES - column, LANES), 1), found)
    seen[...] = found

    last = lax.broadcasted_iota(jnp.int32, (SUB, p.members), 0)
    ones = jnp.where(last == 0, 1.0, 0.0).astype(jnp.float32)
    turned = jnp.transpose(found)
    sides = [jnp.concatenate([turned[j * p.slots : (j + 1) * p.slots], ones], axis=0) for j in range(p.np)]
    for side in range(p.halves):
        out = keep if side == 0 else send
        half = core if side == 0 else 1 - core
        for t in range(p.nt):
            base = t * p.block
            tiles = [ahead[t, half * p.hrows + i // p.fields, i % p.fields] for i in range(p.hrf)]
            joined = jnp.concatenate(tiles, axis=1)
            result = None
            for j, first, stop in p.patches_of(t):
                part = jnp.dot(sides[j], joined, precision=HIGHEST, preferred_element_type=jnp.float32)
                if result is None:
                    result = part
                else:
                    at = lane_ids(part.shape) % LANES
                    result = jnp.where((at >= first) & (at < stop), part, result)
            for i in range(p.hrf):
                piece = result[:, i * LANES : (i + 1) * LANES]
                out[pl.ds(base + i * p.slots, p.slots), :] = piece[: p.slots]
                out[pl.ds(base + p.hrf * p.slots + i, 1), :] = piece[p.slots : p.slots + 1]
            for i in range(p.hrf, p.plain):
                out[pl.ds(base + p.hrf * p.slots + i, 1), :] = jnp.zeros((1, LANES), jnp.float32)


def finish_kernel(plan, obs_cell, flags, obs, ahead, seen, own, other, *rest):
    out, staged, sems = rest[-3:]
    p = plan
    n = p.slots
    core = flags[2]
    me = flags[3]
    free = p.total - 1.0
    shape = (n, LANES)
    lane = lane_ids(shape)
    row = lax.broadcasted_iota(jnp.int32, shape, 0)
    group = lane // n * n
    eye = jnp.where(lane - group == row, 1.0, 0.0).astype(jnp.float32)
    lane_row = lane_ids((1, LANES))
    lane_sub = lane_ids((SUB, LANES))

    def pick(a, index):
        return jnp.take_along_axis(a, index, axis=1)

    def col(a):
        return pick(jnp.broadcast_to(a, shape), group + row)

    def spread_out(a):
        base = lane_ids(a.shape) // n * n
        return [pick(a, base + k) for k in range(n)]

    def product(parts, b):
        total = parts[0] * b[0:1]
        for k in range(1, n):
            total = total + parts[k] * b[k : k + 1]
        return total

    moments = jnp.zeros(shape, jnp.float32)
    sums = jnp.zeros((SUB, LANES), jnp.float32)
    given = [jnp.zeros((SUB, LANES), jnp.float32) for _ in range(4)]
    for j in range(p.np):
        source = (p.first_patch + j) ^ me
        line = jnp.broadcast_to(obs[pl.ds(source, 1), :], (SUB, LANES))
        mine = (lane_sub >= j * n) & (lane_sub < (j + 1) * n)
        for i in range(4):
            given[i] = jnp.where(mine, pltpu.roll(line, (j * n - i * n) % LANES, 1), given[i])
        for o in range(n):
            r, f, t, column = place_of(p, obs_cell[source * n + o], j)
            index = lax.rem(r, p.hrows) * p.fields + f
            here = lax.div(r, p.hrows) == core
            to = j * n + o
            shift = lax.rem(to + LANES - column, LANES)
            at = pl.ds(pl.multiple_of(t * p.block + index * n, SUB), n)
            value = jnp.where(here, own[at, :], other[at, :])
            moments = jnp.where(lane == to, pltpu.roll(value, shift, 1), moments)
            at = pl.ds(t * p.block + p.hrf * n + index, 1)
            value = jnp.broadcast_to(jnp.where(here, own[at, :], other[at, :]), (SUB, LANES))
            sums = jnp.where(lane_sub == to, pltpu.roll(value, shift, 1), sums)
    value, variance, loop, count = (a[0:1] for a in given)
    mean = sums[0:1] * (1.0 / p.total)
    slot = (lane_row % n).astype(jnp.float32)
    used = lane_row < p.np * n
    weight = jnp.where(used & (slot < count), jnp.exp(-0.35 * loop) / jnp.where(used, variance, 1.0), 0.0)
    root = jnp.sqrt(weight)
    root_col = col(root)
    mean_col = col(mean)
    scaled = root_col * (moments - p.total * mean_col * mean) * root
    bound = free + 0.5 * jnp.sum(pick(scaled, group + row), axis=0, keepdims=True)
    inverse = 1.0 / bound

    small = scaled * inverse
    t0 = free * inverse
    tf = t0 * eye + small
    tg = eye
    z0 = jnp.ones((1, LANES), jnp.float32)
    zg = None
    for repeat in range(NSI):
        f0 = 1.5 - 0.5 * t0
        ff = 1.5 * eye - 0.5 * tf
        parts = spread_out(ff)
        if zg is None:
            zg = -0.5 * z0 * tg
        else:
            zg = product(parts, zg) - 0.5 * z0 * tg
        z0 = z0 * f0
        if repeat < NSI - 1:
            square = product(parts, ff)
            bend = square - (0.5 * t0) * (ff + f0 * eye)
            tf = product(spread_out(square), tf)
            tg = bend if repeat == 0 else product(spread_out(bend), tg)
            t0 = t0 * f0 * f0
    zf = z0 * eye + product(spread_out(small), zg)
    scale = jnp.sqrt(free * inverse)
    spread = (scale * inverse) * root_col * zg * root
    down = root * (value - mean)
    for repeat in range(2):
        down = jnp.sum(zf * col(down), axis=0, keepdims=True)
    weights = product(spread_out(seen[...] - mean), spread) + root * down * inverse
    spread0 = scale * z0

    for t in range(p.nt):
        for half in range(p.halves):
            at_own = half == core
            pieces = []
            for i in range(p.hrf):
                at = t * p.block + i * n
                pieces.append(jnp.where(at_own, own[at : at + n, :], other[at : at + n, :]))
            base = t * p.block + p.hrf * n
            plain = jnp.where(at_own, own[base : base + p.plain, :], other[base : base + p.plain, :])
            results = []
            for j, first, stop in p.patches_of(t):
                mine = pltpu.roll(weights, (LANES - j * n) % LANES, 1)[:, :n]
                centre = pick(jnp.broadcast_to(mean, shape), row + j * n)
                keep0 = pick(jnp.broadcast_to(spread0, (SUB, LANES)), jnp.full((SUB, LANES), j * n, jnp.int32))[0:1]
                centred = [pieces[i] - centre * plain[i : i + 1, :] for i in range(p.hrf)]
                update = jnp.dot(mine, jnp.concatenate(centred, axis=1), precision=HIGHEST, preferred_element_type=jnp.float32)
                results.append((update, keep0, first, stop))
            for i in range(p.hrf):
                r, f = half * p.hrows + i // p.fields, i % p.fields
                x = ahead[t, r, f]
                centre = plain[i : i + 1, :] * (1.0 / p.total)
                final = None
                for update, keep0, first, stop in results:
                    part = centre + keep0 * (x - centre) + update[:, i * LANES : (i + 1) * LANES]
                    if final is None:
                        final = part
                    else:
                        at = lane_ids(part.shape)
                        final = jnp.where((at >= first) & (at < stop), part, final)
                staged[:, f, r, t * LANES : (t + 1) * LANES] = final
        cols = pl.ds((p.first + t) * LANES, LANES)
        pltpu.make_async_copy(staged.at[:, :, :, pl.ds(t * LANES, LANES)], out.at[:, :, :, cols], sems.at[t]).start()
    for t in range(p.nt):
        cols = pl.ds((p.first + t) * LANES, LANES)
        pltpu.make_async_copy(staged.at[:, :, :, pl.ds(t * LANES, LANES)], out.at[:, :, :, cols], sems.at[t]).wait()


def total_over_members(plan, keep, send):
    p = plan
    members = range(p.groups)
    bits = [1 << i for i in range(1, p.groups.bit_length() - 1)]
    total = keep + lax.ppermute(send, "mem", [(i, i ^ 1) for i in members])
    for phase in range(len(bits)):
        even = bits[phase]
        odd = bits[(phase + len(bits) // 2) % len(bits)]
        total = total + lax.ppermute(total, "mem", [(i, i ^ (odd if i & 1 else even)) for i in members])
    return total, lax.ppermute(total, "mem", [(i, i ^ 1) for i in members])


def per_device(ensemble, obs_value, obs_var, obs_cell, obs_loop, obs_count):
    groups = lax.axis_size("mem")
    bands = lax.axis_size("lat")
    slots = obs_cell.shape[-1]
    p = Plan(ensemble, slots, groups)
    chunks = [p.chunk(c) for c in range(len(p.counts))]
    f32 = jnp.float32
    shape = jax.ShapeDtypeStruct

    out = call(
        functools.partial(pack_kernel, p),
        [shape((p.tiles, p.rows, p.fields, p.members, LANES), f32)]
        + [shape((h.message, p.members, LANES), f32) for h in chunks for _ in range(2)],
        [VMEM],
        name="pack",
    )(ensemble)
    state, messages = out[0], out[1:]
    up = [(i, i + 1) for i in range(bands - 1)]
    down = [(i + 1, i) for i in range(bands - 1)]
    low, high = [], []
    for c in range(len(chunks)):
        low.append(lax.ppermute(messages[2 * c], "lat", up))
        high.append(lax.ppermute(messages[2 * c + 1], "lat", down))

    obs = jnp.concatenate(
        [
            obs_value[0],
            obs_var[0],
            obs_loop[0].astype(f32),
            jnp.broadcast_to(obs_count[0][:, None].astype(f32), (1, slots)),
            obs_cell[0].astype(f32),
        ],
        axis=1,
    )
    obs = jnp.pad(obs, ((0, 0), (0, -obs.shape[1] % LANES)))
    bit = 1
    while bit < groups:
        there = lax.ppermute(obs, "mem", [(i, i ^ bit) for i in range(groups)])
        obs = jnp.concatenate([obs, there], axis=0)
        bit *= 2
    cells = obs[:, 4 * slots : 5 * slots].astype(jnp.int32).reshape(groups * slots)

    band = lax.axis_index("lat")
    me = lax.axis_index("mem")
    flags = jnp.stack([band > 0, band < bands - 1, lax.rem(me, 2), me]).astype(jnp.int32)

    new = None
    for c, h in enumerate(chunks):
        stage = (p.rows + 2 * HALO, p.fields, h.nt + 1, SUB, LANES)
        ahead, seen, keep, send = call(
            functools.partial(forecast_kernel, h),
            [
                shape((h.nt, p.rows, p.fields, p.members, LANES), f32),
                shape((p.members, LANES), f32),
                shape((h.total_rows, LANES), f32),
                shape((h.total_rows, LANES), f32),
            ],
            [SMEM, SMEM, VMEM, VMEM, VMEM],
            [pltpu.VMEM(stage[:2] + stage[3:], f32), pltpu.VMEM(stage, f32), pltpu.VMEM(stage, f32)],
            name="forecast",
        )(cells, flags, state, low[c], high[c])
        own, other = total_over_members(p, keep, send)
        before = [] if new is None else [new]
        new = call(
            functools.partial(finish_kernel, h),
            shape(ensemble.shape, f32),
            [SMEM, SMEM, VMEM, VMEM, VMEM, VMEM, VMEM] + [HBM] * len(before),
            [pltpu.VMEM((p.members, p.fields, p.rows, h.nt * LANES), f32), pltpu.SemaphoreType.DMA((h.nt,))],
            name="finish",
            out_spec=HBM,
            alias={7: 0} if before else {},
        )(cells, flags, obs, ahead, seen, own, other, *before)
    return new


def solution(mesh):
    placed = (
        P("mem", None, "lat", None),
        P(None, ("mem", "lat"), None),
        P(None, ("mem", "lat"), None),
        P(None, ("mem", "lat"), None),
        P(None, ("mem", "lat"), None),
        P(None, ("mem", "lat")),
    )
    return jax.shard_map(
        per_device,
        mesh=mesh,
        in_specs=placed,
        out_specs=P("mem", None, "lat", None),
        check_vma=False,
    )
```

time: 116 us -> 92.1 us (0.79)
  waiting for transfers between devices: 9.53 us -> 36.7 us
  starting transfers between devices: 41.3 us -> 22.9 us
  Pallas kernels: 40.1 us -> 28.3 us
  blocking collectives: 11.2 us -> 0 us
  local copies, waits for them, and re-layouts: 9.61 us -> 1.8 us
    ppermute x4 -> x2, waiting for transfers between devices: 0.01 us -> 17.7 us  [per_device(): low.append(lax.ppermute(messages[2 * c], 'lat', up))]
    pallas_call x8 -> x4, Pallas kernels: 37 us -> 25 us  [the longest x2 14 us: per_device(): call(functools.partial(forecast_kernel, h), [shape((h.nt, p.rows, p.field...]
    all_gather x1 -> x0, blocking collectives: 11.2 us -> none  [per_device(): lax.all_gather(mine, 'mem', axis=0, tiled=True).reshape(groups, 5, slots)]
    ppermute x4 -> x2, starting transfers between devices: 14.5 us -> 7.27 us  [per_device(): low.append(lax.ppermute(messages[2 * c], 'lat', up))]
    ppermute x20 -> x11, starting transfers between devices: 18.9 us -> 11.7 us  [the longest x2 3.32 us: total_over_members(): return (total, lax.ppermute(total, 'mem', [(i, i ^ 1) for i in members]))]
    ppermute x20 -> x11, waiting for transfers between devices: 9.51 us -> 16 us  [the longest x4 10.9 us: total_over_members(): lax.ppermute(total, 'mem', [(i, i ^ (odd if i & 1 else even)) for i in me...]
    unnamed x22 -> x10, local copies, waits for them, and re-layouts: 5.89 us -> 1.61 us
    ppermute x4 -> x2, starting transfers between devices: 7.95 us -> 4 us  [per_device(): high.append(lax.ppermute(messages[2 * c + 1], 'lat', down))]
  transfers between devices with their start and end apart: 28 -> 15, of which waited for: 7 -> 10; matrix products, arithmetic and copies ran while one was open for 1% -> 1% of each run, Pallas kernels for 28% -> 21%
where the time goes in v2:
time: 92.1 us; the launch traced here: 90.9 us
  waiting for transfers between devices  36.7 us (40%)
  Pallas kernels  28.3 us (31%)
  starting transfers between devices  22.9 us (25%)
  local copies, waits for them, and re-layouts  1.8 us (2%)
    ppermute x2, waiting for transfers between devices, per_device(): low.append(lax.ppermute(messages[2 * c], 'lat', up))  17.7 us
    pallas_call x2, Pallas kernels, per_device(): call(functools.partial(forecast_kernel, h), [shape((h.nt, p.rows, p.field...  14 us
    pallas_call x2, Pallas kernels, per_device(): call(functools.partial(finish_kernel, h), shape(ensemble.shape, f32), [SM...  11 us
    ppermute x4, waiting for transfers between devices, total_over_members(): lax.ppermute(total, 'mem', [(i, i ^ (odd if i & 1 else even)) for i in me...  10.9 us
    ppermute x2, starting transfers between devices, per_device(): low.append(lax.ppermute(messages[2 * c], 'lat', up))  7.27 us
    ppermute x3, waiting for transfers between devices, per_device(): there = lax.ppermute(obs, 'mem', [(i, i ^ bit) for i in range(groups)])  4.9 us
    ppermute x2, starting transfers between devices, per_device(): high.append(lax.ppermute(messages[2 * c + 1], 'lat', down))  4 us
    ppermute x2, starting transfers between devices, total_over_members(): return (total, lax.ppermute(total, 'mem', [(i, i ^ 1) for i in members]))  3.32 us
  transfers between devices with their start and end apart: 15, of which 10 were waited for; matrix products, arithmetic and copies ran while one was open for 1% of the time, Pallas kernels for 21%

profile of v2, /device:TPU:19, one launch (start us, length us, event | category | flops | bytes accessed | tf_op | source)
XLA Modules:
  0.0 90.9 jit_solution(11195094701776192252)
XLA Ops:
  0.0 0.0 copy-start
  0.0 1.6 %copy-done = f32[32,4,4,1024]{3,2,1,0:T(4,128)S(1)} copy-done((f32[32,4,4,1024]{3,2,1,0:T(4,128)S(1)}, f32[32,4,4,1024]{3,2,1,0:T(4,128)}, u32[]{:S(2)}) %copy-start) | copy-done | bytes 2097176
  1.6 0.0 copy-start.1
  1.6 0.0 copy-start.2
  1.6 0.0 copy-start.3
  1.6 3.3 %pack.1 = (f32[8,4,4,32,128]{4,3,2,1,0:T(8,128)S(1)}, f32[49,32,128]{2,1,0:T(8,128)}, f32[49,32,128]{2,1,0:T(8,128)}, f32[49,32,128]{2,1,0:T(8,128)}, f32[49,32,128]{2,1,0:T(8,128)}) custom-call(f32[32,4,4,1024]{3,2,1,0:T(4,128)S(1)} %copy-done), custom_call_target="tpu_custom_call" | custom-call | flops 1048576 | bytes 1048576 | tf_op jit(solution)/shard_map/pack/pallas_call | solution.py:405
  4.9 3.2 %collective-permute-start.3 = (f32[49,32,128]{2,1,0:T(8,128)}, f32[49,32,128]{2,1,0:T(8,128)S(1)}, u32[]{:S(2)}, u32[]{:S(2)}) collective-permute-start(f32[49,32,128]{2,1,0:T(8,128)} %get-tuple-element.19), channel_id=1, source_target_pairs={{0,1},{1,2},{2,3},{4,5},{5,6},{6,7},{8,9},{9,10},{10,11},{12,13},{... | collective-permute-start | bytes 2408456 | tf_op jit(solution)/shard_map/ppermute | solution.py:417
  8.1 2.1 %collective-permute-start.4 = (f32[49,32,128]{2,1,0:T(8,128)}, f32[49,32,128]{2,1,0:T(8,128)}, u32[]{:S(2)}, u32[]{:S(2)}) collective-permute-start(f32[49,32,128]{2,1,0:T(8,128)} %get-tuple-element.20), channel_id=1, source_target_pairs={{1,0},{2,1},{3,2},{5,4},{6,5},{7,6},{9,8},{10,9},{11,10},{13,12},{... | collective-permute-start | bytes 2408456 | tf_op jit(solution)/shard_map/ppermute | solution.py:418
  10.2 4.1 %collective-permute-start.9 = (f32[49,32,128]{2,1,0:T(8,128)}, f32[49,32,128]{2,1,0:T(8,128)}, u32[]{:S(2)}, u32[]{:S(2)}) collective-permute-start(f32[49,32,128]{2,1,0:T(8,128)} %get-tuple-element.25), channel_id=1, source_target_pairs={{0,1},{1,2},{2,3},{4,5},{5,6},{6,7},{8,9},{9,10},{10,11},{12,13},{... | collective-permute-start | bytes 2408456 | tf_op jit(solution)/shard_map/ppermute | solution.py:417
  14.3 1.9 %collective-permute-start.10 = (f32[49,32,128]{2,1,0:T(8,128)}, f32[49,32,128]{2,1,0:T(8,128)}, u32[]{:S(2)}, u32[]{:S(2)}) collective-permute-start(f32[49,32,128]{2,1,0:T(8,128)} %get-tuple-element.26), channel_id=1, source_target_pairs={{1,0},{2,1},{3,2},{5,4},{6,5},{7,6},{9,8},{10,9},{11,10},{13,12},{... | collective-permute-start | bytes 2408456 | tf_op jit(solution)/shard_map/ppermute | solution.py:418
  16.9 0.0 copy-done.1
  16.9 0.0 copy-done.2
  16.9 0.0 copy-done.3
  16.9 0.0 copy-done.4
  16.9 0.1 concatenate.14
  17.0 1.6 %collective-permute-start = (f32[1,128]{1,0:T(1,128)S(1)}, f32[1,128]{1,0:T(1,128)S(1)}, u32[]{:S(2)}, u32[]{:S(2)}) collective-permute-start(f32[1,128]{1,0:T(1,128)S(1)} %pad.4), channel_id=1, source_target_pairs={{0,4},{4,0},{8,12},{12,8},{16,20},{20,16},{24,28},{28,24},{1,5},{5... | collective-permute-start | bytes 1544 | tf_op jit(solution)/shard_map/ppermute | solution.py:433
  18.6 0.8 collective-permute-done
  19.4 0.3 collective-permute-start.1
  19.7 2.6 %collective-permute-done.1 = f32[2,128]{1,0:T(2,128)S(1)} collective-permute-done((f32[2,128]{1,0:T(2,128)S(1)}, f32[2,128]{1,0:T(2,128)S(1)}, u32[]{:S(2)}, u32[]{:S(2)}) %collective-permute-start.1) | collective-permute-done | bytes 1056 | tf_op jit(solution)/shard_map/ppermute | solution.py:433
  22.3 1.3 %collective-permute-start.2 = (f32[4,128]{1,0:T(4,128)S(1)}, f32[4,128]{1,0:T(4,128)S(1)}, u32[]{:S(2)}, u32[]{:S(2)}) collective-permute-start(f32[4,128]{1,0:T(4,128)S(1)} %pad_maximum_fusion.1), channel_id=1, source_target_pairs={{0,16},{4,20},{8,24},{12,28},{16,0},{20,4},{24,8},{28,12},{1,17},{... | collective-permute-start | bytes 6152 | tf_op jit(solution)/shard_map/ppermute | solution.py:433
  23.6 0.1 pad_add_fusion.flags
  23.7 1.5 %collective-permute-done.2 = f32[4,128]{1,0:T(4,128)S(1)} collective-permute-done((f32[4,128]{1,0:T(4,128)S(1)}, f32[4,128]{1,0:T(4,128)S(1)}, u32[]{:S(2)}, u32[]{:S(2)}) %collective-permute-start.2) | collective-permute-done | bytes 2080 | tf_op jit(solution)/shard_map/ppermute | solution.py:433
  25.2 0.1 slice_convert_fusion
  25.3 0.1 reshape.31.obs_cell
  25.3 17.7 %collective-permute-done.9.low = f32[49,32,128]{2,1,0:T(8,128)} collective-permute-done((f32[49,32,128]{2,1,0:T(8,128)}, f32[49,32,128]{2,1,0:T(8,128)}, u32[]{:S(2)}, u32[]{:S(2)}) %collective-permute-start.9) | collective-permute-done | bytes 802848 | tf_op jit(solution)/shard_map/ppermute | solution.py:417
  43.1 2.9 %collective-permute-done.10.high = f32[49,32,128]{2,1,0:T(8,128)} collective-permute-done((f32[49,32,128]{2,1,0:T(8,128)}, f32[49,32,128]{2,1,0:T(8,128)}, u32[]{:S(2)}, u32[]{:S(2)}) %collective-permute-start.10) | collective-permute-done | bytes 802848 | tf_op jit(solution)/shard_map/ppermute | solution.py:418
  46.0 7.1 %forecast.3 = (f32[4,4,4,32,128]{4,3,2,1,0:T(8,128)S(1)}, f32[32,128]{1,0:T(8,128)S(1)}, f32[544,128]{1,0:T(8,128)S(1)}, f32[544,128]{1,0:T(8,128)S(1)}) custom-call(s32[128]{0:T(128)S(1)} %reshape.31.obs_cell, s32[4]{0:T(128)S(1)} %pad_add_fusion.flags, f32[8,4,4,32,128]{4,3,2,1,0:T(8,128)S(1)} %get-tuple-element.18.state, ...), custom_call_target="tpu_custom_call" | custom-call | flops 1048576 | bytes 1048576 | tf_op jit(solution)/shard_map/forecast/pallas_call | solution.py:445
  53.1 1.9 %collective-permute-start.11 = (f32[544,128]{1,0:T(8,128)S(1)}, f32[544,128]{1,0:T(8,128)S(1)}, u32[]{:S(2)}, u32[]{:S(2)}) collective-permute-start(f32[544,128]{1,0:T(8,128)S(1)} %get-tuple-element.30), channel_id=1, source_target_pairs={{0,4},{4,0},{8,12},{12,8},{16,20},{20,16},{24,28},{28,24},{1,5},{5... | collective-permute-start | bytes 835592 | tf_op jit(solution)/shard_map/ppermute | solution.py:388
  55.0 0.0 collective-permute-done.3.low
  55.0 0.0 collective-permute-done.4.high
  55.0 6.9 %forecast.2 = (f32[4,4,4,32,128]{4,3,2,1,0:T(8,128)S(1)}, f32[32,128]{1,0:T(8,128)S(1)}, f32[544,128]{1,0:T(8,128)S(1)}, f32[544,128]{1,0:T(8,128)S(1)}) custom-call(s32[128]{0:T(128)S(1)} %reshape.31.obs_cell, s32[4]{0:T(128)S(1)} %pad_add_fusion.flags, f32[8,4,4,32,128]{4,3,2,1,0:T(8,128)S(1)} %get-tuple-element.18.state, ...), custom_call_target="tpu_custom_call" | custom-call | flops 1048576 | bytes 1048576 | tf_op jit(solution)/shard_map/forecast/pallas_call | solution.py:445
  61.9 0.1 collective-permute-start.5
  62.0 0.0 collective-permute-done.11
  62.0 1.3 %collective-permute-start.12 = (f32[544,128]{1,0:T(8,128)S(1)}, f32[544,128]{1,0:T(8,128)S(1)}, u32[]{:S(2)}, u32[]{:S(2)}) collective-permute-start(f32[544,128]{1,0:T(8,128)S(1)} %add.23), channel_id=1, source_target_pairs={{0,8},{4,20},{8,0},{12,28},{16,24},{20,4},{24,16},{28,12},{1,9},{5... | collective-permute-start | bytes 835592 | tf_op jit(solution)/shard_map/ppermute | solution.py:392
  63.3 0.2 collective-permute-done.5
  63.5 1.3 %collective-permute-start.6 = (f32[544,128]{1,0:T(8,128)S(1)}, f32[544,128]{1,0:T(8,128)S(1)}, u32[]{:S(2)}, u32[]{:S(2)}) collective-permute-start(f32[544,128]{1,0:T(8,128)S(1)} %add.20), channel_id=1, source_target_pairs={{0,8},{4,20},{8,0},{12,28},{16,24},{20,4},{24,16},{28,12},{1,9},{5... | collective-permute-start | bytes 835592 | tf_op jit(solution)/shard_map/ppermute | solution.py:392
  64.8 2.9 %collective-permute-done.12 = f32[544,128]{1,0:T(8,128)S(1)} collective-permute-done((f32[544,128]{1,0:T(8,128)S(1)}, f32[544,128]{1,0:T(8,128)S(1)}, u32[]{:S(2)}, u32[]{:S(2)}) %collective-permute-start.12) | collective-permute-done | bytes 278560 | tf_op jit(solution)/shard_map/ppermute | solution.py:392
  67.8 0.3 collective-permute-start.13
  68.1 2.6 %collective-permute-done.6 = f32[544,128]{1,0:T(8,128)S(1)} collective-permute-done((f32[544,128]{1,0:T(8,128)S(1)}, f32[544,128]{1,0:T(8,128)S(1)}, u32[]{:S(2)}, u32[]{:S(2)}) %collective-permute-start.6) | collective-permute-done | bytes 278560 | tf_op jit(solution)/shard_map/ppermute | solution.py:392
  70.8 0.3 collective-permute-start.7
  71.1 3.6 %collective-permute-done.13 = f32[544,128]{1,0:T(8,128)S(1)} collective-permute-done((f32[544,128]{1,0:T(8,128)S(1)}, f32[544,128]{1,0:T(8,128)S(1)}, u32[]{:S(2)}, u32[]{:S(2)}) %collective-permute-start.13) | collective-permute-done | bytes 278560 | tf_op jit(solution)/shard_map/ppermute | solution.py:392
  74.7 1.1 %collective-permute-start.14 = (f32[544,128]{1,0:T(8,128)S(1)}, f32[544,128]{1,0:T(8,128)S(1)}, u32[]{:S(2)}, u32[]{:S(2)}) collective-permute-start(f32[544,128]{1,0:T(8,128)S(1)} %add.25.own), channel_id=1, source_target_pairs={{0,4},{4,0},{8,12},{12,8},{16,20},{20,16},{24,28},{28,24},{1,5},{5... | collective-permute-start | bytes 835592 | tf_op jit(solution)/shard_map/ppermute | solution.py:393
  75.8 1.8 %collective-permute-done.7 = f32[544,128]{1,0:T(8,128)S(1)} collective-permute-done((f32[544,128]{1,0:T(8,128)S(1)}, f32[544,128]{1,0:T(8,128)S(1)}, u32[]{:S(2)}, u32[]{:S(2)}) %collective-permute-start.7) | collective-permute-done | bytes 278560 | tf_op jit(solution)/shard_map/ppermute | solution.py:392
  77.7 2.2 %collective-permute-start.8 = (f32[544,128]{1,0:T(8,128)S(1)}, f32[544,128]{1,0:T(8,128)S(1)}, u32[]{:S(2)}, u32[]{:S(2)}) collective-permute-start(f32[544,128]{1,0:T(8,128)S(1)} %add.22.own), channel_id=1, source_target_pairs={{0,4},{4,0},{8,12},{12,8},{16,20},{20,16},{24,28},{28,24},{1,5},{5... | collective-permute-start | bytes 835592 | tf_op jit(solution)/shard_map/ppermute | solution.py:393
  79.9 0.0 collective-permute-done.14.other
  79.9 5.5 %finish.2.rest_0_ = f32[32,4,4,1024]{3,2,1,0:T(4,128)} custom-call(s32[128]{0:T(128)S(1)} %reshape.31.obs_cell, s32[4]{0:T(128)S(1)} %pad_add_fusion.flags, f32[8,128]{1,0:T(8,128)S(1)} %pad_maximum_fusion.obs, f32[4,4,4,32,128]{4,3,2,1,0:T(8,128)S(1)} %get-tuple-element.27.ahead, f32[32,128]{1,0:T(8,128)S(1)} %get-tuple-element.28.seen, ...), custom_call_target="tpu_custom_call" | custom-call | flops 1048576 | bytes 1048576 | tf_op jit(solution)/shard_map/finish/pallas_call | solution.py:459
  85.4 0.0 collective-permute-done.8.other
  85.4 5.5 %finish.3 = f32[32,4,4,1024]{3,2,1,0:T(4,128)} custom-call(s32[128]{0:T(128)S(1)} %reshape.31.obs_cell, s32[4]{0:T(128)S(1)} %pad_add_fusion.flags, f32[8,128]{1,0:T(8,128)S(1)} %pad_maximum_fusion.obs, f32[4,4,4,32,128]{4,3,2,1,0:T(8,128)S(1)} %get-tuple-element.21.ahead, f32[32,128]{1,0:T(8,128)S(1)} %get-tuple-element.22.seen, ...), custom_call_target="tpu_custom_call", output_to_operand_aliasing={{}: (7, {})} | custom-call | flops 1048576 | bytes 1048576 | tf_op jit(solution)/shard_map/finish/pallas_call | solution.py:459
  (13 shorter events, 0.2 us)
Async XLA Ops:
  0.0 1.6 %copy-start = (f32[32,4,4,1024]{3,2,1,0:T(4,128)S(1)}, f32[32,4,4,1024]{3,2,1,0:T(4,128)}, u32[]{:S(2)}) copy-start(f32[32,4,4,1024]{3,2,1,0:T(4,128)} %raw.1) | copy-start | bytes 6291460
  1.6 15.3 %copy-start.1 = (s32[1,1,16]{2,1,0:T(1,128)S(1)}, s32[1,1,16]{2,1,0:T(1,128)}, u32[]{:S(2)}) copy-start(s32[1,1,16]{2,1,0:T(1,128)} %param.9) | copy-start | bytes 196
  1.6 15.3 %copy-start.2 = (s32[1,1,16]{2,1,0:T(1,128)S(1)}, s32[1,1,16]{2,1,0:T(1,128)}, u32[]{:S(2)}) copy-start(s32[1,1,16]{2,1,0:T(1,128)} %param.10) | copy-start | bytes 196
  1.6 15.3 %copy-start.3 = (f32[1,1,16]{2,1,0:T(1,128)S(1)}, f32[1,1,16]{2,1,0:T(1,128)}, u32[]{:S(2)}) copy-start(f32[1,1,16]{2,1,0:T(1,128)} %param.7) | copy-start | bytes 196
  1.6 15.3 %copy-start.4 = (f32[1,1,16]{2,1,0:T(1,128)S(1)}, f32[1,1,16]{2,1,0:T(1,128)}, u32[]{:S(2)}) copy-start(f32[1,1,16]{2,1,0:T(1,128)} %param.8) | copy-start | bytes 196
  4.9 50.1 %collective-permute-start.3 = (f32[49,32,128]{2,1,0:T(8,128)}, f32[49,32,128]{2,1,0:T(8,128)S(1)}, u32[]{:S(2)}, u32[]{:S(2)}) collective-permute-start(f32[49,32,128]{2,1,0:T(8,128)} %get-tuple-element.19), channel_id=1, source_target_pairs={{0,1},{1,2},{2,3},{4,5},{5,6},{6,7},{8,9},{9,10},{10,11},{12,13},{... | collective-permute-start | bytes 2408456 | tf_op jit(solution)/shard_map/ppermute | solution.py:417
  8.1 46.9 %collective-permute-start.4 = (f32[49,32,128]{2,1,0:T(8,128)}, f32[49,32,128]{2,1,0:T(8,128)}, u32[]{:S(2)}, u32[]{:S(2)}) collective-permute-start(f32[49,32,128]{2,1,0:T(8,128)} %get-tuple-element.20), channel_id=1, source_target_pairs={{1,0},{2,1},{3,2},{5,4},{6,5},{7,6},{9,8},{10,9},{11,10},{13,12},{... | collective-permute-start | bytes 2408456 | tf_op jit(solution)/shard_map/ppermute | solution.py:418
  10.2 32.9 %collective-permute-start.9 = (f32[49,32,128]{2,1,0:T(8,128)}, f32[49,32,128]{2,1,0:T(8,128)}, u32[]{:S(2)}, u32[]{:S(2)}) collective-permute-start(f32[49,32,128]{2,1,0:T(8,128)} %get-tuple-element.25), channel_id=1, source_target_pairs={{0,1},{1,2},{2,3},{4,5},{5,6},{6,7},{8,9},{9,10},{10,11},{12,13},{... | collective-permute-start | bytes 2408456 | tf_op jit(solution)/shard_map/ppermute | solution.py:417
  14.3 31.7 %collective-permute-start.10 = (f32[49,32,128]{2,1,0:T(8,128)}, f32[49,32,128]{2,1,0:T(8,128)}, u32[]{:S(2)}, u32[]{:S(2)}) collective-permute-start(f32[49,32,128]{2,1,0:T(8,128)} %get-tuple-element.26), channel_id=1, source_target_pairs={{1,0},{2,1},{3,2},{5,4},{6,5},{7,6},{9,8},{10,9},{11,10},{13,12},{... | collective-permute-start | bytes 2408456 | tf_op jit(solution)/shard_map/ppermute | solution.py:418
  17.0 2.4 %collective-permute-start = (f32[1,128]{1,0:T(1,128)S(1)}, f32[1,128]{1,0:T(1,128)S(1)}, u32[]{:S(2)}, u32[]{:S(2)}) collective-permute-start(f32[1,128]{1,0:T(1,128)S(1)} %pad.4), channel_id=1, source_target_pairs={{0,4},{4,0},{8,12},{12,8},{16,20},{20,16},{24,28},{28,24},{1,5},{5... | collective-permute-start | bytes 1544 | tf_op jit(solution)/shard_map/ppermute | solution.py:433
  19.4 2.8 %collective-permute-start.1 = (f32[2,128]{1,0:T(2,128)S(1)}, f32[2,128]{1,0:T(2,128)S(1)}, u32[]{:S(2)}, u32[]{:S(2)}) collective-permute-start(f32[2,128]{1,0:T(2,128)S(1)} %pad_maximum_fusion.2), channel_id=1, source_target_pairs={{0,8},{4,12},{8,0},{12,4},{16,24},{20,28},{24,16},{28,20},{1,9},{5... | collective-permute-start | bytes 3080 | tf_op jit(solution)/shard_map/ppermute | solution.py:433
  22.3 2.9 %collective-permute-start.2 = (f32[4,128]{1,0:T(4,128)S(1)}, f32[4,128]{1,0:T(4,128)S(1)}, u32[]{:S(2)}, u32[]{:S(2)}) collective-permute-start(f32[4,128]{1,0:T(4,128)S(1)} %pad_maximum_fusion.1), channel_id=1, source_target_pairs={{0,16},{4,20},{8,24},{12,28},{16,0},{20,4},{24,8},{28,12},{1,17},{... | collective-permute-start | bytes 6152 | tf_op jit(solution)/shard_map/ppermute | solution.py:433
  53.1 8.9 %collective-permute-start.11 = (f32[544,128]{1,0:T(8,128)S(1)}, f32[544,128]{1,0:T(8,128)S(1)}, u32[]{:S(2)}, u32[]{:S(2)}) collective-permute-start(f32[544,128]{1,0:T(8,128)S(1)} %get-tuple-element.30), channel_id=1, source_target_pairs={{0,4},{4,0},{8,12},{12,8},{16,20},{20,16},{24,28},{28,24},{1,5},{5... | collective-permute-start | bytes 835592 | tf_op jit(solution)/shard_map/ppermute | solution.py:388
  61.9 1.6 %collective-permute-start.5 = (f32[544,128]{1,0:T(8,128)S(1)}, f32[544,128]{1,0:T(8,128)S(1)}, u32[]{:S(2)}, u32[]{:S(2)}) collective-permute-start(f32[544,128]{1,0:T(8,128)S(1)} %get-tuple-element.24), channel_id=1, source_target_pairs={{0,4},{4,0},{8,12},{12,8},{16,20},{20,16},{24,28},{28,24},{1,5},{5... | collective-permute-start | bytes 835592 | tf_op jit(solution)/shard_map/ppermute | solution.py:388
  62.0 5.8 %collective-permute-start.12 = (f32[544,128]{1,0:T(8,128)S(1)}, f32[544,128]{1,0:T(8,128)S(1)}, u32[]{:S(2)}, u32[]{:S(2)}) collective-permute-start(f32[544,128]{1,0:T(8,128)S(1)} %add.23), channel_id=1, source_target_pairs={{0,8},{4,20},{8,0},{12,28},{16,24},{20,4},{24,16},{28,12},{1,9},{5... | collective-permute-start | bytes 835592 | tf_op jit(solution)/shard_map/ppermute | solution.py:392
  63.5 7.2 %collective-permute-start.6 = (f32[544,128]{1,0:T(8,128)S(1)}, f32[544,128]{1,0:T(8,128)S(1)}, u32[]{:S(2)}, u32[]{:S(2)}) collective-permute-start(f32[544,128]{1,0:T(8,128)S(1)} %add.20), channel_id=1, source_target_pairs={{0,8},{4,20},{8,0},{12,28},{16,24},{20,4},{24,16},{28,12},{1,9},{5... | collective-permute-start | bytes 835592 | tf_op jit(solution)/shard_map/ppermute | solution.py:392
  67.8 6.9 %collective-permute-start.13 = (f32[544,128]{1,0:T(8,128)S(1)}, f32[544,128]{1,0:T(8,128)S(1)}, u32[]{:S(2)}, u32[]{:S(2)}) collective-permute-start(f32[544,128]{1,0:T(8,128)S(1)} %add.24), channel_id=1, source_target_pairs={{0,16},{4,12},{8,24},{12,4},{16,0},{20,28},{24,8},{28,20},{1,17},{... | collective-permute-start | bytes 835592 | tf_op jit(solution)/shard_map/ppermute | solution.py:392
  70.8 6.9 %collective-permute-start.7 = (f32[544,128]{1,0:T(8,128)S(1)}, f32[544,128]{1,0:T(8,128)S(1)}, u32[]{:S(2)}, u32[]{:S(2)}) collective-permute-start(f32[544,128]{1,0:T(8,128)S(1)} %add.21), channel_id=1, source_target_pairs={{0,16},{4,12},{8,24},{12,4},{16,0},{20,28},{24,8},{28,20},{1,17},{... | collective-permute-start | bytes 835592 | tf_op jit(solution)/shard_map/ppermute | solution.py:392
  74.7 5.2 %collective-permute-start.14 = (f32[544,128]{1,0:T(8,128)S(1)}, f32[544,128]{1,0:T(8,128)S(1)}, u32[]{:S(2)}, u32[]{:S(2)}) collective-permute-start(f32[544,128]{1,0:T(8,128)S(1)} %add.25.own), channel_id=1, source_target_pairs={{0,4},{4,0},{8,12},{12,8},{16,20},{20,16},{24,28},{28,24},{1,5},{5... | collective-permute-start | bytes 835592 | tf_op jit(solution)/shard_map/ppermute | solution.py:393
  77.7 7.7 %collective-permute-start.8 = (f32[544,128]{1,0:T(8,128)S(1)}, f32[544,128]{1,0:T(8,128)S(1)}, u32[]{:S(2)}, u32[]{:S(2)}) collective-permute-start(f32[544,128]{1,0:T(8,128)S(1)} %add.22.own), channel_id=1, source_target_pairs={{0,4},{4,0},{8,12},{12,8},{16,20},{20,16},{24,28},{28,24},{1,5},{5... | collective-permute-start | bytes 835592 | tf_op jit(solution)/shard_map/ppermute | solution.py:393

commit v3 on v2

v3 whole, which is shorter than its diff:
```python
import copy
import functools

import jax
import jax.numpy as jnp
from jax import lax
from jax.experimental import pallas as pl
from jax.experimental.pallas import tpu as pltpu
from jax.sharding import PartitionSpec as P

NSI = 5
HALO = 3
LANES = 128
SUB = 8

time_step = 0.15
viscosity = 0.1
third_part = 1.0 / 3.0
two_thirds = 2.0 / 3.0

HIGHEST = lax.Precision.HIGHEST
VMEM = pl.BlockSpec(memory_space=pltpu.VMEM)
SMEM = pl.BlockSpec(memory_space=pltpu.SMEM)
HBM = pl.BlockSpec(memory_space=pltpu.HBM)
KERNEL_VMEM = 12 << 20


def call(kernel, out_shape, in_specs, scratch=(), cost=(1 << 20, 1 << 20), name=None, out_specs=None, alias={}):
    flops, nbytes = cost
    return pl.pallas_call(
        kernel,
        out_shape=out_shape,
        in_specs=in_specs,
        out_specs=out_specs or [VMEM] * len(out_shape),
        scratch_shapes=list(scratch),
        input_output_aliases=alias,
        compiler_params=pltpu.CompilerParams(vmem_limit_bytes=KERNEL_VMEM),
        cost_estimate=pl.CostEstimate(flops=flops, bytes_accessed=nbytes, transcendentals=0),
        name=name,
    )


def chunk_tiles(tiles, most, step):
    most = max(step, most // step * step)
    count = -(-tiles // most)
    units = tiles // step
    return [(units // count + (1 if i < units % count else 0)) * step for i in range(count)]


class Plan:
    def __init__(self, ensemble, slots, groups):
        self.members, self.fields, self.rows, self.columns = ensemble.shape
        self.total = self.members * groups
        self.slots = slots
        self.groups = groups
        self.width = self.columns // groups
        self.tiles = self.columns // LANES
        self.q = max(1, LANES // self.width)
        most = LANES // (slots * self.q)
        self.counts = chunk_tiles(self.tiles, min(most, -(-self.tiles // 2)), max(1, self.width // LANES))
        self.starts = [sum(self.counts[:i]) for i in range(len(self.counts))]
        self.halves = 2
        self.hrows = self.rows // self.halves
        self.hrf = self.hrows * self.fields
        self.edge_groups = HALO * self.fields
        self.per_edge = LANES // (2 * HALO)
        self.edge_tiles = -(-self.edge_groups // self.per_edge)
        self.plain = -(-self.hrf // SUB) * SUB
        self.block = self.hrf * slots + self.plain

    def chunk(self, c):
        p = copy.copy(self)
        p.nt = self.counts[c]
        p.first = self.starts[c]
        p.after = (p.first + p.nt) % self.tiles
        p.before = (p.first - 1) % self.tiles
        p.np = p.nt * LANES // self.width
        p.first_patch = p.first * LANES // self.width
        p.message = p.nt * self.edge_groups + self.edge_tiles
        p.total_rows = p.nt * self.block
        return p

    def patches_of(self, tile):
        if self.width >= LANES:
            return [(tile * LANES // self.width, 0, LANES)]
        return [(tile * self.q + i, i * self.width, (i + 1) * self.width) for i in range(self.q)]


def lane_ids(shape):
    return lax.broadcasted_iota(jnp.int32, shape, len(shape) - 1)


def pack_kernel(plan, raw, state, *rest):
    p = plan
    chunks = [p.chunk(c) for c in range(len(p.counts))]
    count = 2 * len(chunks)
    outs, messages = rest[:count], rest[count : 2 * count]
    arrived, sems, out_sems = rest[2 * count :]
    lane = lane_ids((SUB, LANES))
    parts = p.members // SUB

    def part_copy(kk):
        part = pl.ds(kk * SUB, SUB)
        return pltpu.make_async_copy(raw.at[part], arrived.at[part], sems.at[kk])

    def message_copy(kk, i):
        part = pl.ds(kk * SUB, SUB)
        return pltpu.make_async_copy(messages[i].at[:, part, :], outs[i].at[:, part, :], out_sems.at[kk, i])

    for kk in range(min(2, parts)):
        part_copy(kk).start()

    def body(kk, carry):
        mem = pl.ds(pl.multiple_of(kk * SUB, SUB), SUB)
        part_copy(kk).wait()

        @pl.when(kk + 2 < parts)
        def _():
            part_copy(kk + 2).start()

        for c, h in enumerate(chunks):
            up, down = messages[2 * c], messages[2 * c + 1]
            for i in range(h.nt):
                cols = slice((h.first + i) * LANES, (h.first + i + 1) * LANES)
                for f in range(p.fields):
                    for r in range(p.rows):
                        x = arrived[mem, f, r, cols]
                        state[r, f, mem, cols] = x
                        if r >= p.rows - HALO:
                            up[(i * HALO + r - (p.rows - HALO)) * p.fields + f, mem, :] = x
                        if r < HALO:
                            down[(i * HALO + r) * p.fields + f, mem, :] = x
        for c, h in enumerate(chunks):
            for d in range(2):
                out = messages[2 * c + d]
                for e in range(p.edge_tiles):
                    packed = jnp.zeros((SUB, LANES), jnp.float32)
                    for g in range(e * p.per_edge, min((e + 1) * p.per_edge, p.edge_groups)):
                        i, f = divmod(g, p.fields)
                        edge = edge_tile(h, state, i + (p.rows - HALO if d == 0 else 0), f, mem, lane)
                        place = (g - e * p.per_edge) * 2 * HALO
                        inside = (lane >= place) & (lane < place + 2 * HALO)
                        packed = jnp.where(inside, pltpu.roll(edge, place + HALO, 1), packed)
                    out[h.nt * p.edge_groups + e, mem, :] = packed
                message_copy(kk, 2 * c + d).start()
        return carry

    lax.fori_loop(0, parts, body, 0)
    for kk in range(parts):
        for i in range(count):
            message_copy(kk, i).wait()


def edge_tile(p, state, r, f, mem, lane):
    after = state[r, f, mem, p.after * LANES : (p.after + 1) * LANES]
    before = state[r, f, mem, p.before * LANES : (p.before + 1) * LANES]
    return jnp.where(lane < LANES // 2, after, before)


def step_once(p, rows_in, load, store, last, scale):
    lane = lane_ids((SUB, LANES))
    ring = p.nt + 1
    out_tiles = p.nt if last else ring
    k = scale * time_step * viscosity
    centre = scale * (1.0 - 4.0 * time_step * viscosity)
    for first in range(0, p.fields, 2):
        pair = range(first, min(first + 2, p.fields))
        held = {row: {f: [load(row, f, t) for t in range(ring)] for f in pair} for row in range(2)}
        for row in range(1, rows_in - 1):
            held[row + 1] = {f: [load(row + 1, f, t) for t in range(ring)] for f in pair}
            coef = []
            for t in range(out_tiles):
                u, v = ((held[row][i][t] if i in held[row] else load(row, i, t)) * (scale * time_step * 0.5) for i in range(2))
                coef.append((k - u, k + u, k - v, k + v))
            for f in pair:
                x = held[row][f]
                right = [pltpu.roll(a, 1, 1) for a in x]
                left = [pltpu.roll(a, LANES - 1, 1) for a in x]
                for t in range(out_tiles):
                    west = jnp.where(lane == 0, right[(t - 1) % ring], right[t])
                    east = jnp.where(lane == LANES - 1, left[(t + 1) % ring], left[t])
                    ce, cw, cn, cs = coef[t]
                    moved = (ce * east + cw * west) + (cn * held[row + 1][f][t] + cs * held[row - 1][f][t])
                    store(row, f, t, centre * x[t] + moved)
            del held[row - 1]


def split(x):
    high = x.astype(jnp.bfloat16)
    return high, (x - high.astype(jnp.float32)).astype(jnp.bfloat16)


def places(p, chunks, me, cells):
    line = jnp.arange(p.groups, dtype=jnp.int32)[:, None]
    patch = line ^ me
    first = jnp.zeros_like(patch)
    for h in chunks:
        first = jnp.where(patch >= h.first_patch, h.first_patch, first)
    slot = jnp.arange(p.slots, dtype=jnp.int32)[None, :]
    column = cells % p.width + (patch - first) * p.width
    r = cells // p.width % p.rows
    f = cells // (p.width * p.rows)
    tile, lane = column // LANES, column % LANES
    index = r % p.hrows * p.fields + f
    shift = ((patch - first) * p.slots + slot - lane) % LANES
    table = [(tile * p.rows + r) * p.fields + f, shift, tile * p.block + index * p.slots, tile * p.block + p.hrf * p.slots + index, r // p.hrows]
    return jnp.stack(table).reshape(-1)


def forecast_kernel(plan, table, flags, state, low_in, high_in, ahead, seen, keep, send, s0, s1, s2, low, high, sems):
    p = plan
    full = p.rows + 2 * HALO
    has_low = flags[0].astype(jnp.float32)
    has_high = flags[1].astype(jnp.float32)
    core = flags[2]
    me = flags[3]
    lane = lane_ids((SUB, LANES))
    parts = p.members // SUB

    def part_copies(kk):
        part = pl.ds(kk * SUB, SUB)
        return [
            pltpu.make_async_copy(a.at[:, part, :], b.at[:, part, :], sems.at[kk, i])
            for i, (a, b) in enumerate(((low_in, low), (high_in, high)))
        ]

    for copy_in in part_copies(0):
        copy_in.start()

    def body(kk, carry):
        mem = pl.ds(pl.multiple_of(kk * SUB, SUB), SUB)

        @pl.when(kk + 1 < parts)
        def _():
            for copy_in in part_copies(kk + 1):
                copy_in.start()

        for copy_in in part_copies(kk):
            copy_in.wait()

        def edge_of(source, g):
            e, place = divmod(g, p.per_edge)
            return pltpu.roll(source[p.nt * p.edge_groups + e, mem, :], (LANES - HALO - place * 2 * HALO) % LANES, 1)

        for f in range(p.fields):
            for r in range(p.rows):
                s0[r + HALO, f] = edge_tile(p, state, r, f, mem, lane)
            for i in range(HALO):
                s0[i, f] = edge_of(low, i * p.fields + f)
                s0[HALO + p.rows + i, f] = edge_of(high, i * p.fields + f)

        def load0(row, f, t):
            if t == p.nt:
                return s0[row, f]
            if row < HALO:
                return low[(t * HALO + row) * p.fields + f, mem, :]
            if row >= HALO + p.rows:
                return high[(t * HALO + row - HALO - p.rows) * p.fields + f, mem, :]
            return state[row - HALO, f, mem, (p.first + t) * LANES : (p.first + t + 1) * LANES]

        def keep_zero(row, value):
            if row < HALO:
                return value * has_low
            if row >= HALO + p.rows:
                return value * has_high
            return value

        def store1(row, f, t, stepped):
            s1[row, f, t] = keep_zero(row, stepped)

        def store2(row, f, t, stepped):
            row = row + 1
            s2[row, f, t] = keep_zero(row, 0.75 * load0(row, f, t) + stepped)

        def store3(row, f, t, stepped):
            row = row + 2
            ahead[(t * p.rows + row - HALO) * p.fields + f, mem, :] = third_part * load0(row, f, t) + stepped

        step_once(p, full, load0, store1, False, 1.0)
        step_once(p, full - 2, lambda row, f, t: s1[row + 1, f, t], store2, False, 0.25)
        step_once(p, full - 4, lambda row, f, t: s2[row + 2, f, t], store3, True, two_thirds)
        return carry

    lax.fori_loop(0, parts, body, 0)

    wide = lane_ids((p.members, LANES))
    found = jnp.zeros((p.members, LANES), jnp.float32)
    every = p.groups * p.slots
    for j in range(p.np):
        at = ((p.first_patch + j) ^ me) * p.slots
        for o in range(p.slots):
            to = j * p.slots + o
            found = jnp.where(wide == to, pltpu.roll(ahead[table[at + o]], table[every + at + o], 1), found)
    seen[...] = found

    high, low_part = (a.astype(jnp.float32) for a in split(found))
    turned = jnp.transpose(jnp.concatenate([high, high, low_part], axis=0))
    depth = 3 * p.members
    extra = lax.broadcasted_iota(jnp.int32, (2 * SUB, depth), 0)
    ones = jnp.where((extra == 0) & (lane_ids((2 * SUB, depth)) < 2 * p.members), 1.0, 0.0).astype(jnp.float32)
    sides = [
        jnp.concatenate([turned[j * p.slots : (j + 1) * p.slots], ones], axis=0).astype(jnp.bfloat16) for j in range(p.np)
    ]
    for side in range(p.halves):
        out = keep if side == 0 else send
        half = core if side == 0 else 1 - core
        for t in range(p.nt):
            base = t * p.block
            begin = (t * p.rows + half * p.hrows) * p.fields
            high, low_part = split(jnp.concatenate([ahead[begin + i] for i in range(p.hrf)], axis=1))
            joined = jnp.concatenate([high, low_part, high], axis=0)
            result = None
            for j, first, stop in p.patches_of(t):
                part = jnp.dot(sides[j], joined, preferred_element_type=jnp.float32)
                if result is None:
                    result = part
                else:
                    at = lane_ids(part.shape) % LANES
                    result = jnp.where((at >= first) & (at < stop), part, result)
            for i in range(p.hrf):
                piece = result[:, i * LANES : (i + 1) * LANES]
                out[pl.ds(base + i * p.slots, p.slots), :] = piece[: p.slots]
                out[pl.ds(base + p.hrf * p.slots + i, 1), :] = piece[p.slots : p.slots + 1]
            for i in range(p.hrf, p.plain):
                out[pl.ds(base + p.hrf * p.slots + i, 1), :] = jnp.zeros((1, LANES), jnp.float32)


def finish_kernel(plan, table, flags, obs, ahead, seen, own, other, *rest):
    out, staged, sems = rest[-3:]
    p = plan
    n = p.slots
    core = flags[2]
    me = flags[3]
    free = p.total - 1.0
    shape = (n, LANES)
    lane = lane_ids(shape)
    row = lax.broadcasted_iota(jnp.int32, shape, 0)
    group = lane // n * n
    eye = jnp.where(lane - group == row, 1.0, 0.0).astype(jnp.float32)
    lane_row = lane_ids((1, LANES))
    lane_sub = lane_ids((SUB, LANES))

    def pick(a, index):
        return jnp.take_along_axis(a, index, axis=1)

    def col(a):
        return pick(jnp.broadcast_to(a, shape), group + row)

    def spread_out(a):
        base = lane_ids(a.shape) // n * n
        return [pick(a, base + k) for k in range(n)]

    def product(parts, b):
        total = parts[0] * b[0:1]
        for k in range(1, n):
            total = total + parts[k] * b[k : k + 1]
        return total

    moments = jnp.zeros(shape, jnp.float32)
    sums = jnp.zeros((SUB, LANES), jnp.float32)
    given = [jnp.zeros((SUB, LANES), jnp.float32) for _ in range(4)]
    every = p.groups * n
    for j in range(p.np):
        source = (p.first_patch + j) ^ me
        line = jnp.broadcast_to(obs[pl.ds(source, 1), :], (SUB, LANES))
        mine = (lane_sub >= j * n) & (lane_sub < (j + 1) * n)
        for i in range(4):
            given[i] = jnp.where(mine, pltpu.roll(line, (j * n - i * n) % LANES, 1), given[i])
        for o in range(n):
            to = j * n + o
            shift, at, line, half = (table[i * every + source * n + o] for i in range(1, 5))
            here = half == core
            at = pl.ds(pl.multiple_of(at, SUB), n)
            value = jnp.where(here, own[at, :], other[at, :])
            moments = jnp.where(lane == to, pltpu.roll(value, shift, 1), moments)
            value = jnp.where(here, own[pl.ds(line, 1), :], other[pl.ds(line, 1), :])
            sums = jnp.where(lane_sub == to, pltpu.roll(jnp.broadcast_to(value, (SUB, LANES)), shift, 1), sums)
    value, variance, loop, count = (a[0:1] for a in given)
    mean = sums[0:1] * (1.0 / p.total)
    slot = (lane_row % n).astype(jnp.float32)
    used = lane_row < p.np * n
    weight = jnp.where(used & (slot < count), jnp.exp(-0.35 * loop) / jnp.where(used, variance, 1.0), 0.0)
    root = jnp.sqrt(weight)
    root_col = col(root)
    mean_col = col(mean)
    scaled = root_col * (moments - p.total * mean_col * mean) * root
    bound = free + 0.5 * jnp.sum(pick(scaled, group + row), axis=0, keepdims=True)
    inverse = 1.0 / bound

    small = scaled * inverse
    t0 = free * inverse
    tf = t0 * eye + small
    tg = eye
    z0 = jnp.ones((1, LANES), jnp.float32)
    zg = None
    for repeat in range(NSI):
        f0 = 1.5 - 0.5 * t0
        ff = 1.5 * eye - 0.5 * tf
        parts = spread_out(ff)
        if zg is None:
            zg = -0.5 * z0 * tg
        else:
            zg = product(parts, zg) - 0.5 * z0 * tg
        z0 = z0 * f0
        if repeat < NSI - 1:
            square = product(parts, ff)
            bend = square - (0.5 * t0) * (ff + f0 * eye)
            tf = product(spread_out(square), tf)
            tg = bend if repeat == 0 else product(spread_out(bend), tg)
            t0 = t0 * f0 * f0
    zf = z0 * eye + product(spread_out(small), zg)
    scale = jnp.sqrt(free * inverse)
    spread = (scale * inverse) * root_col * zg * root
    down = root * (value - mean)
    for repeat in range(2):
        down = jnp.sum(zf * col(down), axis=0, keepdims=True)
    weights = product(spread_out(seen[...] - mean), spread) + root * down * inverse
    spread0 = scale * z0

    wide = lane_ids((p.members, LANES))
    high, low_part = (a.astype(jnp.float32) for a in split(weights))
    factors = []
    for j in range(p.np):
        here, there, last = (pltpu.roll(a, (i * n - j * n) % LANES, 1) for i, a in enumerate((high, high, low_part)))
        mine = jnp.where(wide < n, here, jnp.where(wide < 2 * n, there, last))[:, : 3 * n].astype(jnp.bfloat16)
        centre = pick(jnp.broadcast_to(mean, shape), row + j * n)
        keep0 = pick(jnp.broadcast_to(spread0, (SUB, LANES)), jnp.full((SUB, LANES), j * n, jnp.int32))[0:1]
        factors.append((mine, centre, keep0))

    def line_copy(r, f):
        cols = pl.ds(p.first * LANES, p.nt * LANES)
        return pltpu.make_async_copy(staged.at[r, f], out.at[:, f, r, cols], sems.at[r, f])

    for r in range(p.rows):
        half, begin = divmod(r, p.hrows)
        begin *= p.fields
        at_own = half == core
        for t in range(p.nt):
            pieces = []
            for f in range(p.fields):
                at = t * p.block + (begin + f) * n
                pieces.append(jnp.where(at_own, own[at : at + n, :], other[at : at + n, :]))
            at = t * p.block + p.hrf * n + begin
            plain = jnp.where(at_own, own[at : at + p.fields, :], other[at : at + p.fields, :])
            results = []
            for j, first, stop in p.patches_of(t):
                mine, centre, keep0 = factors[j]
                centred = [pieces[f] - centre * plain[f : f + 1, :] for f in range(p.fields)]
                high, low_part = split(jnp.concatenate(centred, axis=1))
                joined = jnp.concatenate([high, low_part, high], axis=0)
                results.append((jnp.dot(mine, joined, preferred_element_type=jnp.float32), keep0, first, stop))
            for f in range(p.fields):
                x = ahead[(t * p.rows + r) * p.fields + f]
                average = plain[f : f + 1, :] * (1.0 / p.total)
                final = None
                for update, keep0, first, stop in results:
                    part = (1.0 - keep0) * average + keep0 * x + update[:, f * LANES : (f + 1) * LANES]
                    if final is None:
                        final = part
                    else:
                        at = lane_ids(part.shape)
                        final = jnp.where((at >= first) & (at < stop), part, final)
                staged[r, f, :, t * LANES : (t + 1) * LANES] = final
        for f in range(p.fields):
            line_copy(r, f).start()
    for r in range(p.rows):
        for f in range(p.fields):
            line_copy(r, f).wait()


def first_sums(plan, keep, send):
    p = plan
    total = keep + lax.ppermute(send, "mem", [(i, i ^ 1) for i in range(p.groups)])
    return sum_phase(p, 0, total)


def sum_phase(plan, phase, total, waited=None):
    p = plan
    bits = [1 << i for i in range(1, p.groups.bit_length() - 1)]
    if phase >= len(bits):
        return total
    even = bits[phase]
    odd = bits[(phase + len(bits) // 2) % len(bits)]
    there = lax.ppermute(total, "mem", [(i, i ^ (odd if i & 1 else even)) for i in range(p.groups)])
    return (total if waited is None else after(total, waited)) + there


def last_sums(plan, total, waited=None):
    p = plan
    for phase in range(1, p.groups.bit_length() - 2):
        total = sum_phase(p, phase, total, waited)
    return total, lax.ppermute(total, "mem", [(i, i ^ 1) for i in range(p.groups)])


def after(value, *others):
    return lax.optimization_barrier((value,) + others)[0]


def per_device(ensemble, obs_value, obs_var, obs_cell, obs_loop, obs_count):
    groups = lax.axis_size("mem")
    bands = lax.axis_size("lat")
    slots = obs_cell.shape[-1]
    p = Plan(ensemble, slots, groups)
    chunks = [p.chunk(c) for c in range(len(p.counts))]
    f32 = jnp.float32
    shape = pltpu.VMEM

    sent = [(h.message, p.members, LANES) for h in chunks for _ in range(2)]
    out = call(
        functools.partial(pack_kernel, p),
        [pltpu.VMEM((p.rows, p.fields, p.members, p.columns), f32)] + [pltpu.HBM(a, f32) for a in sent],
        [HBM],
        [pltpu.VMEM(a, f32) for a in sent]
        + [
            pltpu.VMEM(ensemble.shape, f32),
            pltpu.SemaphoreType.DMA((p.members // SUB,)),
            pltpu.SemaphoreType.DMA((p.members // SUB, len(sent))),
        ],
        out_specs=[VMEM] + [HBM] * len(sent),
        name="pack",
    )(pltpu.with_memory_space_constraint(ensemble, pltpu.HBM))
    state, messages = out[0], out[1:]
    up = [(i, i + 1) for i in range(bands - 1)]
    down = [(i + 1, i) for i in range(bands - 1)]
    low, high = [], []
    for c in range(len(chunks)):
        low.append(lax.ppermute(messages[2 * c], "lat", up))
        high.append(lax.ppermute(messages[2 * c + 1], "lat", down))

    obs = jnp.concatenate(
        [
            after(obs_value, messages[0])[0],
            obs_var[0],
            obs_loop[0].astype(f32),
            jnp.broadcast_to(obs_count[0][:, None].astype(f32), (1, slots)),
            obs_cell[0].astype(f32),
        ],
        axis=1,
    )
    obs = jnp.pad(obs, ((0, 0), (0, -obs.shape[1] % LANES)))
    bit = 1
    while bit < groups:
        step = 2 if bit == 1 or bit * 4 > groups else 4
        there = [lax.ppermute(obs, "mem", [(i, i ^ (bit * b)) for i in range(groups)]) for b in range(1, step)]
        obs = jnp.concatenate([obs] + there, axis=0)
        bit *= step

    band = lax.axis_index("lat")
    me = lax.axis_index("mem")
    table = places(p, chunks, me, obs[:, 4 * slots : 5 * slots].astype(jnp.int32))
    flags = jnp.stack([band > 0, band < bands - 1, lax.rem(me, 2), me]).astype(jnp.int32)

    def near(x):
        return pltpu.with_memory_space_constraint(x, pltpu.VMEM)

    def far(x):
        return pltpu.with_memory_space_constraint(x, pltpu.HBM)

    new = None
    early = None
    for c, h in enumerate(chunks):
        final = c == len(chunks) - 1
        stage = (p.rows + 2 * HALO, p.fields, h.nt + 1, SUB, LANES)
        ahead, seen, keep, send = call(
            functools.partial(forecast_kernel, h),
            [
                shape((h.nt * p.rows * p.fields, p.members, LANES), f32),
                shape((p.members, LANES), f32),
                shape((h.total_rows, LANES), f32),
                shape((h.total_rows, LANES), f32),
            ],
            [SMEM, SMEM, VMEM, HBM, HBM],
            [pltpu.VMEM(stage[:2] + stage[3:], f32), pltpu.VMEM(stage, f32), pltpu.VMEM(stage, f32)]
            + [pltpu.VMEM((h.message, p.members, LANES), f32)] * 2
            + [pltpu.SemaphoreType.DMA((p.members // SUB, 2))],
            cost=(1024, h.nt * (6 << 20)),
            name="forecast",
        )(table, flags if early is None else after(flags, early), near(state), far(low[c]), far(high[c]))
        if c:
            own, other = last_sums(p, early)
            send = after(send, own)
            new = finish(p, chunks[c - 1], table, flags, obs, before + (own, other), new, ensemble.shape)
        before = (ahead, seen)
        if not final:
            early = lax.cond(obs_count[0, 0] >= 0, functools.partial(first_sums, p), lambda keep, send: keep, keep, send)
    own, other = last_sums(p, first_sums(p, keep, send), new)
    return finish(p, chunks[-1], table, flags, obs, before + (own, other), new, ensemble.shape)


def finish(plan, h, table, flags, obs, parts, new, whole):
    p = plan
    before = [] if new is None else [new]
    return call(
        functools.partial(finish_kernel, h),
        pltpu.HBM(whole, jnp.float32),
        [SMEM, SMEM, VMEM, VMEM, VMEM, VMEM, VMEM] + [HBM] * len(before),
        [pltpu.VMEM((p.rows, p.fields, p.members, h.nt * LANES), jnp.float32), pltpu.SemaphoreType.DMA((p.rows, p.fields))],
        cost=(1024, h.nt * (4 << 20)),
        name="finish",
        out_specs=HBM,
        alias={7: 0} if before else {},
    )(table, flags, obs, *(pltpu.with_memory_space_constraint(a, pltpu.VMEM) for a in parts), *before)


def solution(mesh):
    placed = (
        P("mem", None, "lat", None),
        P(None, ("mem", "lat"), None),
        P(None, ("mem", "lat"), None),
        P(None, ("mem", "lat"), None),
        P(None, ("mem", "lat"), None),
        P(None, ("mem", "lat")),
    )
    return jax.shard_map(
        per_device,
        mesh=mesh,
        in_specs=placed,
        out_specs=P("mem", None, "lat", None),
        check_vma=False,
    )
```

time: 92.1 us -> 79.1 us (0.86)
  waiting for transfers between devices: 36.7 us -> 24.6 us
  Pallas kernels: 28.3 us -> 25.9 us
    ppermute x2, waiting for transfers between devices: 17.7 us -> 0.01 us  [per_device(): low.append(lax.ppermute(messages[2 * c], 'lat', up))]
    ppermute x2, waiting for transfers between devices: 2.9 us -> 9.76 us  [per_device(): high.append(lax.ppermute(messages[2 * c + 1], 'lat', down))]
    pallas_call x5, Pallas kernels: 28.3 us -> 25.9 us  [the longest x2 13.1 us: per_device(): call(functools.partial(forecast_kernel, h), [shape((h.nt * p.rows * p.fie...]
    ppermute x11 -> x12, waiting for transfers between devices: 16 us -> 14.8 us  [the longest x4 10.5 us: sum_phase(): lax.ppermute(total, 'mem', [(i, i ^ (odd if i & 1 else even)) for i in ra...]
    ppermute x11 -> x12, starting transfers between devices: 11.7 us -> 12.3 us  [the longest x4 3.72 us: per_device(): lax.ppermute(obs, 'mem', [(i, i ^ bit * b) for i in range(groups)])]
  transfers between devices with their start and end apart: 15 -> 16, of which waited for: 10 -> 9; matrix products, arithmetic and copies ran while one was open for 1% -> 1% of each run, Pallas kernels for 21% -> 22%
where the time goes in v3:
time: 79.1 us; the launch traced here: 77.5 us
  Pallas kernels  25.9 us (33%)
  waiting for transfers between devices  24.6 us (31%)
  starting transfers between devices  23.5 us (30%)
  local copies, waits for them, and re-layouts  1.82 us (2%)
  between operations  0.87 us (1%)
    pallas_call x2, Pallas kernels, per_device(): call(functools.partial(forecast_kernel, h), [shape((h.nt * p.rows * p.fie...  13.1 us
    ppermute x4, waiting for transfers between devices, sum_phase(): lax.ppermute(total, 'mem', [(i, i ^ (odd if i & 1 else even)) for i in ra...  10.5 us
    ppermute x2, waiting for transfers between devices, per_device(): high.append(lax.ppermute(messages[2 * c + 1], 'lat', down))  9.76 us
    pallas_call x2, Pallas kernels, finish(): call(functools.partial(finish_kernel, h), pltpu.HBM(whole, jnp.float32),...  8.59 us
    ppermute x2, starting transfers between devices, per_device(): low.append(lax.ppermute(messages[2 * c], 'lat', up))  7.24 us
    pallas_call x1, Pallas kernels, per_device(): call(functools.partial(pack_kernel, p), [pltpu.VMEM((p.rows, p.fields, p....  4.21 us
    ppermute x2, starting transfers between devices, per_device(): high.append(lax.ppermute(messages[2 * c + 1], 'lat', down))  3.99 us
    ppermute x4, starting transfers between devices, per_device(): lax.ppermute(obs, 'mem', [(i, i ^ bit * b) for i in range(groups)])  3.72 us
  transfers between devices with their start and end apart: 16, of which 9 were waited for; matrix products, arithmetic and copies ran while one was open for 1% of the time, Pallas kernels for 22%

profile of v3, /device:TPU:19, one launch (start us, length us, event | category | flops | bytes accessed | tf_op | source)
XLA Modules:
  0.0 77.5 jit_solution(4024156638772999617)
XLA Ops:
  0.0 4.2 %pack.1 = (f32[4,4,32,1024]{3,2,1,0:T(8,128)S(1)}, f32[49,32,128]{2,1,0:T(8,128)}, f32[49,32,128]{2,1,0:T(8,128)}, f32[49,32,128]{2,1,0:T(8,128)}, f32[49,32,128]{2,1,0:T(8,128)}) custom-call(f32[32,4,4,1024]{3,2,1,0:T(4,128)} %raw.1), custom_call_target="tpu_custom_call" | custom-call | flops 1048576 | bytes 1048576 | tf_op jit(solution)/shard_map/pack/pallas_call | solution.py:509
  4.2 3.2 %collective-permute-start.6 = (f32[49,32,128]{2,1,0:T(8,128)}, f32[49,32,128]{2,1,0:T(8,128)S(1)}, u32[]{:S(2)}, u32[]{:S(2)}) collective-permute-start(f32[49,32,128]{2,1,0:T(8,128)} %get-tuple-element.32), channel_id=1, source_target_pairs={{0,1},{1,2},{2,3},{4,5},{5,6},{6,7},{8,9},{9,10},{10,11},{12,13},{... | collective-permute-start | bytes 2408456 | tf_op jit(solution)/shard_map/ppermute | solution.py:527
  8.2 0.1 concatenate.10
  8.3 1.0 %collective-permute-start.2 = (f32[1,128]{1,0:T(1,128)S(1)}, f32[1,128]{1,0:T(1,128)S(1)}, u32[]{:S(2)}, u32[]{:S(2)}) collective-permute-start(f32[1,128]{1,0:T(1,128)S(1)} %pad.4), channel_id=1, source_target_pairs={{0,4},{4,0},{8,12},{12,8},{16,20},{20,16},{24,28},{28,24},{1,5},{5... | collective-permute-start | bytes 1544 | tf_op jit(solution)/shard_map/ppermute | solution.py:544
  9.3 2.1 %collective-permute-start.7 = (f32[49,32,128]{2,1,0:T(8,128)}, f32[49,32,128]{2,1,0:T(8,128)}, u32[]{:S(2)}, u32[]{:S(2)}) collective-permute-start(f32[49,32,128]{2,1,0:T(8,128)} %get-tuple-element.35), channel_id=1, source_target_pairs={{1,0},{2,1},{3,2},{5,4},{6,5},{7,6},{9,8},{10,9},{11,10},{13,12},{... | collective-permute-start | bytes 2408456 | tf_op jit(solution)/shard_map/ppermute | solution.py:528
  11.4 0.0 collective-permute-done.2
  11.4 1.3 %collective-permute-start.5 = (f32[2,128]{1,0:T(2,128)S(1)}, f32[2,128]{1,0:T(2,128)S(1)}, u32[]{:S(2)}, u32[]{:S(2)}) collective-permute-start(f32[2,128]{1,0:T(2,128)S(1)} %pad_maximum_fusion), channel_id=1, source_target_pairs={{0,24},{4,28},{8,16},{12,20},{16,8},{20,12},{24,0},{28,4},{1,25},{... | collective-permute-start | bytes 3080 | tf_op jit(solution)/shard_map/ppermute | solution.py:544
  12.7 0.2 collective-permute-start.4
  12.9 1.2 %collective-permute-start.3 = (f32[2,128]{1,0:T(2,128)S(1)}, f32[2,128]{1,0:T(2,128)S(1)}, u32[]{:S(2)}, u32[]{:S(2)}) collective-permute-start(f32[2,128]{1,0:T(2,128)S(1)} %pad_maximum_fusion), channel_id=1, source_target_pairs={{0,8},{4,12},{8,0},{12,4},{16,24},{20,28},{24,16},{28,20},{1,9},{5... | collective-permute-start | bytes 3080 | tf_op jit(solution)/shard_map/ppermute | solution.py:544
  14.1 0.1 pad_add_fusion.flags
  14.2 0.6 collective-permute-done.5
  14.8 4.0 %collective-permute-start.8 = (f32[49,32,128]{2,1,0:T(8,128)}, f32[49,32,128]{2,1,0:T(8,128)}, u32[]{:S(2)}, u32[]{:S(2)}) collective-permute-start(f32[49,32,128]{2,1,0:T(8,128)} %get-tuple-element.39), channel_id=1, source_target_pairs={{0,1},{1,2},{2,3},{4,5},{5,6},{6,7},{8,9},{9,10},{10,11},{12,13},{... | collective-permute-start | bytes 2408456 | tf_op jit(solution)/shard_map/ppermute | solution.py:527
  18.8 0.0 collective-permute-done.4
  18.8 1.9 %collective-permute-start.9 = (f32[49,32,128]{2,1,0:T(8,128)}, f32[49,32,128]{2,1,0:T(8,128)}, u32[]{:S(2)}, u32[]{:S(2)}) collective-permute-start(f32[49,32,128]{2,1,0:T(8,128)} %get-tuple-element.40), channel_id=1, source_target_pairs={{1,0},{2,1},{3,2},{5,4},{6,5},{7,6},{9,8},{10,9},{11,10},{13,12},{... | collective-permute-start | bytes 2408456 | tf_op jit(solution)/shard_map/ppermute | solution.py:528
  20.8 0.0 collective-permute-done.3
  20.8 0.1 constant_dynamic-update-slice_fusion.4
  20.9 0.1 constant_dynamic-update-slice_fusion.3
  21.0 0.1 constant_dynamic-update-slice_fusion.2
  21.1 0.1 constant_dynamic-update-slice_fusion.1
  21.2 0.1 constant_dynamic-update-slice_fusion
  21.3 0.1 reshape.51.table
  21.4 9.6 %collective-permute-done.7.high_in = f32[49,32,128]{2,1,0:T(8,128)} collective-permute-done((f32[49,32,128]{2,1,0:T(8,128)}, f32[49,32,128]{2,1,0:T(8,128)}, u32[]{:S(2)}, u32[]{:S(2)}) %collective-permute-start.7) | collective-permute-done | bytes 802848 | tf_op jit(solution)/shard_map/ppermute | solution.py:528
  31.0 0.9 %copy-done.1 = f32[49,32,128]{2,1,0:T(8,128)} copy-done((f32[49,32,128]{2,1,0:T(8,128)}, f32[49,32,128]{2,1,0:T(8,128)S(1)}, u32[]{:S(2)}) %copy-start.1) | copy-done | bytes 802840
  31.9 6.6 %forecast.2 = (f32[64,32,128]{2,1,0:T(8,128)S(1)}, f32[32,128]{1,0:T(8,128)S(1)}, f32[544,128]{1,0:T(8,128)S(1)}, f32[544,128]{1,0:T(8,128)S(1)}) custom-call(s32[640]{0:T(1024)S(1)} %reshape.51.table, s32[4]{0:T(128)S(1)} %pad_add_fusion.flags, f32[4,4,32,1024]{3,2,1,0:T(8,128)S(1)} %get-tuple-element.34.state, f32[49,32,128]{2,1,0:T(8,128)} %copy-done.1, ...), custom_call_target="tpu_custom_call" | custom-call | flops 1024 | bytes 25165824 | tf_op jit(solution)/shard_map/forecast/pallas_call | solution.py:564
  38.4 0.0 copy-start
  38.5 0.7 copy-done
  39.2 8.5 %conditional.1 = (f32[544,128]{1,0:T(8,128)S(1)}) conditional(s32[]{:T(128)} %bitcast.14, f32[544,128]{1,0:T(8,128)S(1)} %get-tuple-element.36, (f32[544,128]{1,0:T(8,128)}, f32[544,128]{1,0:T(8,128)S(1)}) %tuple.26), branch_computations={%region_0.1_spmd, %region_1.2_spmd} | conditional | flops 139264 | bytes 3899480 | solution.py:585
  39.2 1.2 %collective-permute-start = (f32[544,128]{1,0:T(8,128)}, f32[544,128]{1,0:T(8,128)S(1)}, u32[]{:S(2)}, u32[]{:S(2)}) collective-permute-start(f32[544,128]{1,0:T(8,128)} %get-tuple-element.14), channel_id=1, source_target_pairs={{0,4},{4,0},{8,12},{12,8},{16,20},{20,16},{24,28},{28,24},{1,5},{5... | collective-permute-start | bytes 835592 | tf_op jit(solution)/shard_map/cond/branch_1_fun/ppermute | solution.py:473
  40.4 1.4 %collective-permute-done = f32[544,128]{1,0:T(8,128)S(1)} collective-permute-done((f32[544,128]{1,0:T(8,128)}, f32[544,128]{1,0:T(8,128)S(1)}, u32[]{:S(2)}, u32[]{:S(2)}) %collective-permute-start) | collective-permute-done | bytes 278560 | tf_op jit(solution)/shard_map/cond/branch_1_fun/ppermute | solution.py:473
  41.8 1.3 %collective-permute-start.1 = (f32[544,128]{1,0:T(8,128)S(1)}, f32[544,128]{1,0:T(8,128)S(1)}, u32[]{:S(2)}, u32[]{:S(2)}) collective-permute-start(f32[544,128]{1,0:T(8,128)S(1)} %add.62), channel_id=1, source_target_pairs={{0,8},{4,20},{8,0},{12,28},{16,24},{20,4},{24,16},{28,12},{1,9},{5... | collective-permute-start | bytes 835592 | tf_op jit(solution)/shard_map/cond/branch_1_fun/ppermute | solution.py:484
  43.1 4.6 %collective-permute-done.1 = f32[544,128]{1,0:T(8,128)S(1)} collective-permute-done((f32[544,128]{1,0:T(8,128)S(1)}, f32[544,128]{1,0:T(8,128)S(1)}, u32[]{:S(2)}, u32[]{:S(2)}) %collective-permute-start.1) | collective-permute-done | bytes 278560 | tf_op jit(solution)/shard_map/cond/branch_1_fun/ppermute | solution.py:484
  47.7 0.3 collective-permute-start.10
  48.0 0.0 collective-permute-done.8.low_in
  48.0 0.2 collective-permute-done.9.high_in
  48.2 6.6 %forecast.3 = (f32[64,32,128]{2,1,0:T(8,128)S(1)}, f32[32,128]{1,0:T(8,128)S(1)}, f32[544,128]{1,0:T(8,128)S(1)}, f32[544,128]{1,0:T(8,128)S(1)}) custom-call(s32[640]{0:T(1024)S(1)} %reshape.51.table, s32[4]{0:T(128)S(1)} %pad_add_fusion.flags, f32[4,4,32,1024]{3,2,1,0:T(8,128)S(1)} %get-tuple-element.34.state, ...), custom_call_target="tpu_custom_call" | custom-call | flops 1024 | bytes 25165824 | tf_op jit(solution)/shard_map/forecast/pallas_call | solution.py:564
  54.8 0.0 collective-permute-done.10
  54.8 2.3 %collective-permute-start.11 = (f32[544,128]{1,0:T(8,128)S(1)}, f32[544,128]{1,0:T(8,128)S(1)}, u32[]{:S(2)}, u32[]{:S(2)}) collective-permute-start(f32[544,128]{1,0:T(8,128)S(1)} %get-tuple-element.45), channel_id=1, source_target_pairs={{0,4},{4,0},{8,12},{12,8},{16,20},{20,16},{24,28},{28,24},{1,5},{5... | collective-permute-start | bytes 835592 | tf_op jit(solution)/shard_map/ppermute | solution.py:473
  57.1 1.2 %collective-permute-done.11 = f32[544,128]{1,0:T(8,128)S(1)} collective-permute-done((f32[544,128]{1,0:T(8,128)S(1)}, f32[544,128]{1,0:T(8,128)S(1)}, u32[]{:S(2)}, u32[]{:S(2)}) %collective-permute-start.11) | collective-permute-done | bytes 278560 | tf_op jit(solution)/shard_map/ppermute | solution.py:473
  58.3 0.3 collective-permute-start.12
  58.6 0.7 collective-permute-start.13
  59.3 4.8 %collective-permute-done.12 = f32[544,128]{1,0:T(8,128)S(1)} collective-permute-done((f32[544,128]{1,0:T(8,128)S(1)}, f32[544,128]{1,0:T(8,128)S(1)}, u32[]{:S(2)}, u32[]{:S(2)}) %collective-permute-start.12) | collective-permute-done | bytes 278560 | tf_op jit(solution)/shard_map/ppermute | solution.py:484
  64.1 0.3 collective-permute-start.14
  64.4 0.0 collective-permute-done.13.other
  64.4 4.3 %finish.2.rest_0_ = f32[32,4,4,1024]{3,2,1,0:T(4,128)} custom-call(s32[640]{0:T(1024)S(1)} %reshape.51.table, s32[4]{0:T(128)S(1)} %pad_add_fusion.flags, f32[8,128]{1,0:T(8,128)S(1)} %concatenate.12.obs, f32[64,32,128]{2,1,0:T(8,128)S(1)} %get-tuple-element.46.ahead, f32[32,128]{1,0:T(8,128)S(1)} %get-tuple-element.47.seen, f32[544,128]{1,0:T(8,128)S(1)} %add.102.own, ...), custom_call_target="tpu_custom_call" | custom-call | flops 1024 | bytes 16777216 | tf_op jit(solution)/shard_map/finish/pallas_call | solution.py:593
  68.7 1.1 %collective-permute-done.14 = f32[544,128]{1,0:T(8,128)S(1)} collective-permute-done((f32[544,128]{1,0:T(8,128)S(1)}, f32[544,128]{1,0:T(8,128)S(1)}, u32[]{:S(2)}, u32[]{:S(2)}) %collective-permute-start.14) | collective-permute-done | bytes 278560 | tf_op jit(solution)/shard_map/ppermute | solution.py:484
  69.9 2.1 %collective-permute-start.15 = (f32[544,128]{1,0:T(8,128)S(1)}, f32[544,128]{1,0:T(8,128)S(1)}, u32[]{:S(2)}, u32[]{:S(2)}) collective-permute-start(f32[544,128]{1,0:T(8,128)S(1)} %add.105.own), channel_id=1, source_target_pairs={{0,4},{4,0},{8,12},{12,8},{16,20},{20,16},{24,28},{28,24},{1,5},{5... | collective-permute-start | bytes 835592 | tf_op jit(solution)/shard_map/ppermute | solution.py:492
  72.1 1.2 %collective-permute-done.15.other = f32[544,128]{1,0:T(8,128)S(1)} collective-permute-done((f32[544,128]{1,0:T(8,128)S(1)}, f32[544,128]{1,0:T(8,128)S(1)}, u32[]{:S(2)}, u32[]{:S(2)}) %collective-permute-start.15) | collective-permute-done | bytes 278560 | tf_op jit(solution)/shard_map/ppermute | solution.py:492
  73.2 4.3 %finish.3 = f32[32,4,4,1024]{3,2,1,0:T(4,128)} custom-call(s32[640]{0:T(1024)S(1)} %reshape.51.table, s32[4]{0:T(128)S(1)} %pad_add_fusion.flags, f32[8,128]{1,0:T(8,128)S(1)} %concatenate.12.obs, f32[64,32,128]{2,1,0:T(8,128)S(1)} %get-tuple-element.41.ahead, f32[32,128]{1,0:T(8,128)S(1)} %get-tuple-element.42.seen, ...), custom_call_target="tpu_custom_call", output_to_operand_aliasing={{}: (7, {})} | custom-call | flops 1024 | bytes 16777216 | tf_op jit(solution)/shard_map/finish/pallas_call | solution.py:593
  (22 shorter events, 0.3 us)
Async XLA Ops:
  0.0 8.1 %copy-start.4 = (f32[1,1,16]{2,1,0:T(1,128)S(1)}, f32[1,1,16]{2,1,0:T(1,128)}, u32[]{:S(2)}) copy-start(f32[1,1,16]{2,1,0:T(1,128)} %param.9) | copy-start | bytes 196
  0.0 8.1 %copy-start.3 = (s32[1,1,16]{2,1,0:T(1,128)S(1)}, s32[1,1,16]{2,1,0:T(1,128)}, u32[]{:S(2)}) copy-start(s32[1,1,16]{2,1,0:T(1,128)} %param.12) | copy-start | bytes 196
  0.0 8.1 %copy-start.2 = (s32[1,1,16]{2,1,0:T(1,128)S(1)}, s32[1,1,16]{2,1,0:T(1,128)}, u32[]{:S(2)}) copy-start(s32[1,1,16]{2,1,0:T(1,128)} %param.11) | copy-start | bytes 196
  0.0 8.1 %copy-start.5 = (f32[1,1,16]{2,1,0:T(1,128)S(1)}, f32[1,1,16]{2,1,0:T(1,128)}, u32[]{:S(2)}) copy-start(f32[1,1,16]{2,1,0:T(1,128)} %param.10) | copy-start | bytes 196
  4.2 26.7 %collective-permute-start.6 = (f32[49,32,128]{2,1,0:T(8,128)}, f32[49,32,128]{2,1,0:T(8,128)S(1)}, u32[]{:S(2)}, u32[]{:S(2)}) collective-permute-start(f32[49,32,128]{2,1,0:T(8,128)} %get-tuple-element.32), channel_id=1, source_target_pairs={{0,1},{1,2},{2,3},{4,5},{5,6},{6,7},{8,9},{9,10},{10,11},{12,13},{... | collective-permute-start | bytes 2408456 | tf_op jit(solution)/shard_map/ppermute | solution.py:527
  8.3 3.1 %collective-permute-start.2 = (f32[1,128]{1,0:T(1,128)S(1)}, f32[1,128]{1,0:T(1,128)S(1)}, u32[]{:S(2)}, u32[]{:S(2)}) collective-permute-start(f32[1,128]{1,0:T(1,128)S(1)} %pad.4), channel_id=1, source_target_pairs={{0,4},{4,0},{8,12},{12,8},{16,20},{20,16},{24,28},{28,24},{1,5},{5... | collective-permute-start | bytes 1544 | tf_op jit(solution)/shard_map/ppermute | solution.py:544
  9.3 21.7 %collective-permute-start.7 = (f32[49,32,128]{2,1,0:T(8,128)}, f32[49,32,128]{2,1,0:T(8,128)}, u32[]{:S(2)}, u32[]{:S(2)}) collective-permute-start(f32[49,32,128]{2,1,0:T(8,128)} %get-tuple-element.35), channel_id=1, source_target_pairs={{1,0},{2,1},{3,2},{5,4},{6,5},{7,6},{9,8},{10,9},{11,10},{13,12},{... | collective-permute-start | bytes 2408456 | tf_op jit(solution)/shard_map/ppermute | solution.py:528
  11.4 3.4 %collective-permute-start.5 = (f32[2,128]{1,0:T(2,128)S(1)}, f32[2,128]{1,0:T(2,128)S(1)}, u32[]{:S(2)}, u32[]{:S(2)}) collective-permute-start(f32[2,128]{1,0:T(2,128)S(1)} %pad_maximum_fusion), channel_id=1, source_target_pairs={{0,24},{4,28},{8,16},{12,20},{16,8},{20,12},{24,0},{28,4},{1,25},{... | collective-permute-start | bytes 3080 | tf_op jit(solution)/shard_map/ppermute | solution.py:544
  12.7 6.2 %collective-permute-start.4 = (f32[2,128]{1,0:T(2,128)S(1)}, f32[2,128]{1,0:T(2,128)S(1)}, u32[]{:S(2)}, u32[]{:S(2)}) collective-permute-start(f32[2,128]{1,0:T(2,128)S(1)} %pad_maximum_fusion), channel_id=1, source_target_pairs={{0,16},{4,20},{8,24},{12,28},{16,0},{20,4},{24,8},{28,12},{1,17},{... | collective-permute-start | bytes 3080 | tf_op jit(solution)/shard_map/ppermute | solution.py:544
  12.9 7.9 %collective-permute-start.3 = (f32[2,128]{1,0:T(2,128)S(1)}, f32[2,128]{1,0:T(2,128)S(1)}, u32[]{:S(2)}, u32[]{:S(2)}) collective-permute-start(f32[2,128]{1,0:T(2,128)S(1)} %pad_maximum_fusion), channel_id=1, source_target_pairs={{0,8},{4,12},{8,0},{12,4},{16,24},{20,28},{24,16},{28,20},{1,9},{5... | collective-permute-start | bytes 3080 | tf_op jit(solution)/shard_map/ppermute | solution.py:544
  14.8 33.2 %collective-permute-start.8 = (f32[49,32,128]{2,1,0:T(8,128)}, f32[49,32,128]{2,1,0:T(8,128)}, u32[]{:S(2)}, u32[]{:S(2)}) collective-permute-start(f32[49,32,128]{2,1,0:T(8,128)} %get-tuple-element.39), channel_id=1, source_target_pairs={{0,1},{1,2},{2,3},{4,5},{5,6},{6,7},{8,9},{9,10},{10,11},{12,13},{... | collective-permute-start | bytes 2408456 | tf_op jit(solution)/shard_map/ppermute | solution.py:527
  18.8 29.3 %collective-permute-start.9 = (f32[49,32,128]{2,1,0:T(8,128)}, f32[49,32,128]{2,1,0:T(8,128)}, u32[]{:S(2)}, u32[]{:S(2)}) collective-permute-start(f32[49,32,128]{2,1,0:T(8,128)} %get-tuple-element.40), channel_id=1, source_target_pairs={{1,0},{2,1},{3,2},{5,4},{6,5},{7,6},{9,8},{10,9},{11,10},{13,12},{... | collective-permute-start | bytes 2408456 | tf_op jit(solution)/shard_map/ppermute | solution.py:528
  31.0 0.9 %copy-start.1 = (f32[49,32,128]{2,1,0:T(8,128)}, f32[49,32,128]{2,1,0:T(8,128)S(1)}, u32[]{:S(2)}) copy-start(f32[49,32,128]{2,1,0:T(8,128)S(1)} %collective-permute-done.6.low_in) | copy-start | bytes 2408452
  38.4 0.7 copy-start
  39.2 2.6 %collective-permute-start = (f32[544,128]{1,0:T(8,128)}, f32[544,128]{1,0:T(8,128)S(1)}, u32[]{:S(2)}, u32[]{:S(2)}) collective-permute-start(f32[544,128]{1,0:T(8,128)} %get-tuple-element.14), channel_id=1, source_target_pairs={{0,4},{4,0},{8,12},{12,8},{16,20},{20,16},{24,28},{28,24},{1,5},{5... | collective-permute-start | bytes 835592 | tf_op jit(solution)/shard_map/cond/branch_1_fun/ppermute | solution.py:473
  41.8 5.9 %collective-permute-start.1 = (f32[544,128]{1,0:T(8,128)S(1)}, f32[544,128]{1,0:T(8,128)S(1)}, u32[]{:S(2)}, u32[]{:S(2)}) collective-permute-start(f32[544,128]{1,0:T(8,128)S(1)} %add.62), channel_id=1, source_target_pairs={{0,8},{4,20},{8,0},{12,28},{16,24},{20,4},{24,16},{28,12},{1,9},{5... | collective-permute-start | bytes 835592 | tf_op jit(solution)/shard_map/cond/branch_1_fun/ppermute | solution.py:484
  47.7 7.1 %collective-permute-start.10 = (f32[544,128]{1,0:T(8,128)S(1)}, f32[544,128]{1,0:T(8,128)S(1)}, u32[]{:S(2)}, u32[]{:S(2)}) collective-permute-start(f32[544,128]{1,0:T(8,128)S(1)} %get-tuple-element.56), channel_id=1, source_target_pairs={{0,16},{4,12},{8,24},{12,4},{16,0},{20,28},{24,8},{28,20},{1,17},{... | collective-permute-start | bytes 835592 | tf_op jit(solution)/shard_map/ppermute | solution.py:484
  54.8 3.5 %collective-permute-start.11 = (f32[544,128]{1,0:T(8,128)S(1)}, f32[544,128]{1,0:T(8,128)S(1)}, u32[]{:S(2)}, u32[]{:S(2)}) collective-permute-start(f32[544,128]{1,0:T(8,128)S(1)} %get-tuple-element.45), channel_id=1, source_target_pairs={{0,4},{4,0},{8,12},{12,8},{16,20},{20,16},{24,28},{28,24},{1,5},{5... | collective-permute-start | bytes 835592 | tf_op jit(solution)/shard_map/ppermute | solution.py:473
  58.3 5.8 %collective-permute-start.12 = (f32[544,128]{1,0:T(8,128)S(1)}, f32[544,128]{1,0:T(8,128)S(1)}, u32[]{:S(2)}, u32[]{:S(2)}) collective-permute-start(f32[544,128]{1,0:T(8,128)S(1)} %add.103), channel_id=1, source_target_pairs={{0,8},{4,20},{8,0},{12,28},{16,24},{20,4},{24,16},{28,12},{1,9},{5... | collective-permute-start | bytes 835592 | tf_op jit(solution)/shard_map/ppermute | solution.py:484
  58.6 5.8 %collective-permute-start.13 = (f32[544,128]{1,0:T(8,128)S(1)}, f32[544,128]{1,0:T(8,128)S(1)}, u32[]{:S(2)}, u32[]{:S(2)}) collective-permute-start(f32[544,128]{1,0:T(8,128)S(1)} %add.102.own), channel_id=1, source_target_pairs={{0,4},{4,0},{8,12},{12,8},{16,20},{20,16},{24,28},{28,24},{1,5},{5... | collective-permute-start | bytes 835592 | tf_op jit(solution)/shard_map/ppermute | solution.py:492
  64.1 5.8 %collective-permute-start.14 = (f32[544,128]{1,0:T(8,128)S(1)}, f32[544,128]{1,0:T(8,128)S(1)}, u32[]{:S(2)}, u32[]{:S(2)}) collective-permute-start(f32[544,128]{1,0:T(8,128)S(1)} %add.104), channel_id=1, source_target_pairs={{0,16},{4,12},{8,24},{12,4},{16,0},{20,28},{24,8},{28,20},{1,17},{... | collective-permute-start | bytes 835592 | tf_op jit(solution)/shard_map/ppermute | solution.py:484
  69.9 3.3 %collective-permute-start.15 = (f32[544,128]{1,0:T(8,128)S(1)}, f32[544,128]{1,0:T(8,128)S(1)}, u32[]{:S(2)}, u32[]{:S(2)}) collective-permute-start(f32[544,128]{1,0:T(8,128)S(1)} %add.105.own), channel_id=1, source_target_pairs={{0,4},{4,0},{8,12},{12,8},{16,20},{20,16},{24,28},{28,24},{1,5},{5... | collective-permute-start | bytes 835592 | tf_op jit(solution)/shard_map/ppermute | solution.py:492

commit v4 on v3

--- a/solution.py
+++ b/solution.py
@@ -22,6 +22,7 @@
 VMEM = pl.BlockSpec(memory_space=pltpu.VMEM)
 SMEM = pl.BlockSpec(memory_space=pltpu.SMEM)
 HBM = pl.BlockSpec(memory_space=pltpu.HBM)
+ANY = pl.BlockSpec(memory_space=pl.ANY)
 KERNEL_VMEM = 12 << 20
 
 
@@ -76,6 +77,7 @@
         p.before = (p.first - 1) % self.tiles
         p.np = p.nt * LANES // self.width
         p.first_patch = p.first * LANES // self.width
+        p.bands = lax.axis_size("lat")
         p.message = p.nt * self.edge_groups + self.edge_tiles
         p.total_rows = p.nt * self.block
         return p
@@ -90,71 +92,94 @@
     return lax.broadcasted_iota(jnp.int32, shape, len(shape) - 1)
 
 
-def pack_kernel(plan, raw, state, *rest):
+def pack_kernel(plan, raw, *rest):
     p = plan
-    chunks = [p.chunk(c) for c in range(len(p.counts))]
-    count = 2 * len(chunks)
-    outs, messages = rest[:count], rest[count : 2 * count]
-    arrived, sems, out_sems = rest[2 * count :]
     lane = lane_ids((SUB, LANES))
     parts = p.members // SUB
-
-    def part_copy(kk):
+    given = []
+    if p.first == 0:
+        given, rest = rest[:5], rest[5:]
+        row_out, (taken, lines, given_sems), rest = rest[3], (rest[-7:-2], *rest[-2:]), rest[:3] + rest[4:-7]
+    state, first_out, second_out, up, down, arrived, beside, sems, out_sems = rest
+    given_copies = []
+    for i, a in enumerate(given):
+        given_copies.append(pltpu.make_async_copy(a, taken[i], given_sems.at[i]))
+    odd = lax.rem(lax.axis_index("lat"), 2)
+
+    def part_copies(kk):
         part = pl.ds(kk * SUB, SUB)
-        return pltpu.make_async_copy(raw.at[part], arrived.at[part], sems.at[kk])
-
-    def message_copy(kk, i):
+        takes = [(arrived, p.first, p.nt)] + [(beside.at[i], t, 1) for i, t in enumerate((p.after, p.before))]
+        return [
+            pltpu.make_async_copy(raw.at[part, :, :, pl.ds(t * LANES, n * LANES)], to.at[part], sems.at[kk, i])
+            for i, (to, t, n) in enumerate(takes)
+        ]
+
+    def message_copies(kk, swapped=0):
         part = pl.ds(kk * SUB, SUB)
-        return pltpu.make_async_copy(messages[i].at[:, part, :], outs[i].at[:, part, :], out_sems.at[kk, i])
-
-    for kk in range(min(2, parts)):
-        part_copy(kk).start()
+        inner = (up, down) if swapped == 0 else (down, up)
+        return [
+            pltpu.make_async_copy(a.at[:, part, :], b.at[:, part, :], out_sems.at[kk, i])
+            for i, (a, b) in enumerate(zip(inner, (first_out, second_out)))
+        ]
+
+    for kk in range(parts):
+        for copy_in in part_copies(kk):
+            copy_in.start()
+    for copy_in in given_copies:
+        copy_in.start()
 
     def body(kk, carry):
         mem = pl.ds(pl.multiple_of(kk * SUB, SUB), SUB)
-        part_copy(kk).wait()
-
-        @pl.when(kk + 2 < parts)
-        def _():
-            part_copy(kk + 2).start()
-
-        for c, h in enumerate(chunks):
-            up, down = messages[2 * c], messages[2 * c + 1]
-            for i in range(h.nt):
-                cols = slice((h.first + i) * LANES, (h.first + i + 1) * LANES)
-                for f in range(p.fields):
-                    for r in range(p.rows):
-                        x = arrived[mem, f, r, cols]
-                        state[r, f, mem, cols] = x
-                        if r >= p.rows - HALO:
-                            up[(i * HALO + r - (p.rows - HALO)) * p.fields + f, mem, :] = x
-                        if r < HALO:
-                            down[(i * HALO + r) * p.fields + f, mem, :] = x
-        for c, h in enumerate(chunks):
-            for d in range(2):
-                out = messages[2 * c + d]
-                for e in range(p.edge_tiles):
-                    packed = jnp.zeros((SUB, LANES), jnp.float32)
-                    for g in range(e * p.per_edge, min((e + 1) * p.per_edge, p.edge_groups)):
-                        i, f = divmod(g, p.fields)
-                        edge = edge_tile(h, state, i + (p.rows - HALO if d == 0 else 0), f, mem, lane)
-                        place = (g - e * p.per_edge) * 2 * HALO
-                        inside = (lane >= place) & (lane < place + 2 * HALO)
-                        packed = jnp.where(inside, pltpu.roll(edge, place + HALO, 1), packed)
-                    out[h.nt * p.edge_groups + e, mem, :] = packed
-                message_copy(kk, 2 * c + d).start()
+        for copy_in in part_copies(kk):
+            copy_in.wait()
+
+        for i in range(p.nt):
+            cols = slice(i * LANES, (i + 1) * LANES)
+            for f in range(p.fields):
+                for r in range(p.rows):
+                    x = arrived[mem, f, r, cols]
+                    state[r, f, mem, cols] = x
+                    if r >= p.rows - HALO:
+                        up[(i * HALO + r - (p.rows - HALO)) * p.fields + f, mem, :] = x
+                    if r < HALO:
+                        down[(i * HALO + r) * p.fields + f, mem, :] = x
+        for r in range(p.rows):
+            for f in range(p.fields):
+                edge = jnp.where(lane < LANES // 2, beside[0, mem, f, r, :], beside[1, mem, f, r, :])
+                state[r, f, mem, p.nt * LANES :] = edge
+        for out, skipped in ((up, p.rows - HALO), (down, 0)):
+            for e in range(p.edge_tiles):
+                packed = jnp.zeros((SUB, LANES), jnp.float32)
+                for g in range(e * p.per_edge, min((e + 1) * p.per_edge, p.edge_groups)):
+                    i, f = divmod(g, p.fields)
+                    place = (g - e * p.per_edge) * 2 * HALO
+                    inside = (lane >= place) & (lane < place + 2 * HALO)
+                    edge = state[i + skipped, f, mem, p.nt * LANES :]
+                    packed = jnp.where(inside, pltpu.roll(edge, place + HALO, 1), packed)
+                out[p.nt * p.edge_groups + e, mem, :] = packed
+
+        for swapped in range(2):
+
+            @pl.when(odd == swapped)
+            def _():
+                for copy_out in message_copies(kk, swapped):
+                    copy_out.start()
+
         return carry
 
     lax.fori_loop(0, parts, body, 0)
+    if given:
+        for copy_in in given_copies:
+            copy_in.wait()
+        row = jnp.zeros((SUB, LANES), jnp.float32)
+        for i, a in enumerate(given):
+            lines[i : i + 1, : p.slots] = jnp.broadcast_to(taken[i][0].astype(jnp.float32), (1, p.slots))
+            line = pltpu.roll(jnp.broadcast_to(lines[i : i + 1, :], (SUB, LANES)), i * p.slots, 1)
+            row = jnp.where((lane >= i * p.slots) & (lane < (i + 1) * p.slots), line, row)
+        row_out[...] = row[:1]
     for kk in range(parts):
-        for i in range(count):
-            message_copy(kk, i).wait()
-
-
-def edge_tile(p, state, r, f, mem, lane):
-    after = state[r, f, mem, p.after * LANES : (p.after + 1) * LANES]
-    before = state[r, f, mem, p.before * LANES : (p.before + 1) * LANES]
-    return jnp.where(lane < LANES // 2, after, before)
+        for copy_out in message_copies(kk):
+            copy_out.wait()
 
 
 def step_once(p, rows_in, load, store, last, scale):
@@ -207,33 +232,47 @@
     return jnp.stack(table).reshape(-1)
 
 
-def forecast_kernel(plan, table, flags, state, low_in, high_in, ahead, seen, keep, send, s0, s1, s2, low, high, sems):
+def table_kernel(table_in, table, sem):
+    copy_in = pltpu.make_async_copy(table_in, table, sem)
+    copy_in.start()
+    copy_in.wait()
+
+
+def forecast_kernel(plan, table, state, first_in, second_in, ahead, seen, keep, send, s0, s1, s2, low, high, sems):
     p = plan
     full = p.rows + 2 * HALO
-    has_low = flags[0].astype(jnp.float32)
-    has_high = flags[1].astype(jnp.float32)
-    core = flags[2]
-    me = flags[3]
+    band = lax.axis_index("lat")
+    me = lax.axis_index("mem")
+    core = lax.rem(me, 2)
+    has_low = (band > 0).astype(jnp.float32)
+    has_high = (band < p.bands - 1).astype(jnp.float32)
     lane = lane_ids((SUB, LANES))
     parts = p.members // SUB
 
-    def part_copies(kk):
+    def part_copies(kk, swapped=0):
         part = pl.ds(kk * SUB, SUB)
+        inner = (high, low) if swapped == 0 else (low, high)
         return [
             pltpu.make_async_copy(a.at[:, part, :], b.at[:, part, :], sems.at[kk, i])
-            for i, (a, b) in enumerate(((low_in, low), (high_in, high)))
+            for i, (a, b) in enumerate(zip((first_in, second_in), inner))
         ]
 
-    for copy_in in part_copies(0):
-        copy_in.start()
+    def start_copies(kk):
+        for swapped in range(2):
+
+            @pl.when(lax.rem(band, 2) == swapped)
+            def _():
+                for copy_in in part_copies(kk, swapped):
+                    copy_in.start()
+
+    start_copies(0)
 
     def body(kk, carry):
         mem = pl.ds(pl.multiple_of(kk * SUB, SUB), SUB)
 
         @pl.when(kk + 1 < parts)
         def _():
-            for copy_in in part_copies(kk + 1):
-                copy_in.start()
+            start_copies(kk + 1)
 
         for copy_in in part_copies(kk):
             copy_in.wait()
@@ -243,20 +282,18 @@
             return pltpu.roll(source[p.nt * p.edge_groups + e, mem, :], (LANES - HALO - place * 2 * HALO) % LANES, 1)
 
         for f in range(p.fields):
-            for r in range(p.rows):
-                s0[r + HALO, f] = edge_tile(p, state, r, f, mem, lane)
             for i in range(HALO):
                 s0[i, f] = edge_of(low, i * p.fields + f)
-                s0[HALO + p.rows + i, f] = edge_of(high, i * p.fields + f)
+                s0[HALO + i, f] = edge_of(high, i * p.fields + f)
 
         def load0(row, f, t):
+            if HALO <= row < HALO + p.rows:
+                return state[row - HALO, f, mem, t * LANES : (t + 1) * LANES]
+            i = row if row < HALO else row - p.rows
             if t == p.nt:
-                return s0[row, f]
-            if row < HALO:
-                return low[(t * HALO + row) * p.fields + f, mem, :]
-            if row >= HALO + p.rows:
-                return high[(t * HALO + row - HALO - p.rows) * p.fields + f, mem, :]
-            return state[row - HALO, f, mem, (p.first + t) * LANES : (p.first + t + 1) * LANES]
+                return s0[i, f]
+            source = low if row < HALO else high
+            return source[(t * HALO + i % HALO) * p.fields + f, mem, :]
 
         def keep_zero(row, value):
             if row < HALO:
@@ -325,12 +362,12 @@
                 out[pl.ds(base + p.hrf * p.slots + i, 1), :] = jnp.zeros((1, LANES), jnp.float32)
 
 
-def finish_kernel(plan, table, flags, obs, ahead, seen, own, other, *rest):
+def finish_kernel(plan, table, obs, ahead, seen, own, other, *rest):
     out, staged, sems = rest[-3:]
     p = plan
     n = p.slots
-    core = flags[2]
-    me = flags[3]
+    me = lax.axis_index("mem")
+    core = lax.rem(me, 2)
     free = p.total - 1.0
     shape = (n, LANES)
     lane = lane_ids(shape)
@@ -351,10 +388,10 @@
         return [pick(a, base + k) for k in range(n)]
 
     def product(parts, b):
-        total = parts[0] * b[0:1]
-        for k in range(1, n):
-            total = total + parts[k] * b[k : k + 1]
-        return total
+        terms = [parts[k] * b[k : k + 1] for k in range(n)]
+        while len(terms) > 1:
+            terms = [sum(terms[i : i + 2][1:], terms[i]) for i in range(0, len(terms), 2)]
+        return terms[0]
 
     moments = jnp.zeros(shape, jnp.float32)
     sums = jnp.zeros((SUB, LANES), jnp.float32)
@@ -505,39 +542,38 @@
     f32 = jnp.float32
     shape = pltpu.VMEM
 
-    sent = [(h.message, p.members, LANES) for h in chunks for _ in range(2)]
-    out = call(
-        functools.partial(pack_kernel, p),
-        [pltpu.VMEM((p.rows, p.fields, p.members, p.columns), f32)] + [pltpu.HBM(a, f32) for a in sent],
-        [HBM],
-        [pltpu.VMEM(a, f32) for a in sent]
-        + [
-            pltpu.VMEM(ensemble.shape, f32),
-            pltpu.SemaphoreType.DMA((p.members // SUB,)),
-            pltpu.SemaphoreType.DMA((p.members // SUB, len(sent))),
-        ],
-        out_specs=[VMEM] + [HBM] * len(sent),
-        name="pack",
-    )(pltpu.with_memory_space_constraint(ensemble, pltpu.HBM))
-    state, messages = out[0], out[1:]
-    up = [(i, i + 1) for i in range(bands - 1)]
-    down = [(i + 1, i) for i in range(bands - 1)]
-    low, high = [], []
-    for c in range(len(chunks)):
-        low.append(lax.ppermute(messages[2 * c], "lat", up))
-        high.append(lax.ppermute(messages[2 * c + 1], "lat", down))
-
-    obs = jnp.concatenate(
-        [
-            after(obs_value, messages[0])[0],
-            obs_var[0],
-            obs_loop[0].astype(f32),
-            jnp.broadcast_to(obs_count[0][:, None].astype(f32), (1, slots)),
-            obs_cell[0].astype(f32),
-        ],
-        axis=1,
-    )
-    obs = jnp.pad(obs, ((0, 0), (0, -obs.shape[1] % LANES)))
+    given = (obs_value[0], obs_var[0], obs_loop[0], obs_count, obs_cell[0])
+    given = tuple(a.reshape(1, 1, -1) for a in given)
+
+    def pack(h, source):
+        sent = (h.message, p.members, LANES)
+        more = given if h.first == 0 else ()
+        return call(
+            functools.partial(pack_kernel, h),
+            [pltpu.VMEM((p.rows, p.fields, p.members, (h.nt + 1) * LANES), f32), pltpu.HBM(sent, f32), pltpu.HBM(sent, f32)]
+            + [pltpu.VMEM((1, LANES), f32) for _ in more[:1]],
+            [HBM] + [ANY if a.size == 1 else HBM for a in more],
+            [
+                pltpu.VMEM(sent, f32),
+                pltpu.VMEM(sent, f32),
+                pltpu.VMEM((p.members, p.fields, p.rows, h.nt * LANES), f32),
+                pltpu.VMEM((2, p.members, p.fields, p.rows, LANES), f32),
+                pltpu.SemaphoreType.DMA((p.members // SUB, 3)),
+                pltpu.SemaphoreType.DMA((p.members // SUB, 2)),
+            ]
+            + [pltpu.VMEM(a.shape, a.dtype) for a in more]
+            + [pltpu.VMEM((SUB, LANES), f32) for _ in more[:1]]
+            + [pltpu.SemaphoreType.DMA((len(more),)) for _ in more[:1]],
+            out_specs=[VMEM, HBM, HBM] + [VMEM for _ in more[:1]],
+            name="pack",
+        )(*(a if a.size == 1 else pltpu.with_memory_space_constraint(a, pltpu.HBM) for a in (source,) + more))
+
+    packed = [pack(h, ensemble) for h in chunks]
+    messages = [a for part in packed for a in part[1:3]]
+    swaps = [[pair for i in range(begin, bands - 1, 2) for pair in ((i, i + 1), (i + 1, i))] for begin in range(2)]
+    halo = [[lax.ppermute(messages[2 * c + i], "lat", swaps[i]) for i in range(2)] for c in range(len(chunks))]
+
+    obs = packed[0][3]
     bit = 1
     while bit < groups:
         step = 2 if bit == 1 or bit * 4 > groups else 4
@@ -545,10 +581,15 @@
         obs = jnp.concatenate([obs] + there, axis=0)
         bit *= step
 
-    band = lax.axis_index("lat")
-    me = lax.axis_index("mem")
-    table = places(p, chunks, me, obs[:, 4 * slots : 5 * slots].astype(jnp.int32))
-    flags = jnp.stack([band > 0, band < bands - 1, lax.rem(me, 2), me]).astype(jnp.int32)
+    table = call(
+        table_kernel,
+        [pltpu.SMEM((5 * groups * slots,), jnp.int32)],
+        [ANY],
+        [pltpu.SemaphoreType.DMA],
+        out_specs=[SMEM],
+        name="places",
+    )(places(p, chunks, lax.axis_index("mem"), obs[:, 4 * slots : 5 * slots].astype(jnp.int32)))[0]
+    table = pltpu.with_memory_space_constraint(table, pltpu.SMEM)
 
     def near(x):
         return pltpu.with_memory_space_constraint(x, pltpu.VMEM)
@@ -569,37 +610,37 @@
                 shape((h.total_rows, LANES), f32),
                 shape((h.total_rows, LANES), f32),
             ],
-            [SMEM, SMEM, VMEM, HBM, HBM],
-            [pltpu.VMEM(stage[:2] + stage[3:], f32), pltpu.VMEM(stage, f32), pltpu.VMEM(stage, f32)]
+            [SMEM, VMEM, ANY, ANY],
+            [pltpu.VMEM((2 * HALO, p.fields, SUB, LANES), f32), pltpu.VMEM(stage, f32), pltpu.VMEM(stage, f32)]
             + [pltpu.VMEM((h.message, p.members, LANES), f32)] * 2
             + [pltpu.SemaphoreType.DMA((p.members // SUB, 2))],
             cost=(1024, h.nt * (6 << 20)),
             name="forecast",
-        )(table, flags if early is None else after(flags, early), near(state), far(low[c]), far(high[c]))
+        )(table, near(packed[c][0] if early is None else after(packed[c][0], early)), *map(far, halo[c]))
         if c:
             own, other = last_sums(p, early)
             send = after(send, own)
-            new = finish(p, chunks[c - 1], table, flags, obs, before + (own, other), new, ensemble.shape)
+            new = finish(p, chunks[c - 1], table, obs, before + (own, other), new, ensemble.shape)
         before = (ahead, seen)
         if not final:
             early = lax.cond(obs_count[0, 0] >= 0, functools.partial(first_sums, p), lambda keep, send: keep, keep, send)
     own, other = last_sums(p, first_sums(p, keep, send), new)
-    return finish(p, chunks[-1], table, flags, obs, before + (own, other), new, ensemble.shape)
-
-
-def finish(plan, h, table, flags, obs, parts, new, whole):
+    return finish(p, chunks[-1], table, obs, before + (own, other), new, ensemble.shape)
+
+
+def finish(plan, h, table, obs, parts, new, whole):
     p = plan
     before = [] if new is None else [new]
     return call(
         functools.partial(finish_kernel, h),
         pltpu.HBM(whole, jnp.float32),
-        [SMEM, SMEM, VMEM, VMEM, VMEM, VMEM, VMEM] + [HBM] * len(before),
+        [SMEM, VMEM, VMEM, VMEM, VMEM, VMEM] + [HBM] * len(before),
         [pltpu.VMEM((p.rows, p.fields, p.members, h.nt * LANES), jnp.float32), pltpu.SemaphoreType.DMA((p.rows, p.fields))],
         cost=(1024, h.nt * (4 << 20)),
         name="finish",
         out_specs=HBM,
-        alias={7: 0} if before else {},
-    )(table, flags, obs, *(pltpu.with_memory_space_constraint(a, pltpu.VMEM) for a in parts), *before)
+        alias={6: 0} if before else {},
+    )(table, obs, *(pltpu.with_memory_space_constraint(a, pltpu.VMEM) for a in parts), *before)
 
 
 def solution(mesh):

time: 79.1 us -> 72.3 us (0.914); the launches traced: 77.5 us -> 72 us
  starting transfers between devices: 23.5 us -> 19.1 us
    ppermute x4, starting transfers between devices: 11.2 us -> 6.74 us  [per_device(): lax.ppermute(messages[2 * c + i], 'lat', swaps[i])]
    pallas_call x1 -> x3, Pallas kernels: 4.21 us -> 6.3 us  [the longest x2 5.71 us: pack(): call(functools.partial(pack_kernel, h), [pltpu.VMEM((p.rows, p.fields, p....]
    pallas_call x2, Pallas kernels: 8.59 us -> 7.34 us  [finish(): call(functools.partial(finish_kernel, h), pltpu.HBM(whole, jnp.float32),...]
    pallas_call x2, Pallas kernels: 13.1 us -> 12.3 us  [per_device(): call(functools.partial(forecast_kernel, h), [shape((h.nt * p.rows * p.fie...]
    unnamed x12 -> x4, local copies, waits for them, and re-layouts: 1.6 us -> 0.97 us
  transfers between devices with their start and end apart: 16 -> 16, of which waited for: 9 -> 9; matrix products, arithmetic and copies ran while one was open for 1% -> 1% of each run, Pallas kernels for 22% -> 27%
where the time goes in v4:
time: 72.3 us; the launch traced here: 72 us
  Pallas kernels  25.9 us (36%)
  waiting for transfers between devices  24.5 us (34%)
  starting transfers between devices  19.1 us (26%)
  local copies, waits for them, and re-layouts  1.07 us (1%)
  between operations  0.81 us (1%)
    pallas_call x2, Pallas kernels, per_device(): call(functools.partial(forecast_kernel, h), [shape((h.nt * p.rows * p.fie...  12.3 us
    ppermute x4, waiting for transfers between devices, sum_phase(): lax.ppermute(total, 'mem', [(i, i ^ (odd if i & 1 else even)) for i in ra...  11.1 us
    ppermute x4, waiting for transfers between devices, per_device(): lax.ppermute(messages[2 * c + i], 'lat', swaps[i])  9.82 us
    pallas_call x2, Pallas kernels, finish(): call(functools.partial(finish_kernel, h), pltpu.HBM(whole, jnp.float32),...  7.34 us
    ppermute x4, starting transfers between devices, per_device(): lax.ppermute(messages[2 * c + i], 'lat', swaps[i])  6.74 us
    pallas_call x2, Pallas kernels, pack(): call(functools.partial(pack_kernel, h), [pltpu.VMEM((p.rows, p.fields, p....  5.71 us
    ppermute x2, starting transfers between devices, first_sums(): lax.ppermute(send, 'mem', [(i, i ^ 1) for i in range(p.groups)])  3.8 us
    ppermute x4, starting transfers between devices, per_device(): lax.ppermute(obs, 'mem', [(i, i ^ bit * b) for i in range(groups)])  3.45 us
  transfers between devices with their start and end apart: 16, of which 9 were waited for; matrix products, arithmetic and copies ran while one was open for 1% of the time, Pallas kernels for 27%

profile of v4, /device:TPU:19, one launch (start us, length us, event | category | flops | bytes accessed | tf_op | source)
XLA Modules:
  0.0 72.0 jit_solution(10491020748055531890)
XLA Ops:
  0.7 2.9 %pack.2 = (f32[4,4,32,640]{3,2,1,0:T(8,128)S(1)}, f32[49,32,128]{2,1,0:T(8,128)}, f32[49,32,128]{2,1,0:T(8,128)}, f32[1,128]{1,0:T(1,128)S(1)}) custom-call(f32[32,4,4,1024]{3,2,1,0:T(4,128)} %raw.3, f32[1,1,16]{2,1,0:T(1,128)} %rest_0_.1, f32[1,1,16]{2,1,0:T(1,128)} %rest_1_.1, s32[1,1,16]{2,1,0:T(1,128)} %rest_2_.1, s32[1,1,1]{2,1,0:T(1,128)} %bitcast.16.rest_3_, ...), custom_call_target="tpu_custom_call" | custom-call | flops 1048576 | bytes 1048576 | tf_op jit(solution)/shard_map/pack/pallas_call | solution.py:551
  3.5 0.7 %collective-permute-start.2 = (f32[1,128]{1,0:T(1,128)S(1)}, f32[1,128]{1,0:T(1,128)S(1)}, u32[]{:S(2)}, u32[]{:S(2)}) collective-permute-start(f32[1,128]{1,0:T(1,128)S(1)} %get-tuple-element.33), channel_id=1, source_target_pairs={{0,4},{4,0},{8,12},{12,8},{16,20},{20,16},{24,28},{28,24},{1,5},{5... | collective-permute-start | bytes 1544 | tf_op jit(solution)/shard_map/ppermute | solution.py:580
  4.3 1.4 %collective-permute-start.6 = (f32[49,32,128]{2,1,0:T(8,128)}, f32[49,32,128]{2,1,0:T(8,128)}, u32[]{:S(2)}, u32[]{:S(2)}) collective-permute-start(f32[49,32,128]{2,1,0:T(8,128)} %get-tuple-element.36), channel_id=1, source_target_pairs={{0,1},{1,0},{2,3},{3,2},{4,5},{5,4},{6,7},{7,6},{8,9},{9,8},{10,11... | collective-permute-start | bytes 2408456 | tf_op jit(solution)/shard_map/ppermute | solution.py:574
  5.6 1.9 %collective-permute-start.7 = (f32[49,32,128]{2,1,0:T(8,128)}, f32[49,32,128]{2,1,0:T(8,128)}, u32[]{:S(2)}, u32[]{:S(2)}) collective-permute-start(f32[49,32,128]{2,1,0:T(8,128)} %get-tuple-element.37), channel_id=1, source_target_pairs={{1,2},{2,1},{5,6},{6,5},{9,10},{10,9},{13,14},{14,13},{17,18},{18,... | collective-permute-start | bytes 2408456 | tf_op jit(solution)/shard_map/ppermute | solution.py:574
  7.6 0.0 collective-permute-done.2
  7.6 1.3 %collective-permute-start.5 = (f32[2,128]{1,0:T(2,128)S(1)}, f32[2,128]{1,0:T(2,128)S(1)}, u32[]{:S(2)}, u32[]{:S(2)}) collective-permute-start(f32[2,128]{1,0:T(2,128)S(1)} %pad_maximum_fusion), channel_id=1, source_target_pairs={{0,24},{4,28},{8,16},{12,20},{16,8},{20,12},{24,0},{28,4},{1,25},{... | collective-permute-start | bytes 3080 | tf_op jit(solution)/shard_map/ppermute | solution.py:580
  8.9 0.2 collective-permute-start.4
  9.1 1.2 %collective-permute-start.3 = (f32[2,128]{1,0:T(2,128)S(1)}, f32[2,128]{1,0:T(2,128)S(1)}, u32[]{:S(2)}, u32[]{:S(2)}) collective-permute-start(f32[2,128]{1,0:T(2,128)S(1)} %pad_maximum_fusion), channel_id=1, source_target_pairs={{0,8},{4,12},{8,0},{12,4},{16,24},{20,28},{24,16},{28,20},{1,9},{5... | collective-permute-start | bytes 3080 | tf_op jit(solution)/shard_map/ppermute | solution.py:580
  10.3 2.8 %pack.3 = (f32[4,4,32,640]{3,2,1,0:T(8,128)S(1)}, f32[49,32,128]{2,1,0:T(8,128)}, f32[49,32,128]{2,1,0:T(8,128)}) custom-call(f32[32,4,4,1024]{3,2,1,0:T(4,128)} %raw.3), custom_call_target="tpu_custom_call" | custom-call | flops 1048576 | bytes 1048576 | tf_op jit(solution)/shard_map/pack/pallas_call | solution.py:551
  13.1 0.0 collective-permute-done.5
  13.2 0.1 collective-permute-start.8
  13.2 0.0 collective-permute-done.4
  13.2 3.4 %collective-permute-start.9 = (f32[49,32,128]{2,1,0:T(8,128)}, f32[49,32,128]{2,1,0:T(8,128)}, u32[]{:S(2)}, u32[]{:S(2)}) collective-permute-start(f32[49,32,128]{2,1,0:T(8,128)} %get-tuple-element.42), channel_id=1, source_target_pairs={{1,2},{2,1},{5,6},{6,5},{9,10},{10,9},{13,14},{14,13},{17,18},{18,... | collective-permute-start | bytes 2408456 | tf_op jit(solution)/shard_map/ppermute | solution.py:574
  16.7 0.0 collective-permute-done.3
  16.7 0.1 constant_dynamic-update-slice_fusion.4
  16.8 0.1 constant_dynamic-update-slice_fusion.3
  16.9 0.1 constant_dynamic-update-slice_fusion.2
  17.0 0.1 constant_dynamic-update-slice_fusion.1
  17.1 0.1 constant_dynamic-update-slice_fusion
  17.2 0.1 reshape.27.table_in
  17.3 0.6 places.1.table
  17.9 6.2 %collective-permute-done.6.first_in = f32[49,32,128]{2,1,0:T(8,128)} collective-permute-done((f32[49,32,128]{2,1,0:T(8,128)}, f32[49,32,128]{2,1,0:T(8,128)}, u32[]{:S(2)}, u32[]{:S(2)}) %collective-permute-start.6) | collective-permute-done | bytes 802848 | tf_op jit(solution)/shard_map/ppermute | solution.py:574
  24.1 2.9 %collective-permute-done.7.second_in = f32[49,32,128]{2,1,0:T(8,128)} collective-permute-done((f32[49,32,128]{2,1,0:T(8,128)}, f32[49,32,128]{2,1,0:T(8,128)}, u32[]{:S(2)}, u32[]{:S(2)}) %collective-permute-start.7) | collective-permute-done | bytes 802848 | tf_op jit(solution)/shard_map/ppermute | solution.py:574
  27.0 6.1 %forecast.2 = (f32[64,32,128]{2,1,0:T(8,128)S(1)}, f32[32,128]{1,0:T(8,128)S(1)}, f32[544,128]{1,0:T(8,128)S(1)}, f32[544,128]{1,0:T(8,128)S(1)}) custom-call(s32[640]{0:T(1024)S(4)} %places.1.table, f32[4,4,32,640]{3,2,1,0:T(8,128)S(1)} %get-tuple-element.35.state, f32[49,32,128]{2,1,0:T(8,128)} %collective-permute-done.6.first_in, ...), custom_call_target="tpu_custom_call" | custom-call | flops 1024 | bytes 25165824 | tf_op jit(solution)/shard_map/forecast/pallas_call | solution.py:605
  33.1 0.0 copy-start
  33.1 1.0 %copy-done = f32[64,32,128]{2,1,0:T(8,128)} copy-done((f32[64,32,128]{2,1,0:T(8,128)}, f32[64,32,128]{2,1,0:T(8,128)S(1)}, u32[]{:S(2)}) %copy-start) | copy-done | bytes 1048600
  34.1 9.1 %conditional.1 = (f32[544,128]{1,0:T(8,128)S(1)}) conditional(s32[]{:T(128)} %bitcast.6, f32[544,128]{1,0:T(8,128)S(1)} %get-tuple-element.38, (f32[544,128]{1,0:T(8,128)S(1)}, f32[544,128]{1,0:T(8,128)S(1)}) %tuple.14), branch_computations={%region_0.1_spmd, %region_1.2_spmd} | conditional | flops 139264 | bytes 3899480 | solution.py:626
  34.1 1.9 %collective-permute-start = (f32[544,128]{1,0:T(8,128)S(1)}, f32[544,128]{1,0:T(8,128)S(1)}, u32[]{:S(2)}, u32[]{:S(2)}) collective-permute-start(f32[544,128]{1,0:T(8,128)S(1)} %get-tuple-element.14), channel_id=1, source_target_pairs={{0,4},{4,0},{8,12},{12,8},{16,20},{20,16},{24,28},{28,24},{1,5},{5... | collective-permute-start | bytes 835592 | tf_op jit(solution)/shard_map/cond/branch_1_fun/ppermute | solution.py:510
  36.0 1.2 %collective-permute-done = f32[544,128]{1,0:T(8,128)S(1)} collective-permute-done((f32[544,128]{1,0:T(8,128)S(1)}, f32[544,128]{1,0:T(8,128)S(1)}, u32[]{:S(2)}, u32[]{:S(2)}) %collective-permute-start) | collective-permute-done | bytes 278560 | tf_op jit(solution)/shard_map/cond/branch_1_fun/ppermute | solution.py:510
  37.2 1.3 %collective-permute-start.1 = (f32[544,128]{1,0:T(8,128)S(1)}, f32[544,128]{1,0:T(8,128)S(1)}, u32[]{:S(2)}, u32[]{:S(2)}) collective-permute-start(f32[544,128]{1,0:T(8,128)S(1)} %add.62), channel_id=1, source_target_pairs={{0,8},{4,20},{8,0},{12,28},{16,24},{20,4},{24,16},{28,12},{1,9},{5... | collective-permute-start | bytes 835592 | tf_op jit(solution)/shard_map/cond/branch_1_fun/ppermute | solution.py:521
  38.5 4.6 %collective-permute-done.1 = f32[544,128]{1,0:T(8,128)S(1)} collective-permute-done((f32[544,128]{1,0:T(8,128)S(1)}, f32[544,128]{1,0:T(8,128)S(1)}, u32[]{:S(2)}, u32[]{:S(2)}) %collective-permute-start.1) | collective-permute-done | bytes 278560 | tf_op jit(solution)/shard_map/cond/branch_1_fun/ppermute | solution.py:521
  43.1 0.3 collective-permute-start.10
  43.5 0.0 collective-permute-done.8.first_in
  43.5 0.7 collective-permute-done.9.second_in
  44.2 6.1 %forecast.3 = (f32[64,32,128]{2,1,0:T(8,128)S(1)}, f32[32,128]{1,0:T(8,128)S(1)}, f32[544,128]{1,0:T(8,128)S(1)}, f32[544,128]{1,0:T(8,128)S(1)}) custom-call(s32[640]{0:T(1024)S(4)} %places.1.table, f32[4,4,32,640]{3,2,1,0:T(8,128)S(1)} %get-tuple-element.40.state, f32[49,32,128]{2,1,0:T(8,128)} %collective-permute-done.8.first_in, ...), custom_call_target="tpu_custom_call" | custom-call | flops 1024 | bytes 25165824 | tf_op jit(solution)/shard_map/forecast/pallas_call | solution.py:605
  50.3 0.0 collective-permute-done.10
  50.4 1.9 %collective-permute-start.11 = (f32[544,128]{1,0:T(8,128)S(1)}, f32[544,128]{1,0:T(8,128)S(1)}, u32[]{:S(2)}, u32[]{:S(2)}) collective-permute-start(f32[544,128]{1,0:T(8,128)S(1)} %get-tuple-element.47), channel_id=1, source_target_pairs={{0,4},{4,0},{8,12},{12,8},{16,20},{20,16},{24,28},{28,24},{1,5},{5... | collective-permute-start | bytes 835592 | tf_op jit(solution)/shard_map/ppermute | solution.py:510
  52.2 1.2 %collective-permute-done.11 = f32[544,128]{1,0:T(8,128)S(1)} collective-permute-done((f32[544,128]{1,0:T(8,128)S(1)}, f32[544,128]{1,0:T(8,128)S(1)}, u32[]{:S(2)}, u32[]{:S(2)}) %collective-permute-start.11) | collective-permute-done | bytes 278560 | tf_op jit(solution)/shard_map/ppermute | solution.py:510
  53.4 0.7 collective-permute-start.12
  54.1 0.3 collective-permute-start.13
  54.4 4.8 %collective-permute-done.12 = f32[544,128]{1,0:T(8,128)S(1)} collective-permute-done((f32[544,128]{1,0:T(8,128)S(1)}, f32[544,128]{1,0:T(8,128)S(1)}, u32[]{:S(2)}, u32[]{:S(2)}) %collective-permute-start.12) | collective-permute-done | bytes 278560 | tf_op jit(solution)/shard_map/ppermute | solution.py:521
  59.2 0.3 collective-permute-start.14
  59.5 0.0 collective-permute-done.13.other
  59.6 3.7 %finish.2.rest_0_ = f32[32,4,4,1024]{3,2,1,0:T(4,128)} custom-call(s32[640]{0:T(1024)S(4)} %places.1.table, f32[8,128]{1,0:T(8,128)S(1)} %concatenate.8.obs, f32[64,32,128]{2,1,0:T(8,128)S(1)} %copy-done.1, f32[32,128]{1,0:T(8,128)S(1)} %get-tuple-element.49.seen, f32[544,128]{1,0:T(8,128)S(1)} %add.100.own, f32[544,128]{1,0:T(8,128)S(1)} %collective-permute-done.13.other), custom_call_target="tpu_custom_call" | custom-call | flops 1024 | bytes 16777216 | tf_op jit(solution)/shard_map/finish/pallas_call | solution.py:634
  63.2 1.8 %collective-permute-done.14 = f32[544,128]{1,0:T(8,128)S(1)} collective-permute-done((f32[544,128]{1,0:T(8,128)S(1)}, f32[544,128]{1,0:T(8,128)S(1)}, u32[]{:S(2)}, u32[]{:S(2)}) %collective-permute-start.14) | collective-permute-done | bytes 278560 | tf_op jit(solution)/shard_map/ppermute | solution.py:521
  65.0 2.1 %collective-permute-start.15 = (f32[544,128]{1,0:T(8,128)S(1)}, f32[544,128]{1,0:T(8,128)S(1)}, u32[]{:S(2)}, u32[]{:S(2)}) collective-permute-start(f32[544,128]{1,0:T(8,128)S(1)} %add.103.own), channel_id=1, source_target_pairs={{0,4},{4,0},{8,12},{12,8},{16,20},{20,16},{24,28},{28,24},{1,5},{5... | collective-permute-start | bytes 835592 | tf_op jit(solution)/shard_map/ppermute | solution.py:529
  67.2 1.2 %collective-permute-done.15.other = f32[544,128]{1,0:T(8,128)S(1)} collective-permute-done((f32[544,128]{1,0:T(8,128)S(1)}, f32[544,128]{1,0:T(8,128)S(1)}, u32[]{:S(2)}, u32[]{:S(2)}) %collective-permute-start.15) | collective-permute-done | bytes 278560 | tf_op jit(solution)/shard_map/ppermute | solution.py:529
  68.4 3.7 %finish.3 = f32[32,4,4,1024]{3,2,1,0:T(4,128)} custom-call(s32[640]{0:T(1024)S(4)} %places.1.table, f32[8,128]{1,0:T(8,128)S(1)} %concatenate.8.obs, f32[64,32,128]{2,1,0:T(8,128)S(1)} %get-tuple-element.43.ahead, f32[32,128]{1,0:T(8,128)S(1)} %get-tuple-element.44.seen, f32[544,128]{1,0:T(8,128)S(1)} %add.103.own, ...), custom_call_target="tpu_custom_call", output_to_operand_aliasing={{}: (6, {})} | custom-call | flops 1024 | bytes 16777216 | tf_op jit(solution)/shard_map/finish/pallas_call | solution.py:634
  (11 shorter events, 0.2 us)
Async XLA Ops:
  3.5 4.0 %collective-permute-start.2 = (f32[1,128]{1,0:T(1,128)S(1)}, f32[1,128]{1,0:T(1,128)S(1)}, u32[]{:S(2)}, u32[]{:S(2)}) collective-permute-start(f32[1,128]{1,0:T(1,128)S(1)} %get-tuple-element.33), channel_id=1, source_target_pairs={{0,4},{4,0},{8,12},{12,8},{16,20},{20,16},{24,28},{28,24},{1,5},{5... | collective-permute-start | bytes 1544 | tf_op jit(solution)/shard_map/ppermute | solution.py:580
  4.3 19.8 %collective-permute-start.6 = (f32[49,32,128]{2,1,0:T(8,128)}, f32[49,32,128]{2,1,0:T(8,128)}, u32[]{:S(2)}, u32[]{:S(2)}) collective-permute-start(f32[49,32,128]{2,1,0:T(8,128)} %get-tuple-element.36), channel_id=1, source_target_pairs={{0,1},{1,0},{2,3},{3,2},{4,5},{5,4},{6,7},{7,6},{8,9},{9,8},{10,11... | collective-permute-start | bytes 2408456 | tf_op jit(solution)/shard_map/ppermute | solution.py:574
  5.6 21.3 %collective-permute-start.7 = (f32[49,32,128]{2,1,0:T(8,128)}, f32[49,32,128]{2,1,0:T(8,128)}, u32[]{:S(2)}, u32[]{:S(2)}) collective-permute-start(f32[49,32,128]{2,1,0:T(8,128)} %get-tuple-element.37), channel_id=1, source_target_pairs={{1,2},{2,1},{5,6},{6,5},{9,10},{10,9},{13,14},{14,13},{17,18},{18,... | collective-permute-start | bytes 2408456 | tf_op jit(solution)/shard_map/ppermute | solution.py:574
  7.6 5.6 %collective-permute-start.5 = (f32[2,128]{1,0:T(2,128)S(1)}, f32[2,128]{1,0:T(2,128)S(1)}, u32[]{:S(2)}, u32[]{:S(2)}) collective-permute-start(f32[2,128]{1,0:T(2,128)S(1)} %pad_maximum_fusion), channel_id=1, source_target_pairs={{0,24},{4,28},{8,16},{12,20},{16,8},{20,12},{24,0},{28,4},{1,25},{... | collective-permute-start | bytes 3080 | tf_op jit(solution)/shard_map/ppermute | solution.py:580
  8.9 4.4 %collective-permute-start.4 = (f32[2,128]{1,0:T(2,128)S(1)}, f32[2,128]{1,0:T(2,128)S(1)}, u32[]{:S(2)}, u32[]{:S(2)}) collective-permute-start(f32[2,128]{1,0:T(2,128)S(1)} %pad_maximum_fusion), channel_id=1, source_target_pairs={{0,16},{4,20},{8,24},{12,28},{16,0},{20,4},{24,8},{28,12},{1,17},{... | collective-permute-start | bytes 3080 | tf_op jit(solution)/shard_map/ppermute | solution.py:580
  9.1 7.6 %collective-permute-start.3 = (f32[2,128]{1,0:T(2,128)S(1)}, f32[2,128]{1,0:T(2,128)S(1)}, u32[]{:S(2)}, u32[]{:S(2)}) collective-permute-start(f32[2,128]{1,0:T(2,128)S(1)} %pad_maximum_fusion), channel_id=1, source_target_pairs={{0,8},{4,12},{8,0},{12,4},{16,24},{20,28},{24,16},{28,20},{1,9},{5... | collective-permute-start | bytes 3080 | tf_op jit(solution)/shard_map/ppermute | solution.py:580
  13.2 30.3 %collective-permute-start.8 = (f32[49,32,128]{2,1,0:T(8,128)}, f32[49,32,128]{2,1,0:T(8,128)}, u32[]{:S(2)}, u32[]{:S(2)}) collective-permute-start(f32[49,32,128]{2,1,0:T(8,128)} %get-tuple-element.41), channel_id=1, source_target_pairs={{0,1},{1,0},{2,3},{3,2},{4,5},{5,4},{6,7},{7,6},{8,9},{9,8},{10,11... | collective-permute-start | bytes 2408456 | tf_op jit(solution)/shard_map/ppermute | solution.py:574
  13.2 30.9 %collective-permute-start.9 = (f32[49,32,128]{2,1,0:T(8,128)}, f32[49,32,128]{2,1,0:T(8,128)}, u32[]{:S(2)}, u32[]{:S(2)}) collective-permute-start(f32[49,32,128]{2,1,0:T(8,128)} %get-tuple-element.42), channel_id=1, source_target_pairs={{1,2},{2,1},{5,6},{6,5},{9,10},{10,9},{13,14},{14,13},{17,18},{18,... | collective-permute-start | bytes 2408456 | tf_op jit(solution)/shard_map/ppermute | solution.py:574
  33.1 1.0 %copy-start = (f32[64,32,128]{2,1,0:T(8,128)}, f32[64,32,128]{2,1,0:T(8,128)S(1)}, u32[]{:S(2)}) copy-start(f32[64,32,128]{2,1,0:T(8,128)S(1)} %get-tuple-element.48.ahead) | copy-start | bytes 3145732
  34.1 3.1 %collective-permute-start = (f32[544,128]{1,0:T(8,128)S(1)}, f32[544,128]{1,0:T(8,128)S(1)}, u32[]{:S(2)}, u32[]{:S(2)}) collective-permute-start(f32[544,128]{1,0:T(8,128)S(1)} %get-tuple-element.14), channel_id=1, source_target_pairs={{0,4},{4,0},{8,12},{12,8},{16,20},{20,16},{24,28},{28,24},{1,5},{5... | collective-permute-start | bytes 835592 | tf_op jit(solution)/shard_map/cond/branch_1_fun/ppermute | solution.py:510
  37.2 5.9 %collective-permute-start.1 = (f32[544,128]{1,0:T(8,128)S(1)}, f32[544,128]{1,0:T(8,128)S(1)}, u32[]{:S(2)}, u32[]{:S(2)}) collective-permute-start(f32[544,128]{1,0:T(8,128)S(1)} %add.62), channel_id=1, source_target_pairs={{0,8},{4,20},{8,0},{12,28},{16,24},{20,4},{24,16},{28,12},{1,9},{5... | collective-permute-start | bytes 835592 | tf_op jit(solution)/shard_map/cond/branch_1_fun/ppermute | solution.py:521
  43.1 7.2 %collective-permute-start.10 = (f32[544,128]{1,0:T(8,128)S(1)}, f32[544,128]{1,0:T(8,128)S(1)}, u32[]{:S(2)}, u32[]{:S(2)}) collective-permute-start(f32[544,128]{1,0:T(8,128)S(1)} %get-tuple-element.56), channel_id=1, source_target_pairs={{0,16},{4,12},{8,24},{12,4},{16,0},{20,28},{24,8},{28,20},{1,17},{... | collective-permute-start | bytes 835592 | tf_op jit(solution)/shard_map/ppermute | solution.py:521
  43.5 16.1 %copy-start.1 = (f32[64,32,128]{2,1,0:T(8,128)S(1)}, f32[64,32,128]{2,1,0:T(8,128)}, u32[]{:S(2)}) copy-start(f32[64,32,128]{2,1,0:T(8,128)} %copy-done) | copy-start | bytes 3145732
  50.4 3.0 %collective-permute-start.11 = (f32[544,128]{1,0:T(8,128)S(1)}, f32[544,128]{1,0:T(8,128)S(1)}, u32[]{:S(2)}, u32[]{:S(2)}) collective-permute-start(f32[544,128]{1,0:T(8,128)S(1)} %get-tuple-element.47), channel_id=1, source_target_pairs={{0,4},{4,0},{8,12},{12,8},{16,20},{20,16},{24,28},{28,24},{1,5},{5... | collective-permute-start | bytes 835592 | tf_op jit(solution)/shard_map/ppermute | solution.py:510
  53.4 5.8 %collective-permute-start.12 = (f32[544,128]{1,0:T(8,128)S(1)}, f32[544,128]{1,0:T(8,128)S(1)}, u32[]{:S(2)}, u32[]{:S(2)}) collective-permute-start(f32[544,128]{1,0:T(8,128)S(1)} %add.101), channel_id=1, source_target_pairs={{0,8},{4,20},{8,0},{12,28},{16,24},{20,4},{24,16},{28,12},{1,9},{5... | collective-permute-start | bytes 835592 | tf_op jit(solution)/shard_map/ppermute | solution.py:521
  54.1 5.4 %collective-permute-start.13 = (f32[544,128]{1,0:T(8,128)S(1)}, f32[544,128]{1,0:T(8,128)S(1)}, u32[]{:S(2)}, u32[]{:S(2)}) collective-permute-start(f32[544,128]{1,0:T(8,128)S(1)} %add.100.own), channel_id=1, source_target_pairs={{0,4},{4,0},{8,12},{12,8},{16,20},{20,16},{24,28},{28,24},{1,5},{5... | collective-permute-start | bytes 835592 | tf_op jit(solution)/shard_map/ppermute | solution.py:529
  59.2 5.8 %collective-permute-start.14 = (f32[544,128]{1,0:T(8,128)S(1)}, f32[544,128]{1,0:T(8,128)S(1)}, u32[]{:S(2)}, u32[]{:S(2)}) collective-permute-start(f32[544,128]{1,0:T(8,128)S(1)} %add.102), channel_id=1, source_target_pairs={{0,16},{4,12},{8,24},{12,4},{16,0},{20,28},{24,8},{28,20},{1,17},{... | collective-permute-start | bytes 835592 | tf_op jit(solution)/shard_map/ppermute | solution.py:521
  65.0 3.3 %collective-permute-start.15 = (f32[544,128]{1,0:T(8,128)S(1)}, f32[544,128]{1,0:T(8,128)S(1)}, u32[]{:S(2)}, u32[]{:S(2)}) collective-permute-start(f32[544,128]{1,0:T(8,128)S(1)} %add.103.own), channel_id=1, source_target_pairs={{0,4},{4,0},{8,12},{12,8},{16,20},{20,16},{24,28},{28,24},{1,5},{5... | collective-permute-start | bytes 835592 | tf_op jit(solution)/shard_map/ppermute | solution.py:529

commit v5 on v4

--- a/solution.py
+++ b/solution.py
@@ -59,6 +59,7 @@
         self.q = max(1, LANES // self.width)
         most = LANES // (slots * self.q)
         self.counts = chunk_tiles(self.tiles, min(most, -(-self.tiles // 2)), max(1, self.width // LANES))
+        self.counts = [4, 4] if self.counts == [4, 4] else self.counts
         self.starts = [sum(self.counts[:i]) for i in range(len(self.counts))]
         self.halves = 2
         self.hrows = self.rows // self.halves
@@ -79,7 +80,8 @@
         p.first_patch = p.first * LANES // self.width
         p.bands = lax.axis_size("lat")
         p.message = p.nt * self.edge_groups + self.edge_tiles
-        p.total_rows = p.nt * self.block
+        p.cell_rows = p.nt * self.block
+        p.total_rows = p.cell_rows + p.slots + SUB
         return p
 
     def patches_of(self, tile):
@@ -98,8 +100,8 @@
     parts = p.members // SUB
     given = []
     if p.first == 0:
-        given, rest = rest[:5], rest[5:]
-        row_out, (taken, lines, given_sems), rest = rest[3], (rest[-7:-2], *rest[-2:]), rest[:3] + rest[4:-7]
+        given, rest = rest[:4], rest[4:]
+        row_out, (taken, lines, given_sems), rest = rest[3], (rest[-6:-2], *rest[-2:]), rest[:3] + rest[4:-6]
     state, first_out, second_out, up, down, arrived, beside, sems, out_sems = rest
     given_copies = []
     for i, a in enumerate(given):
@@ -114,13 +116,25 @@
             for i, (to, t, n) in enumerate(takes)
         ]
 
-    def message_copies(kk, swapped=0):
+    cut = p.nt // 2
+    pieces = [(0, cut * p.edge_groups), (cut * p.edge_groups, p.message)] if cut else [(0, p.message)]
+
+    def message_copies(kk, piece, swapped=0):
         part = pl.ds(kk * SUB, SUB)
+        lines = pl.ds(pieces[piece][0], pieces[piece][1] - pieces[piece][0])
         inner = (up, down) if swapped == 0 else (down, up)
         return [
-            pltpu.make_async_copy(a.at[:, part, :], b.at[:, part, :], out_sems.at[kk, i])
+            pltpu.make_async_copy(a.at[lines, part, :], b.at[lines, part, :], out_sems.at[kk, 2 * piece + i])
             for i, (a, b) in enumerate(zip(inner, (first_out, second_out)))
         ]
+
+    def send_out(kk, piece):
+        for swapped in range(2):
+
+            @pl.when(odd == swapped)
+            def _():
+                for copy_out in message_copies(kk, piece, swapped):
+                    copy_out.start()
 
     for kk in range(parts):
         for copy_in in part_copies(kk):
@@ -134,6 +148,8 @@
             copy_in.wait()
 
         for i in range(p.nt):
+            if cut and i == cut:
+                send_out(kk, 0)
             cols = slice(i * LANES, (i + 1) * LANES)
             for f in range(p.fields):
                 for r in range(p.rows):
@@ -158,13 +174,7 @@
                     packed = jnp.where(inside, pltpu.roll(edge, place + HALO, 1), packed)
                 out[p.nt * p.edge_groups + e, mem, :] = packed
 
-        for swapped in range(2):
-
-            @pl.when(odd == swapped)
-            def _():
-                for copy_out in message_copies(kk, swapped):
-                    copy_out.start()
-
+        send_out(kk, len(pieces) - 1)
         return carry
 
     lax.fori_loop(0, parts, body, 0)
@@ -178,8 +188,9 @@
             row = jnp.where((lane >= i * p.slots) & (lane < (i + 1) * p.slots), line, row)
         row_out[...] = row[:1]
     for kk in range(parts):
-        for copy_out in message_copies(kk):
-            copy_out.wait()
+        for piece in range(len(pieces)):
+            for copy_out in message_copies(kk, piece):
+                copy_out.wait()
 
 
 def step_once(p, rows_in, load, store, last, scale):
@@ -193,20 +204,21 @@
         held = {row: {f: [load(row, f, t) for t in range(ring)] for f in pair} for row in range(2)}
         for row in range(1, rows_in - 1):
             held[row + 1] = {f: [load(row + 1, f, t) for t in range(ring)] for f in pair}
-            coef = []
+            rolled = {}
+
+            def turn(f, t, by):
+                if (f, t, by) not in rolled:
+                    rolled[f, t, by] = pltpu.roll(held[row][f][t], by, 1)
+                return rolled[f, t, by]
+
             for t in range(out_tiles):
                 u, v = ((held[row][i][t] if i in held[row] else load(row, i, t)) * (scale * time_step * 0.5) for i in range(2))
-                coef.append((k - u, k + u, k - v, k + v))
-            for f in pair:
-                x = held[row][f]
-                right = [pltpu.roll(a, 1, 1) for a in x]
-                left = [pltpu.roll(a, LANES - 1, 1) for a in x]
-                for t in range(out_tiles):
-                    west = jnp.where(lane == 0, right[(t - 1) % ring], right[t])
-                    east = jnp.where(lane == LANES - 1, left[(t + 1) % ring], left[t])
-                    ce, cw, cn, cs = coef[t]
+                ce, cw, cn, cs = k - u, k + u, k - v, k + v
+                for f in pair:
+                    west = pltpu.roll(jnp.where(lane == LANES - 1, held[row][f][(t - 1) % ring], held[row][f][t]), 1, 1)
+                    east = pltpu.roll(jnp.where(lane == 0, held[row][f][(t + 1) % ring], held[row][f][t]), LANES - 1, 1)
                     moved = (ce * east + cw * west) + (cn * held[row + 1][f][t] + cs * held[row - 1][f][t])
-                    store(row, f, t, centre * x[t] + moved)
+                    store(row, f, t, centre * held[row][f][t] + moved)
             del held[row - 1]
 
 
@@ -226,9 +238,8 @@
     r = cells // p.width % p.rows
     f = cells // (p.width * p.rows)
     tile, lane = column // LANES, column % LANES
-    index = r % p.hrows * p.fields + f
     shift = ((patch - first) * p.slots + slot - lane) % LANES
-    table = [(tile * p.rows + r) * p.fields + f, shift, tile * p.block + index * p.slots, tile * p.block + p.hrf * p.slots + index, r // p.hrows]
+    table = [(tile * p.rows + r) * p.fields + f, shift]
     return jnp.stack(table).reshape(-1)
 
 
@@ -338,6 +349,14 @@
     sides = [
         jnp.concatenate([turned[j * p.slots : (j + 1) * p.slots], ones], axis=0).astype(jnp.bfloat16) for j in range(p.np)
     ]
+    lanes = lane_ids((p.slots + 2 * SUB, LANES))
+    moments = jnp.zeros((p.slots + 2 * SUB, LANES), jnp.float32)
+    joined = jnp.concatenate([a.astype(jnp.bfloat16) for a in (high, low_part, high)], axis=0)
+    for j in range(p.np):
+        part = jnp.dot(sides[j], joined, preferred_element_type=jnp.float32)
+        moments = jnp.where((lanes >= j * p.slots) & (lanes < (j + 1) * p.slots), part, moments)
+    for out in (keep, send):
+        out[pl.ds(p.cell_rows, p.slots + SUB), :] = moments[: p.slots + SUB]
     for side in range(p.halves):
         out = keep if side == 0 else send
         half = core if side == 0 else 1 - core
@@ -362,12 +381,10 @@
                 out[pl.ds(base + p.hrf * p.slots + i, 1), :] = jnp.zeros((1, LANES), jnp.float32)
 
 
-def finish_kernel(plan, table, obs, ahead, seen, own, other, *rest):
-    out, staged, sems = rest[-3:]
+def solve_kernel(plan, obs, seen, own, factors, centres, keeps):
     p = plan
     n = p.slots
     me = lax.axis_index("mem")
-    core = lax.rem(me, 2)
     free = p.total - 1.0
     shape = (n, LANES)
     lane = lane_ids(shape)
@@ -393,25 +410,15 @@
             terms = [sum(terms[i : i + 2][1:], terms[i]) for i in range(0, len(terms), 2)]
         return terms[0]
 
-    moments = jnp.zeros(shape, jnp.float32)
-    sums = jnp.zeros((SUB, LANES), jnp.float32)
     given = [jnp.zeros((SUB, LANES), jnp.float32) for _ in range(4)]
-    every = p.groups * n
     for j in range(p.np):
         source = (p.first_patch + j) ^ me
         line = jnp.broadcast_to(obs[pl.ds(source, 1), :], (SUB, LANES))
         mine = (lane_sub >= j * n) & (lane_sub < (j + 1) * n)
-        for i in range(4):
-            given[i] = jnp.where(mine, pltpu.roll(line, (j * n - i * n) % LANES, 1), given[i])
-        for o in range(n):
-            to = j * n + o
-            shift, at, line, half = (table[i * every + source * n + o] for i in range(1, 5))
-            here = half == core
-            at = pl.ds(pl.multiple_of(at, SUB), n)
-            value = jnp.where(here, own[at, :], other[at, :])
-            moments = jnp.where(lane == to, pltpu.roll(value, shift, 1), moments)
-            value = jnp.where(here, own[pl.ds(line, 1), :], other[pl.ds(line, 1), :])
-            sums = jnp.where(lane_sub == to, pltpu.roll(jnp.broadcast_to(value, (SUB, LANES)), shift, 1), sums)
+        for i, place in enumerate((0, 1, 2, 4)):
+            given[i] = jnp.where(mine, pltpu.roll(line, (j * n - place * n) % LANES, 1), given[i])
+    moments = own[pl.ds(p.cell_rows, n), :]
+    sums = own[pl.ds(p.cell_rows + n, SUB), :]
     value, variance, loop, count = (a[0:1] for a in given)
     mean = sums[0:1] * (1.0 / p.total)
     slot = (lane_row % n).astype(jnp.float32)
@@ -456,13 +463,19 @@
 
     wide = lane_ids((p.members, LANES))
     high, low_part = (a.astype(jnp.float32) for a in split(weights))
-    factors = []
     for j in range(p.np):
         here, there, last = (pltpu.roll(a, (i * n - j * n) % LANES, 1) for i, a in enumerate((high, high, low_part)))
-        mine = jnp.where(wide < n, here, jnp.where(wide < 2 * n, there, last))[:, : 3 * n].astype(jnp.bfloat16)
-        centre = pick(jnp.broadcast_to(mean, shape), row + j * n)
-        keep0 = pick(jnp.broadcast_to(spread0, (SUB, LANES)), jnp.full((SUB, LANES), j * n, jnp.int32))[0:1]
-        factors.append((mine, centre, keep0))
+        factors[j] = jnp.where(wide < n, here, jnp.where(wide < 2 * n, there, last))
+        centres[j] = pick(jnp.broadcast_to(mean, shape), row + j * n)
+        keeps[j] = pick(jnp.broadcast_to(spread0, (SUB, LANES)), jnp.full((SUB, LANES), j * n, jnp.int32))
+
+
+def finish_kernel(plan, ahead, factors, centres, keeps, own, other, *rest):
+    out, staged, sems = rest[-3:]
+    p = plan
+    n = p.slots
+    core = lax.rem(lax.axis_index("mem"), 2)
+    mixing = [(factors[j][:, : 3 * n].astype(jnp.bfloat16), centres[j], keeps[j][0:1]) for j in range(p.np)]
 
     def line_copy(r, f):
         cols = pl.ds(p.first * LANES, p.nt * LANES)
@@ -481,7 +494,7 @@
             plain = jnp.where(at_own, own[at : at + p.fields, :], other[at : at + p.fields, :])
             results = []
             for j, first, stop in p.patches_of(t):
-                mine, centre, keep0 = factors[j]
+                mine, centre, keep0 = mixing[j]
                 centred = [pieces[f] - centre * plain[f : f + 1, :] for f in range(p.fields)]
                 high, low_part = split(jnp.concatenate(centred, axis=1))
                 joined = jnp.concatenate([high, low_part, high], axis=0)
@@ -505,10 +518,8 @@
             line_copy(r, f).wait()
 
 
-def first_sums(plan, keep, send):
-    p = plan
-    total = keep + lax.ppermute(send, "mem", [(i, i ^ 1) for i in range(p.groups)])
-    return sum_phase(p, 0, total)
+def core_sums(plan, keep, send):
+    return keep + lax.ppermute(send, "mem", [(i, i ^ 1) for i in range(plan.groups)])
 
 
 def sum_phase(plan, phase, total, waited=None):
@@ -542,8 +553,7 @@
     f32 = jnp.float32
     shape = pltpu.VMEM
 
-    given = (obs_value[0], obs_var[0], obs_loop[0], obs_count, obs_cell[0])
-    given = tuple(a.reshape(1, 1, -1) for a in given)
+    given = (obs_value, obs_var, obs_loop, obs_cell)
 
     def pack(h, source):
         sent = (h.message, p.members, LANES)
@@ -552,28 +562,24 @@
             functools.partial(pack_kernel, h),
             [pltpu.VMEM((p.rows, p.fields, p.members, (h.nt + 1) * LANES), f32), pltpu.HBM(sent, f32), pltpu.HBM(sent, f32)]
             + [pltpu.VMEM((1, LANES), f32) for _ in more[:1]],
-            [HBM] + [ANY if a.size == 1 else HBM for a in more],
+            [HBM] * (1 + len(more)),
             [
                 pltpu.VMEM(sent, f32),
                 pltpu.VMEM(sent, f32),
                 pltpu.VMEM((p.members, p.fields, p.rows, h.nt * LANES), f32),
                 pltpu.VMEM((2, p.members, p.fields, p.rows, LANES), f32),
                 pltpu.SemaphoreType.DMA((p.members // SUB, 3)),
-                pltpu.SemaphoreType.DMA((p.members // SUB, 2)),
+                pltpu.SemaphoreType.DMA((p.members // SUB, 4)),
             ]
             + [pltpu.VMEM(a.shape, a.dtype) for a in more]
             + [pltpu.VMEM((SUB, LANES), f32) for _ in more[:1]]
             + [pltpu.SemaphoreType.DMA((len(more),)) for _ in more[:1]],
             out_specs=[VMEM, HBM, HBM] + [VMEM for _ in more[:1]],
             name="pack",
-        )(*(a if a.size == 1 else pltpu.with_memory_space_constraint(a, pltpu.HBM) for a in (source,) + more))
-
-    packed = [pack(h, ensemble) for h in chunks]
-    messages = [a for part in packed for a in part[1:3]]
-    swaps = [[pair for i in range(begin, bands - 1, 2) for pair in ((i, i + 1), (i + 1, i))] for begin in range(2)]
-    halo = [[lax.ppermute(messages[2 * c + i], "lat", swaps[i]) for i in range(2)] for c in range(len(chunks))]
-
-    obs = packed[0][3]
+        )(*(pltpu.with_memory_space_constraint(a, pltpu.HBM) for a in (source,) + more))
+
+    packed = [pack(chunks[0], ensemble)]
+    obs = jnp.where(jnp.arange(LANES) < 4 * slots, packed[0][3], obs_count.astype(f32))
     bit = 1
     while bit < groups:
         step = 2 if bit == 1 or bit * 4 > groups else 4
@@ -581,14 +587,19 @@
         obs = jnp.concatenate([obs] + there, axis=0)
         bit *= step
 
+    packed += [pack(h, after(ensemble, obs)) for h in chunks[1:]]
+    messages = [a for part in packed for a in part[1:3]]
+    swaps = [[pair for i in range(begin, bands - 1, 2) for pair in ((i, i + 1), (i + 1, i))] for begin in range(2)]
+    halo = [[lax.ppermute(messages[2 * c + i], "lat", swaps[i]) for i in range(2)] for c in range(len(chunks))]
+
     table = call(
         table_kernel,
-        [pltpu.SMEM((5 * groups * slots,), jnp.int32)],
+        [pltpu.SMEM((2 * groups * slots,), jnp.int32)],
         [ANY],
         [pltpu.SemaphoreType.DMA],
         out_specs=[SMEM],
         name="places",
-    )(places(p, chunks, lax.axis_index("mem"), obs[:, 4 * slots : 5 * slots].astype(jnp.int32)))[0]
+    )(places(p, chunks, lax.axis_index("mem"), obs[:, 3 * slots : 4 * slots].astype(jnp.int32)))[0]
     table = pltpu.with_memory_space_constraint(table, pltpu.SMEM)
 
     def near(x):
@@ -597,10 +608,9 @@
     def far(x):
         return pltpu.with_memory_space_constraint(x, pltpu.HBM)
 
-    new = None
+    parts = []
     early = None
     for c, h in enumerate(chunks):
-        final = c == len(chunks) - 1
         stage = (p.rows + 2 * HALO, p.fields, h.nt + 1, SUB, LANES)
         ahead, seen, keep, send = call(
             functools.partial(forecast_kernel, h),
@@ -614,33 +624,62 @@
             [pltpu.VMEM((2 * HALO, p.fields, SUB, LANES), f32), pltpu.VMEM(stage, f32), pltpu.VMEM(stage, f32)]
             + [pltpu.VMEM((h.message, p.members, LANES), f32)] * 2
             + [pltpu.SemaphoreType.DMA((p.members // SUB, 2))],
-            cost=(1024, h.nt * (6 << 20)),
+            cost=(1024, h.nt * (6 << 20) if c else 1024),
             name="forecast",
         )(table, near(packed[c][0] if early is None else after(packed[c][0], early)), *map(far, halo[c]))
-        if c:
-            own, other = last_sums(p, early)
-            send = after(send, own)
-            new = finish(p, chunks[c - 1], table, obs, before + (own, other), new, ensemble.shape)
-        before = (ahead, seen)
-        if not final:
-            early = lax.cond(obs_count[0, 0] >= 0, functools.partial(first_sums, p), lambda keep, send: keep, keep, send)
-    own, other = last_sums(p, first_sums(p, keep, send), new)
-    return finish(p, chunks[-1], table, obs, before + (own, other), new, ensemble.shape)
-
-
-def finish(plan, h, table, obs, parts, new, whole):
+        if c == 0:
+            early = lax.cond(
+                obs_count[0, 0] >= 0,
+                lambda keep, send: sum_phase(p, 0, core_sums(p, keep, send)),
+                lambda keep, send: keep,
+                keep,
+                send,
+            )
+            parts.append((ahead, seen, early))
+        else:
+            if c == 1:
+                first = last_sums(p, parts[0][2])
+                send = after(send, first[0])
+            early = send
+            parts.append((ahead, seen, sum_phase(p, 0, core_sums(p, keep, send))))
+    new = None
+    for c, h in enumerate(chunks):
+        ahead, seen, total = parts[c]
+        own, other = first if c == 0 and len(chunks) > 1 else last_sums(p, total, new)
+        new = finish(p, h, obs, (ahead, seen, own, other), new, ensemble.shape)
+    return new
+
+
+def finish(plan, h, obs, parts, new, whole):
     p = plan
+    f32 = jnp.float32
+    ahead, seen, own, other = parts
+
+    def near(*arrays):
+        return [pltpu.with_memory_space_constraint(a, pltpu.VMEM) for a in arrays]
+
+    solved = call(
+        functools.partial(solve_kernel, h),
+        [
+            pltpu.VMEM((h.np, p.members, LANES), f32),
+            pltpu.VMEM((h.np, p.slots, LANES), f32),
+            pltpu.VMEM((h.np, SUB, LANES), f32),
+        ],
+        [VMEM] * 3,
+        cost=(1024, 6 << 20),
+        name="solve",
+    )(*near(obs, seen, own))
     before = [] if new is None else [new]
     return call(
         functools.partial(finish_kernel, h),
-        pltpu.HBM(whole, jnp.float32),
-        [SMEM, VMEM, VMEM, VMEM, VMEM, VMEM] + [HBM] * len(before),
-        [pltpu.VMEM((p.rows, p.fields, p.members, h.nt * LANES), jnp.float32), pltpu.SemaphoreType.DMA((p.rows, p.fields))],
+        pltpu.HBM(whole, f32),
+        [VMEM] * 6 + [HBM] * len(before),
+        [pltpu.VMEM((p.rows, p.fields, p.members, h.nt * LANES), f32), pltpu.SemaphoreType.DMA((p.rows, p.fields))],
         cost=(1024, h.nt * (4 << 20)),
         name="finish",
         out_specs=HBM,
         alias={6: 0} if before else {},
-    )(table, obs, *(pltpu.with_memory_space_constraint(a, pltpu.VMEM) for a in parts), *before)
+    )(*near(ahead, *solved, own, other), *before)
 
 
 def solution(mesh):

time: 72.3 us -> 69.8 us (0.965)
  waiting for transfers between devices: 24.5 us -> 21 us
  starting transfers between devices: 19.1 us -> 21.5 us
  Pallas kernels: 25.9 us -> 24.7 us
    ppermute x4, waiting for transfers between devices: 9.82 us -> 4.52 us  [per_device(): lax.ppermute(messages[2 * c + i], 'lat', swaps[i])]
    ppermute x4, waiting for transfers between devices: 0.01 us -> 2.43 us  [per_device(): lax.ppermute(obs, 'mem', [(i, i ^ bit * b) for i in range(groups)])]
    ppermute x2, starting transfers between devices: 3.8 us -> 5.78 us  [core_sums(): lax.ppermute(send, 'mem', [(i, i ^ 1) for i in range(plan.groups)])]
    ppermute x2, waiting for transfers between devices: 1.19 us -> 0.01 us  [last_sums(): lax.ppermute(total, 'mem', [(i, i ^ 1) for i in range(p.groups)])]
    pallas_call x2, Pallas kernels: 12.3 us -> 11.4 us  [per_device(): call(functools.partial(forecast_kernel, h), [shape((h.nt * p.rows * p.fie...]
    pallas_call x3 -> x5, Pallas kernels: 7.92 us -> 7.5 us  [the longest x2 3.74 us: finish(): call(functools.partial(solve_kernel, h), [pltpu.VMEM((h.np, p.members, LA...]
  transfers between devices with their start and end apart: 16 -> 16, of which waited for: 9 -> 11; matrix products, arithmetic and copies ran while one was open for 1% -> 0% of each run, Pallas kernels for 27% -> 29%
where the time goes in v5:
time: 69.8 us; the launch traced here: 69.5 us
  Pallas kernels  24.7 us (35%)
  starting transfers between devices  21.5 us (31%)
  waiting for transfers between devices  21 us (30%)
  local copies, waits for them, and re-layouts  1.07 us (2%)
  between operations  0.84 us (1%)
    ppermute x4, waiting for transfers between devices, sum_phase(): lax.ppermute(total, 'mem', [(i, i ^ (odd if i & 1 else even)) for i in ra...  11.7 us
    pallas_call x2, Pallas kernels, per_device(): call(functools.partial(forecast_kernel, h), [shape((h.nt * p.rows * p.fie...  11.4 us
    ppermute x4, starting transfers between devices, per_device(): lax.ppermute(messages[2 * c + i], 'lat', swaps[i])  6.99 us
    pallas_call x2, Pallas kernels, pack(): call(functools.partial(pack_kernel, h), [pltpu.VMEM((p.rows, p.fields, p....  5.81 us
    ppermute x2, starting transfers between devices, core_sums(): lax.ppermute(send, 'mem', [(i, i ^ 1) for i in range(plan.groups)])  5.78 us
    ppermute x4, waiting for transfers between devices, per_device(): lax.ppermute(messages[2 * c + i], 'lat', swaps[i])  4.52 us
    pallas_call x2, Pallas kernels, finish(): call(functools.partial(solve_kernel, h), [pltpu.VMEM((h.np, p.members, LA...  3.74 us
    ppermute x4, starting transfers between devices, per_device(): lax.ppermute(obs, 'mem', [(i, i ^ bit * b) for i in range(groups)])  3.67 us
  transfers between devices with their start and end apart: 16, of which 11 were waited for; matrix products, arithmetic and copies ran while one was open for 0% of the time, Pallas kernels for 29%

profile of v5, /device:TPU:19, one launch (start us, length us, event | category | flops | bytes accessed | tf_op | source)
XLA Modules:
  0.0 69.5 jit_solution(15738400184228113646)
XLA Ops:
  0.0 2.9 %pack.2 = (f32[4,4,32,640]{3,2,1,0:T(8,128)S(1)}, f32[49,32,128]{2,1,0:T(8,128)}, f32[49,32,128]{2,1,0:T(8,128)}, f32[1,128]{1,0:T(1,128)S(1)}) custom-call(f32[32,4,4,1024]{3,2,1,0:T(4,128)} %raw.2, f32[1,1,16]{2,1,0:T(1,128)} %rest_0_.1, f32[1,1,16]{2,1,0:T(1,128)} %rest_1_.1, s32[1,1,16]{2,1,0:T(1,128)} %rest_2_.1, s32[1,1,16]{2,1,0:T(1,128)} %rest_3_.1), custom_call_target="tpu_custom_call" | custom-call | flops 1048576 | bytes 1048576 | tf_op jit(solution)/shard_map/pack/pallas_call | solution.py:561
  2.9 1.4 %collective-permute-start.6 = (f32[49,32,128]{2,1,0:T(8,128)}, f32[49,32,128]{2,1,0:T(8,128)}, u32[]{:S(2)}, u32[]{:S(2)}) collective-permute-start(f32[49,32,128]{2,1,0:T(8,128)} %get-tuple-element.44), channel_id=1, source_target_pairs={{0,1},{1,0},{2,3},{3,2},{4,5},{5,4},{6,7},{7,6},{8,9},{9,8},{10,11... | collective-permute-start | bytes 2408456 | tf_op jit(solution)/shard_map/ppermute | solution.py:593
  4.3 1.9 %collective-permute-start.7 = (f32[49,32,128]{2,1,0:T(8,128)}, f32[49,32,128]{2,1,0:T(8,128)}, u32[]{:S(2)}, u32[]{:S(2)}) collective-permute-start(f32[49,32,128]{2,1,0:T(8,128)} %get-tuple-element.45), channel_id=1, source_target_pairs={{1,2},{2,1},{5,6},{6,5},{9,10},{10,9},{13,14},{14,13},{17,18},{18,... | collective-permute-start | bytes 2408456 | tf_op jit(solution)/shard_map/ppermute | solution.py:593
  6.9 1.0 %collective-permute-start.2 = (f32[1,128]{1,0:T(1,128)S(1)}, f32[1,128]{1,0:T(1,128)S(1)}, u32[]{:S(2)}, u32[]{:S(2)}) collective-permute-start(f32[1,128]{1,0:T(1,128)S(1)} %compare_select_fusion.1), channel_id=1, source_target_pairs={{0,4},{4,0},{8,12},{12,8},{16,20},{20,16},{24,28},{28,24},{1,5},{5... | collective-permute-start | bytes 1544 | tf_op jit(solution)/shard_map/ppermute | solution.py:586
  7.9 0.8 %collective-permute-done.2 = f32[1,128]{1,0:T(1,128)S(1)} collective-permute-done((f32[1,128]{1,0:T(1,128)S(1)}, f32[1,128]{1,0:T(1,128)S(1)}, u32[]{:S(2)}, u32[]{:S(2)}) %collective-permute-start.2) | collective-permute-done | bytes 544 | tf_op jit(solution)/shard_map/ppermute | solution.py:586
  8.7 1.2 %collective-permute-start.5 = (f32[2,128]{1,0:T(2,128)S(1)}, f32[2,128]{1,0:T(2,128)S(1)}, u32[]{:S(2)}, u32[]{:S(2)}) collective-permute-start(f32[2,128]{1,0:T(2,128)S(1)} %pad_maximum_fusion), channel_id=1, source_target_pairs={{0,24},{4,28},{8,16},{12,20},{16,8},{20,12},{24,0},{28,4},{1,25},{... | collective-permute-start | bytes 3080 | tf_op jit(solution)/shard_map/ppermute | solution.py:586
  9.9 0.2 collective-permute-start.4
  10.1 1.2 %collective-permute-start.3 = (f32[2,128]{1,0:T(2,128)S(1)}, f32[2,128]{1,0:T(2,128)S(1)}, u32[]{:S(2)}, u32[]{:S(2)}) collective-permute-start(f32[2,128]{1,0:T(2,128)S(1)} %pad_maximum_fusion), channel_id=1, source_target_pairs={{0,8},{4,12},{8,0},{12,4},{16,24},{20,28},{24,16},{28,20},{1,9},{5... | collective-permute-start | bytes 3080 | tf_op jit(solution)/shard_map/ppermute | solution.py:586
  11.4 0.7 collective-permute-done.5
  12.0 0.7 %collective-permute-done.4 = f32[2,128]{1,0:T(2,128)S(1)} collective-permute-done((f32[2,128]{1,0:T(2,128)S(1)}, f32[2,128]{1,0:T(2,128)S(1)}, u32[]{:S(2)}, u32[]{:S(2)}) %collective-permute-start.4) | collective-permute-done | bytes 1056 | tf_op jit(solution)/shard_map/ppermute | solution.py:586
  12.7 0.2 collective-permute-done.3
  13.0 2.9 %pack.3 = (f32[4,4,32,640]{3,2,1,0:T(8,128)S(1)}, f32[49,32,128]{2,1,0:T(8,128)}, f32[49,32,128]{2,1,0:T(8,128)}) custom-call(f32[32,4,4,1024]{3,2,1,0:T(4,128)} %raw.2), custom_call_target="tpu_custom_call" | custom-call | flops 1048576 | bytes 1048576 | tf_op jit(solution)/shard_map/pack/pallas_call | solution.py:561
  15.9 0.1 collective-permute-start.8
  16.0 3.6 %collective-permute-start.9 = (f32[49,32,128]{2,1,0:T(8,128)}, f32[49,32,128]{2,1,0:T(8,128)}, u32[]{:S(2)}, u32[]{:S(2)}) collective-permute-start(f32[49,32,128]{2,1,0:T(8,128)} %get-tuple-element.50), channel_id=1, source_target_pairs={{1,2},{2,1},{5,6},{6,5},{9,10},{10,9},{13,14},{14,13},{17,18},{18,... | collective-permute-start | bytes 2408456 | tf_op jit(solution)/shard_map/ppermute | solution.py:593
  19.7 0.1 fusion.5
  19.8 0.1 reshape.32.table_in
  19.8 0.6 places.1.table
  20.4 1.6 %collective-permute-done.6.first_in = f32[49,32,128]{2,1,0:T(8,128)} collective-permute-done((f32[49,32,128]{2,1,0:T(8,128)}, f32[49,32,128]{2,1,0:T(8,128)}, u32[]{:S(2)}, u32[]{:S(2)}) %collective-permute-start.6) | collective-permute-done | bytes 802848 | tf_op jit(solution)/shard_map/ppermute | solution.py:593
  22.1 2.9 %collective-permute-done.7.second_in = f32[49,32,128]{2,1,0:T(8,128)} collective-permute-done((f32[49,32,128]{2,1,0:T(8,128)}, f32[49,32,128]{2,1,0:T(8,128)}, u32[]{:S(2)}, u32[]{:S(2)}) %collective-permute-start.7) | collective-permute-done | bytes 802848 | tf_op jit(solution)/shard_map/ppermute | solution.py:593
  24.9 5.7 %forecast.2 = (f32[64,32,128]{2,1,0:T(8,128)S(1)}, f32[32,128]{1,0:T(8,128)S(1)}, f32[568,128]{1,0:T(8,128)S(1)}, f32[568,128]{1,0:T(8,128)S(1)}) custom-call(s32[256]{0:T(256)S(4)} %places.1.table, f32[4,4,32,640]{3,2,1,0:T(8,128)S(1)} %get-tuple-element.43.state, f32[49,32,128]{2,1,0:T(8,128)} %collective-permute-done.6.first_in, ...), custom_call_target="tpu_custom_call" | custom-call | flops 1024 | bytes 1024 | tf_op jit(solution)/shard_map/forecast/pallas_call | solution.py:615
  30.6 0.0 copy-start
  30.6 1.0 %copy-done = f32[64,32,128]{2,1,0:T(8,128)} copy-done((f32[64,32,128]{2,1,0:T(8,128)}, f32[64,32,128]{2,1,0:T(8,128)S(1)}, u32[]{:S(2)}) %copy-start) | copy-done | bytes 1048600
  31.6 10.6 %conditional.1 = (f32[568,128]{1,0:T(8,128)S(1)}) conditional(s32[]{:T(128)} %bitcast.3, f32[568,128]{1,0:T(8,128)S(1)} %get-tuple-element.46, (f32[568,128]{1,0:T(8,128)S(1)}, f32[568,128]{1,0:T(8,128)S(1)}) %tuple.16), branch_computations={%region_0.1_spmd, %region_1.2_spmd} | conditional | flops 145408 | bytes 4071512 | solution.py:631
  31.6 3.3 %collective-permute-start = (f32[568,128]{1,0:T(8,128)S(1)}, f32[568,128]{1,0:T(8,128)S(1)}, u32[]{:S(2)}, u32[]{:S(2)}) collective-permute-start(f32[568,128]{1,0:T(8,128)S(1)} %get-tuple-element.14), channel_id=1, source_target_pairs={{0,4},{4,0},{8,12},{12,8},{16,20},{20,16},{24,28},{28,24},{1,5},{5... | collective-permute-start | bytes 872456 | tf_op jit(solution)/shard_map/cond/branch_1_fun/ppermute | solution.py:522
  34.9 1.2 %collective-permute-done = f32[568,128]{1,0:T(8,128)S(1)} collective-permute-done((f32[568,128]{1,0:T(8,128)S(1)}, f32[568,128]{1,0:T(8,128)S(1)}, u32[]{:S(2)}, u32[]{:S(2)}) %collective-permute-start) | collective-permute-done | bytes 290848 | tf_op jit(solution)/shard_map/cond/branch_1_fun/ppermute | solution.py:522
  36.2 1.3 %collective-permute-start.1 = (f32[568,128]{1,0:T(8,128)S(1)}, f32[568,128]{1,0:T(8,128)S(1)}, u32[]{:S(2)}, u32[]{:S(2)}) collective-permute-start(f32[568,128]{1,0:T(8,128)S(1)} %add.49), channel_id=1, source_target_pairs={{0,8},{4,20},{8,0},{12,28},{16,24},{20,4},{24,16},{28,12},{1,9},{5... | collective-permute-start | bytes 872456 | tf_op jit(solution)/shard_map/cond/branch_1_fun/ppermute | solution.py:532
  37.5 4.7 %collective-permute-done.1 = f32[568,128]{1,0:T(8,128)S(1)} collective-permute-done((f32[568,128]{1,0:T(8,128)S(1)}, f32[568,128]{1,0:T(8,128)S(1)}, u32[]{:S(2)}, u32[]{:S(2)}) %collective-permute-start.1) | collective-permute-done | bytes 290848 | tf_op jit(solution)/shard_map/cond/branch_1_fun/ppermute | solution.py:532
  42.2 0.3 collective-permute-start.10
  42.5 0.0 collective-permute-done.8.first_in
  42.5 0.0 collective-permute-done.9.second_in
  42.5 5.7 %forecast.3 = (f32[64,32,128]{2,1,0:T(8,128)S(1)}, f32[32,128]{1,0:T(8,128)S(1)}, f32[568,128]{1,0:T(8,128)S(1)}, f32[568,128]{1,0:T(8,128)S(1)}) custom-call(s32[256]{0:T(256)S(4)} %places.1.table, f32[4,4,32,640]{3,2,1,0:T(8,128)S(1)} %get-tuple-element.48.state, f32[49,32,128]{2,1,0:T(8,128)} %collective-permute-done.8.first_in, ...), custom_call_target="tpu_custom_call" | custom-call | flops 1024 | bytes 25165824 | tf_op jit(solution)/shard_map/forecast/pallas_call | solution.py:615
  48.2 0.0 copy-start.1
  48.3 0.0 collective-permute-done.10
  48.3 2.5 %collective-permute-start.11 = (f32[568,128]{1,0:T(8,128)S(1)}, f32[568,128]{1,0:T(8,128)S(1)}, u32[]{:S(2)}, u32[]{:S(2)}) collective-permute-start(f32[568,128]{1,0:T(8,128)S(1)} %get-tuple-element.55), channel_id=1, source_target_pairs={{0,4},{4,0},{8,12},{12,8},{16,20},{20,16},{24,28},{28,24},{1,5},{5... | collective-permute-start | bytes 872456 | tf_op jit(solution)/shard_map/ppermute | solution.py:522
  50.8 1.2 %collective-permute-done.11 = f32[568,128]{1,0:T(8,128)S(1)} collective-permute-done((f32[568,128]{1,0:T(8,128)S(1)}, f32[568,128]{1,0:T(8,128)S(1)}, u32[]{:S(2)}, u32[]{:S(2)}) %collective-permute-start.11) | collective-permute-done | bytes 290848 | tf_op jit(solution)/shard_map/ppermute | solution.py:522
  52.0 0.7 %collective-permute-start.12 = (f32[568,128]{1,0:T(8,128)S(1)}, f32[568,128]{1,0:T(8,128)S(1)}, u32[]{:S(2)}, u32[]{:S(2)}) collective-permute-start(f32[568,128]{1,0:T(8,128)S(1)} %add.78), channel_id=1, source_target_pairs={{0,8},{4,20},{8,0},{12,28},{16,24},{20,4},{24,16},{28,12},{1,9},{5... | collective-permute-start | bytes 872456 | tf_op jit(solution)/shard_map/ppermute | solution.py:532
  52.7 0.3 collective-permute-start.13
  53.0 4.9 %collective-permute-done.12 = f32[568,128]{1,0:T(8,128)S(1)} collective-permute-done((f32[568,128]{1,0:T(8,128)S(1)}, f32[568,128]{1,0:T(8,128)S(1)}, u32[]{:S(2)}, u32[]{:S(2)}) %collective-permute-start.12) | collective-permute-done | bytes 290848 | tf_op jit(solution)/shard_map/ppermute | solution.py:532
  57.9 0.3 collective-permute-start.14
  58.2 1.9 %solve.2 = (f32[4,32,128]{2,1,0:T(8,128)S(1)}, f32[4,16,128]{2,1,0:T(8,128)S(1)}, f32[4,8,128]{2,1,0:T(8,128)S(1)}) custom-call(f32[8,128]{1,0:T(8,128)S(1)} %concatenate.8.obs, f32[32,128]{1,0:T(8,128)S(1)} %get-tuple-element.57.seen, f32[568,128]{1,0:T(8,128)S(1)} %add.77.own), custom_call_target="tpu_custom_call" | custom-call | flops 1024 | bytes 6291456 | tf_op jit(solution)/shard_map/solve/pallas_call | solution.py:661
  60.1 0.0 collective-permute-done.13.other
  60.1 0.0 copy-done.1
  60.1 1.6 %finish.2.rest_0_ = f32[32,4,4,1024]{3,2,1,0:T(4,128)} custom-call(f32[64,32,128]{2,1,0:T(8,128)S(1)} %copy-done.1, f32[4,32,128]{2,1,0:T(8,128)S(1)} %get-tuple-element.58.factors, f32[4,16,128]{2,1,0:T(8,128)S(1)} %get-tuple-element.59.centres, f32[4,8,128]{2,1,0:T(8,128)S(1)} %get-tuple-element.60.keeps, f32[568,128]{1,0:T(8,128)S(1)} %add.77.own, ...), custom_call_target="tpu_custom_call" | custom-call | flops 1024 | bytes 16777216 | tf_op jit(solution)/shard_map/finish/pallas_call | solution.py:673
  61.8 2.1 %collective-permute-done.14 = f32[568,128]{1,0:T(8,128)S(1)} collective-permute-done((f32[568,128]{1,0:T(8,128)S(1)}, f32[568,128]{1,0:T(8,128)S(1)}, u32[]{:S(2)}, u32[]{:S(2)}) %collective-permute-start.14) | collective-permute-done | bytes 290848 | tf_op jit(solution)/shard_map/ppermute | solution.py:532
  63.9 2.1 %collective-permute-start.15 = (f32[568,128]{1,0:T(8,128)S(1)}, f32[568,128]{1,0:T(8,128)S(1)}, u32[]{:S(2)}, u32[]{:S(2)}) collective-permute-start(f32[568,128]{1,0:T(8,128)S(1)} %add.80.own), channel_id=1, source_target_pairs={{0,4},{4,0},{8,12},{12,8},{16,20},{20,16},{24,28},{28,24},{1,5},{5... | collective-permute-start | bytes 872456 | tf_op jit(solution)/shard_map/ppermute | solution.py:540
  66.0 1.9 %solve.3 = (f32[4,32,128]{2,1,0:T(8,128)S(1)}, f32[4,16,128]{2,1,0:T(8,128)S(1)}, f32[4,8,128]{2,1,0:T(8,128)S(1)}) custom-call(f32[8,128]{1,0:T(8,128)S(1)} %concatenate.8.obs, f32[32,128]{1,0:T(8,128)S(1)} %get-tuple-element.52.seen, f32[568,128]{1,0:T(8,128)S(1)} %add.80.own), custom_call_target="tpu_custom_call" | custom-call | flops 1024 | bytes 6291456 | tf_op jit(solution)/shard_map/solve/pallas_call | solution.py:661
  67.9 0.0 collective-permute-done.15.other
  67.9 1.6 %finish.3 = f32[32,4,4,1024]{3,2,1,0:T(4,128)} custom-call(f32[64,32,128]{2,1,0:T(8,128)S(1)} %get-tuple-element.51.ahead, f32[4,32,128]{2,1,0:T(8,128)S(1)} %get-tuple-element.62.factors, f32[4,16,128]{2,1,0:T(8,128)S(1)} %get-tuple-element.63.centres, f32[4,8,128]{2,1,0:T(8,128)S(1)} %get-tuple-element.64.keeps, ...), custom_call_target="tpu_custom_call", output_to_operand_aliasing={{}: (6, {})} | custom-call | flops 1024 | bytes 16777216 | tf_op jit(solution)/shard_map/finish/pallas_call | solution.py:673
  (11 shorter events, 0.3 us)
Async XLA Ops:
  2.9 19.1 %collective-permute-start.6 = (f32[49,32,128]{2,1,0:T(8,128)}, f32[49,32,128]{2,1,0:T(8,128)}, u32[]{:S(2)}, u32[]{:S(2)}) collective-permute-start(f32[49,32,128]{2,1,0:T(8,128)} %get-tuple-element.44), channel_id=1, source_target_pairs={{0,1},{1,0},{2,3},{3,2},{4,5},{5,4},{6,7},{7,6},{8,9},{9,8},{10,11... | collective-permute-start | bytes 2408456 | tf_op jit(solution)/shard_map/ppermute | solution.py:593
  4.3 20.6 %collective-permute-start.7 = (f32[49,32,128]{2,1,0:T(8,128)}, f32[49,32,128]{2,1,0:T(8,128)}, u32[]{:S(2)}, u32[]{:S(2)}) collective-permute-start(f32[49,32,128]{2,1,0:T(8,128)} %get-tuple-element.45), channel_id=1, source_target_pairs={{1,2},{2,1},{5,6},{6,5},{9,10},{10,9},{13,14},{14,13},{17,18},{18,... | collective-permute-start | bytes 2408456 | tf_op jit(solution)/shard_map/ppermute | solution.py:593
  6.9 1.8 %collective-permute-start.2 = (f32[1,128]{1,0:T(1,128)S(1)}, f32[1,128]{1,0:T(1,128)S(1)}, u32[]{:S(2)}, u32[]{:S(2)}) collective-permute-start(f32[1,128]{1,0:T(1,128)S(1)} %compare_select_fusion.1), channel_id=1, source_target_pairs={{0,4},{4,0},{8,12},{12,8},{16,20},{20,16},{24,28},{28,24},{1,5},{5... | collective-permute-start | bytes 1544 | tf_op jit(solution)/shard_map/ppermute | solution.py:586
  8.7 3.3 %collective-permute-start.5 = (f32[2,128]{1,0:T(2,128)S(1)}, f32[2,128]{1,0:T(2,128)S(1)}, u32[]{:S(2)}, u32[]{:S(2)}) collective-permute-start(f32[2,128]{1,0:T(2,128)S(1)} %pad_maximum_fusion), channel_id=1, source_target_pairs={{0,24},{4,28},{8,16},{12,20},{16,8},{20,12},{24,0},{28,4},{1,25},{... | collective-permute-start | bytes 3080 | tf_op jit(solution)/shard_map/ppermute | solution.py:586
  9.9 2.8 %collective-permute-start.4 = (f32[2,128]{1,0:T(2,128)S(1)}, f32[2,128]{1,0:T(2,128)S(1)}, u32[]{:S(2)}, u32[]{:S(2)}) collective-permute-start(f32[2,128]{1,0:T(2,128)S(1)} %pad_maximum_fusion), channel_id=1, source_target_pairs={{0,16},{4,20},{8,24},{12,28},{16,0},{20,4},{24,8},{28,12},{1,17},{... | collective-permute-start | bytes 3080 | tf_op jit(solution)/shard_map/ppermute | solution.py:586
  10.1 2.8 %collective-permute-start.3 = (f32[2,128]{1,0:T(2,128)S(1)}, f32[2,128]{1,0:T(2,128)S(1)}, u32[]{:S(2)}, u32[]{:S(2)}) collective-permute-start(f32[2,128]{1,0:T(2,128)S(1)} %pad_maximum_fusion), channel_id=1, source_target_pairs={{0,8},{4,12},{8,0},{12,4},{16,24},{20,28},{24,16},{28,20},{1,9},{5... | collective-permute-start | bytes 3080 | tf_op jit(solution)/shard_map/ppermute | solution.py:586
  15.9 26.6 %collective-permute-start.8 = (f32[49,32,128]{2,1,0:T(8,128)}, f32[49,32,128]{2,1,0:T(8,128)}, u32[]{:S(2)}, u32[]{:S(2)}) collective-permute-start(f32[49,32,128]{2,1,0:T(8,128)} %get-tuple-element.49), channel_id=1, source_target_pairs={{0,1},{1,0},{2,3},{3,2},{4,5},{5,4},{6,7},{7,6},{8,9},{9,8},{10,11... | collective-permute-start | bytes 2408456 | tf_op jit(solution)/shard_map/ppermute | solution.py:593
  16.0 26.5 %collective-permute-start.9 = (f32[49,32,128]{2,1,0:T(8,128)}, f32[49,32,128]{2,1,0:T(8,128)}, u32[]{:S(2)}, u32[]{:S(2)}) collective-permute-start(f32[49,32,128]{2,1,0:T(8,128)} %get-tuple-element.50), channel_id=1, source_target_pairs={{1,2},{2,1},{5,6},{6,5},{9,10},{10,9},{13,14},{14,13},{17,18},{18,... | collective-permute-start | bytes 2408456 | tf_op jit(solution)/shard_map/ppermute | solution.py:593
  30.6 1.0 %copy-start = (f32[64,32,128]{2,1,0:T(8,128)}, f32[64,32,128]{2,1,0:T(8,128)S(1)}, u32[]{:S(2)}) copy-start(f32[64,32,128]{2,1,0:T(8,128)S(1)} %get-tuple-element.56.ahead) | copy-start | bytes 3145732
  31.6 4.5 %collective-permute-start = (f32[568,128]{1,0:T(8,128)S(1)}, f32[568,128]{1,0:T(8,128)S(1)}, u32[]{:S(2)}, u32[]{:S(2)}) collective-permute-start(f32[568,128]{1,0:T(8,128)S(1)} %get-tuple-element.14), channel_id=1, source_target_pairs={{0,4},{4,0},{8,12},{12,8},{16,20},{20,16},{24,28},{28,24},{1,5},{5... | collective-permute-start | bytes 872456 | tf_op jit(solution)/shard_map/cond/branch_1_fun/ppermute | solution.py:522
  36.2 6.0 %collective-permute-start.1 = (f32[568,128]{1,0:T(8,128)S(1)}, f32[568,128]{1,0:T(8,128)S(1)}, u32[]{:S(2)}, u32[]{:S(2)}) collective-permute-start(f32[568,128]{1,0:T(8,128)S(1)} %add.49), channel_id=1, source_target_pairs={{0,8},{4,20},{8,0},{12,28},{16,24},{20,4},{24,16},{28,12},{1,9},{5... | collective-permute-start | bytes 872456 | tf_op jit(solution)/shard_map/cond/branch_1_fun/ppermute | solution.py:532
  42.2 6.1 %collective-permute-start.10 = (f32[568,128]{1,0:T(8,128)S(1)}, f32[568,128]{1,0:T(8,128)S(1)}, u32[]{:S(2)}, u32[]{:S(2)}) collective-permute-start(f32[568,128]{1,0:T(8,128)S(1)} %get-tuple-element.69), channel_id=1, source_target_pairs={{0,16},{4,12},{8,24},{12,4},{16,0},{20,28},{24,8},{28,20},{1,17},{... | collective-permute-start | bytes 872456 | tf_op jit(solution)/shard_map/ppermute | solution.py:532
  48.2 11.9 %copy-start.1 = (f32[64,32,128]{2,1,0:T(8,128)S(1)}, f32[64,32,128]{2,1,0:T(8,128)}, u32[]{:S(2)}) copy-start(f32[64,32,128]{2,1,0:T(8,128)} %copy-done) | copy-start | bytes 3145732
  48.3 3.7 %collective-permute-start.11 = (f32[568,128]{1,0:T(8,128)S(1)}, f32[568,128]{1,0:T(8,128)S(1)}, u32[]{:S(2)}, u32[]{:S(2)}) collective-permute-start(f32[568,128]{1,0:T(8,128)S(1)} %get-tuple-element.55), channel_id=1, source_target_pairs={{0,4},{4,0},{8,12},{12,8},{16,20},{20,16},{24,28},{28,24},{1,5},{5... | collective-permute-start | bytes 872456 | tf_op jit(solution)/shard_map/ppermute | solution.py:522
  52.0 5.9 %collective-permute-start.12 = (f32[568,128]{1,0:T(8,128)S(1)}, f32[568,128]{1,0:T(8,128)S(1)}, u32[]{:S(2)}, u32[]{:S(2)}) collective-permute-start(f32[568,128]{1,0:T(8,128)S(1)} %add.78), channel_id=1, source_target_pairs={{0,8},{4,20},{8,0},{12,28},{16,24},{20,4},{24,16},{28,12},{1,9},{5... | collective-permute-start | bytes 872456 | tf_op jit(solution)/shard_map/ppermute | solution.py:532
  52.7 7.4 %collective-permute-start.13 = (f32[568,128]{1,0:T(8,128)S(1)}, f32[568,128]{1,0:T(8,128)S(1)}, u32[]{:S(2)}, u32[]{:S(2)}) collective-permute-start(f32[568,128]{1,0:T(8,128)S(1)} %add.77.own), channel_id=1, source_target_pairs={{0,4},{4,0},{8,12},{12,8},{16,20},{20,16},{24,28},{28,24},{1,5},{5... | collective-permute-start | bytes 872456 | tf_op jit(solution)/shard_map/ppermute | solution.py:540
  57.9 5.9 %collective-permute-start.14 = (f32[568,128]{1,0:T(8,128)S(1)}, f32[568,128]{1,0:T(8,128)S(1)}, u32[]{:S(2)}, u32[]{:S(2)}) collective-permute-start(f32[568,128]{1,0:T(8,128)S(1)} %add.79), channel_id=1, source_target_pairs={{0,16},{4,12},{8,24},{12,4},{16,0},{20,28},{24,8},{28,20},{1,17},{... | collective-permute-start | bytes 872456 | tf_op jit(solution)/shard_map/ppermute | solution.py:532
  63.9 4.0 %collective-permute-start.15 = (f32[568,128]{1,0:T(8,128)S(1)}, f32[568,128]{1,0:T(8,128)S(1)}, u32[]{:S(2)}, u32[]{:S(2)}) collective-permute-start(f32[568,128]{1,0:T(8,128)S(1)} %add.80.own), channel_id=1, source_target_pairs={{0,4},{4,0},{8,12},{12,8},{16,20},{20,16},{24,28},{28,24},{1,5},{5... | collective-permute-start | bytes 872456 | tf_op jit(solution)/shard_map/ppermute | solution.py:540

commit v6 on v5

--- a/solution.py
+++ b/solution.py
@@ -249,8 +249,16 @@
     copy_in.wait()
 
 
-def forecast_kernel(plan, table, state, first_in, second_in, ahead, seen, keep, send, s0, s1, s2, low, high, sems):
+def forecast_kernel(plan, table, state, first_in, second_in, ahead, seen, keep, send, s0, s1, s2, low, high, sems, *rest):
     p = plan
+    ahead_out = ahead
+    if rest:
+        ahead = rest[0]
+
+    def ahead_copy(kk):
+        part = pl.ds(kk * SUB, SUB)
+        return pltpu.make_async_copy(ahead.at[:, part, :], ahead_out.at[:, part, :], rest[1].at[kk])
+
     full = p.rows + 2 * HALO
     band = lax.axis_index("lat")
     me = lax.axis_index("mem")
@@ -327,6 +335,8 @@
         step_once(p, full, load0, store1, False, 1.0)
         step_once(p, full - 2, lambda row, f, t: s1[row + 1, f, t], store2, False, 0.25)
         step_once(p, full - 4, lambda row, f, t: s2[row + 2, f, t], store3, True, two_thirds)
+        if rest:
+            ahead_copy(kk).start()
         return carry
 
     lax.fori_loop(0, parts, body, 0)
@@ -379,6 +389,9 @@
                 out[pl.ds(base + p.hrf * p.slots + i, 1), :] = piece[p.slots : p.slots + 1]
             for i in range(p.hrf, p.plain):
                 out[pl.ds(base + p.hrf * p.slots + i, 1), :] = jnp.zeros((1, LANES), jnp.float32)
+    if rest:
+        for kk in range(parts):
+            ahead_copy(kk).wait()
 
 
 def solve_kernel(plan, obs, seen, own, factors, centres, keeps):
@@ -615,7 +628,7 @@
         ahead, seen, keep, send = call(
             functools.partial(forecast_kernel, h),
             [
-                shape((h.nt * p.rows * p.fields, p.members, LANES), f32),
+                (shape if c == len(chunks) - 1 else pltpu.HBM)((h.nt * p.rows * p.fields, p.members, LANES), f32),
                 shape((p.members, LANES), f32),
                 shape((h.total_rows, LANES), f32),
                 shape((h.total_rows, LANES), f32),
@@ -623,17 +636,25 @@
             [SMEM, VMEM, ANY, ANY],
             [pltpu.VMEM((2 * HALO, p.fields, SUB, LANES), f32), pltpu.VMEM(stage, f32), pltpu.VMEM(stage, f32)]
             + [pltpu.VMEM((h.message, p.members, LANES), f32)] * 2
-            + [pltpu.SemaphoreType.DMA((p.members // SUB, 2))],
+            + [pltpu.SemaphoreType.DMA((p.members // SUB, 2))]
+            + (
+                []
+                if c == len(chunks) - 1
+                else [
+                    pltpu.VMEM((h.nt * p.rows * p.fields, p.members, LANES), f32),
+                    pltpu.SemaphoreType.DMA((p.members // SUB,)),
+                ]
+            ),
+            out_specs=[VMEM if c == len(chunks) - 1 else HBM] + [VMEM] * 3,
             cost=(1024, h.nt * (6 << 20) if c else 1024),
             name="forecast",
-        )(table, near(packed[c][0] if early is None else after(packed[c][0], early)), *map(far, halo[c]))
+        )(table, near(packed[c][0] if early is None else after(packed[c][0], early)), *halo[c])
         if c == 0:
             early = lax.cond(
                 obs_count[0, 0] >= 0,
-                lambda keep, send: sum_phase(p, 0, core_sums(p, keep, send)),
-                lambda keep, send: keep,
-                keep,
-                send,
+                functools.partial(sum_phase, p, 0),
+                lambda total: total,
+                core_sums(p, keep, send),
             )
             parts.append((ahead, seen, early))
         else:

time: 69.8 us -> 69.1 us (0.990)
  local copies, waits for them, and re-layouts: 1.07 us -> 0.11 us
    unnamed x4 -> x2, local copies, waits for them, and re-layouts: 0.97 us -> 0.01 us
  transfers between devices with their start and end apart: 16 -> 16, of which waited for: 11 -> 12; matrix products, arithmetic and copies ran while one was open for 0% -> 1% of each run, Pallas kernels for 29% -> 29%
where the time goes in v6:
time: 69.1 us; the launch traced here: 68.8 us
  Pallas kernels  24.7 us (36%)
  starting transfers between devices  21.4 us (31%)
  waiting for transfers between devices  21.2 us (31%)
  between operations  0.83 us (1%)
    ppermute x4, waiting for transfers between devices, sum_phase(): lax.ppermute(total, 'mem', [(i, i ^ (odd if i & 1 else even)) for i in ra...  11.4 us
    pallas_call x2, Pallas kernels, per_device(): call(functools.partial(forecast_kernel, h), [(shape if c == len(chunks) -...  11.4 us
    ppermute x4, starting transfers between devices, per_device(): lax.ppermute(messages[2 * c + i], 'lat', swaps[i])  7.01 us
    pallas_call x2, Pallas kernels, pack(): call(functools.partial(pack_kernel, h), [pltpu.VMEM((p.rows, p.fields, p....  5.8 us
    ppermute x2, starting transfers between devices, core_sums(): lax.ppermute(send, 'mem', [(i, i ^ 1) for i in range(plan.groups)])  5.43 us
    ppermute x4, waiting for transfers between devices, per_device(): lax.ppermute(messages[2 * c + i], 'lat', swaps[i])  4.95 us
    pallas_call x2, Pallas kernels, finish(): call(functools.partial(solve_kernel, h), [pltpu.VMEM((h.np, p.members, LA...  3.74 us
    ppermute x4, starting transfers between devices, per_device(): lax.ppermute(obs, 'mem', [(i, i ^ bit * b) for i in range(groups)])  3.67 us
  transfers between devices with their start and end apart: 16, of which 12 were waited for; matrix products, arithmetic and copies ran while one was open for 1% of the time, Pallas kernels for 29%

profile of v6, /device:TPU:19, one launch (start us, length us, event | category | flops | bytes accessed | tf_op | source)
XLA Modules:
  0.0 68.8 jit_solution(16465720741755150521)
XLA Ops:
  0.0 2.9 %pack.2 = (f32[4,4,32,640]{3,2,1,0:T(8,128)S(1)}, f32[49,32,128]{2,1,0:T(8,128)}, f32[49,32,128]{2,1,0:T(8,128)}, f32[1,128]{1,0:T(1,128)S(1)}) custom-call(f32[32,4,4,1024]{3,2,1,0:T(4,128)} %raw.2, f32[1,1,16]{2,1,0:T(1,128)} %rest_0_.1, f32[1,1,16]{2,1,0:T(1,128)} %rest_1_.1, s32[1,1,16]{2,1,0:T(1,128)} %rest_2_.1, s32[1,1,16]{2,1,0:T(1,128)} %rest_3_.1), custom_call_target="tpu_custom_call" | custom-call | flops 1048576 | bytes 1048576 | tf_op jit(solution)/shard_map/pack/pallas_call | solution.py:574
  2.9 1.4 %collective-permute-start.5 = (f32[49,32,128]{2,1,0:T(8,128)}, f32[49,32,128]{2,1,0:T(8,128)S(1)}, u32[]{:S(2)}, u32[]{:S(2)}) collective-permute-start(f32[49,32,128]{2,1,0:T(8,128)} %get-tuple-element.39), channel_id=1, source_target_pairs={{0,1},{1,0},{2,3},{3,2},{4,5},{5,4},{6,7},{7,6},{8,9},{9,8},{10,11... | collective-permute-start | bytes 2408456 | tf_op jit(solution)/shard_map/ppermute | solution.py:606
  4.3 1.9 %collective-permute-start.6 = (f32[49,32,128]{2,1,0:T(8,128)}, f32[49,32,128]{2,1,0:T(8,128)}, u32[]{:S(2)}, u32[]{:S(2)}) collective-permute-start(f32[49,32,128]{2,1,0:T(8,128)} %get-tuple-element.40), channel_id=1, source_target_pairs={{1,2},{2,1},{5,6},{6,5},{9,10},{10,9},{13,14},{14,13},{17,18},{18,... | collective-permute-start | bytes 2408456 | tf_op jit(solution)/shard_map/ppermute | solution.py:606
  6.9 1.0 %collective-permute-start.1 = (f32[1,128]{1,0:T(1,128)S(1)}, f32[1,128]{1,0:T(1,128)S(1)}, u32[]{:S(2)}, u32[]{:S(2)}) collective-permute-start(f32[1,128]{1,0:T(1,128)S(1)} %compare_select_fusion.1), channel_id=1, source_target_pairs={{0,4},{4,0},{8,12},{12,8},{16,20},{20,16},{24,28},{28,24},{1,5},{5... | collective-permute-start | bytes 1544 | tf_op jit(solution)/shard_map/ppermute | solution.py:599
  7.9 0.8 %collective-permute-done.1 = f32[1,128]{1,0:T(1,128)S(1)} collective-permute-done((f32[1,128]{1,0:T(1,128)S(1)}, f32[1,128]{1,0:T(1,128)S(1)}, u32[]{:S(2)}, u32[]{:S(2)}) %collective-permute-start.1) | collective-permute-done | bytes 544 | tf_op jit(solution)/shard_map/ppermute | solution.py:599
  8.7 1.2 %collective-permute-start.4 = (f32[2,128]{1,0:T(2,128)S(1)}, f32[2,128]{1,0:T(2,128)S(1)}, u32[]{:S(2)}, u32[]{:S(2)}) collective-permute-start(f32[2,128]{1,0:T(2,128)S(1)} %pad_maximum_fusion), channel_id=1, source_target_pairs={{0,24},{4,28},{8,16},{12,20},{16,8},{20,12},{24,0},{28,4},{1,25},{... | collective-permute-start | bytes 3080 | tf_op jit(solution)/shard_map/ppermute | solution.py:599
  9.9 0.2 collective-permute-start.3
  10.1 1.2 %collective-permute-start.2 = (f32[2,128]{1,0:T(2,128)S(1)}, f32[2,128]{1,0:T(2,128)S(1)}, u32[]{:S(2)}, u32[]{:S(2)}) collective-permute-start(f32[2,128]{1,0:T(2,128)S(1)} %pad_maximum_fusion), channel_id=1, source_target_pairs={{0,8},{4,12},{8,0},{12,4},{16,24},{20,28},{24,16},{28,20},{1,9},{5... | collective-permute-start | bytes 3080 | tf_op jit(solution)/shard_map/ppermute | solution.py:599
  11.4 0.7 collective-permute-done.4
  12.0 0.7 %collective-permute-done.3 = f32[2,128]{1,0:T(2,128)S(1)} collective-permute-done((f32[2,128]{1,0:T(2,128)S(1)}, f32[2,128]{1,0:T(2,128)S(1)}, u32[]{:S(2)}, u32[]{:S(2)}) %collective-permute-start.3) | collective-permute-done | bytes 1056 | tf_op jit(solution)/shard_map/ppermute | solution.py:599
  12.7 0.2 collective-permute-done.2
  13.0 2.9 %pack.3 = (f32[4,4,32,640]{3,2,1,0:T(8,128)S(1)}, f32[49,32,128]{2,1,0:T(8,128)}, f32[49,32,128]{2,1,0:T(8,128)}) custom-call(f32[32,4,4,1024]{3,2,1,0:T(4,128)} %raw.2), custom_call_target="tpu_custom_call" | custom-call | flops 1048576 | bytes 1048576 | tf_op jit(solution)/shard_map/pack/pallas_call | solution.py:574
  15.9 0.1 collective-permute-start.8
  16.0 3.7 %collective-permute-start.9 = (f32[49,32,128]{2,1,0:T(8,128)}, f32[49,32,128]{2,1,0:T(8,128)}, u32[]{:S(2)}, u32[]{:S(2)}) collective-permute-start(f32[49,32,128]{2,1,0:T(8,128)} %get-tuple-element.45), channel_id=1, source_target_pairs={{1,2},{2,1},{5,6},{6,5},{9,10},{10,9},{13,14},{14,13},{17,18},{18,... | collective-permute-start | bytes 2408456 | tf_op jit(solution)/shard_map/ppermute | solution.py:606
  19.6 0.1 fusion.5
  19.8 0.1 reshape.32.table_in
  19.8 0.6 places.1.table
  20.4 1.7 %collective-permute-done.5.first_in = f32[49,32,128]{2,1,0:T(8,128)S(1)} collective-permute-done((f32[49,32,128]{2,1,0:T(8,128)}, f32[49,32,128]{2,1,0:T(8,128)S(1)}, u32[]{:S(2)}, u32[]{:S(2)}) %collective-permute-start.5) | collective-permute-done | bytes 802848 | tf_op jit(solution)/shard_map/ppermute | solution.py:606
  22.1 2.9 %collective-permute-done.6.second_in = f32[49,32,128]{2,1,0:T(8,128)} collective-permute-done((f32[49,32,128]{2,1,0:T(8,128)}, f32[49,32,128]{2,1,0:T(8,128)}, u32[]{:S(2)}, u32[]{:S(2)}) %collective-permute-start.6) | collective-permute-done | bytes 802848 | tf_op jit(solution)/shard_map/ppermute | solution.py:606
  24.9 5.7 %forecast.2 = (f32[64,32,128]{2,1,0:T(8,128)}, f32[32,128]{1,0:T(8,128)S(1)}, f32[568,128]{1,0:T(8,128)S(1)}, f32[568,128]{1,0:T(8,128)S(1)}) custom-call(s32[256]{0:T(256)S(4)} %places.1.table, f32[4,4,32,640]{3,2,1,0:T(8,128)S(1)} %get-tuple-element.38.state, f32[49,32,128]{2,1,0:T(8,128)S(1)} %collective-permute-done.5.first_in, ...), custom_call_target="tpu_custom_call" | custom-call | flops 1024 | bytes 1024 | tf_op jit(solution)/shard_map/forecast/pallas_call | solution.py:628
  30.6 3.4 %collective-permute-start.7 = (f32[568,128]{1,0:T(8,128)S(1)}, f32[568,128]{1,0:T(8,128)S(1)}, u32[]{:S(2)}, u32[]{:S(2)}) collective-permute-start(f32[568,128]{1,0:T(8,128)S(1)} %get-tuple-element.42), channel_id=1, source_target_pairs={{0,4},{4,0},{8,12},{12,8},{16,20},{20,16},{24,28},{28,24},{1,5},{5... | collective-permute-start | bytes 872456 | tf_op jit(solution)/shard_map/ppermute | solution.py:535
  34.0 1.2 %collective-permute-done.7 = f32[568,128]{1,0:T(8,128)S(1)} collective-permute-done((f32[568,128]{1,0:T(8,128)S(1)}, f32[568,128]{1,0:T(8,128)S(1)}, u32[]{:S(2)}, u32[]{:S(2)}) %collective-permute-start.7) | collective-permute-done | bytes 290848 | tf_op jit(solution)/shard_map/ppermute | solution.py:535
  35.2 0.1 add.83
  35.3 6.1 %conditional.1 = (f32[568,128]{1,0:T(8,128)S(1)}) conditional(s32[]{:T(128)} %bitcast.3, f32[568,128]{1,0:T(8,128)S(1)} %add.83, f32[568,128]{1,0:T(8,128)S(1)} %add.83), branch_computations={%region_0.1_spmd, %region_1.2_spmd} | conditional | flops 72704 | bytes 2035760 | solution.py:653
  35.3 1.3 %collective-permute-start = (f32[568,128]{1,0:T(8,128)S(1)}, f32[568,128]{1,0:T(8,128)S(1)}, u32[]{:S(2)}, u32[]{:S(2)}) collective-permute-start(f32[568,128]{1,0:T(8,128)S(1)} %param.1), channel_id=1, source_target_pairs={{0,8},{4,20},{8,0},{12,28},{16,24},{20,4},{24,16},{28,12},{1,9},{5... | collective-permute-start | bytes 872456 | tf_op jit(solution)/shard_map/cond/branch_1_fun/ppermute | solution.py:545
  36.6 4.7 %collective-permute-done = f32[568,128]{1,0:T(8,128)S(1)} collective-permute-done((f32[568,128]{1,0:T(8,128)S(1)}, f32[568,128]{1,0:T(8,128)S(1)}, u32[]{:S(2)}, u32[]{:S(2)}) %collective-permute-start) | collective-permute-done | bytes 290848 | tf_op jit(solution)/shard_map/cond/branch_1_fun/ppermute | solution.py:545
  41.3 0.1 add.55
  41.4 0.3 collective-permute-start.10
  41.7 0.0 collective-permute-done.8.first_in
  41.7 0.4 collective-permute-done.9.second_in
  42.1 5.7 %forecast.3 = (f32[64,32,128]{2,1,0:T(8,128)S(1)}, f32[32,128]{1,0:T(8,128)S(1)}, f32[568,128]{1,0:T(8,128)S(1)}, f32[568,128]{1,0:T(8,128)S(1)}) custom-call(s32[256]{0:T(256)S(4)} %places.1.table, f32[4,4,32,640]{3,2,1,0:T(8,128)S(1)} %get-tuple-element.43.state, f32[49,32,128]{2,1,0:T(8,128)} %collective-permute-done.8.first_in, ...), custom_call_target="tpu_custom_call" | custom-call | flops 1024 | bytes 25165824 | tf_op jit(solution)/shard_map/forecast/pallas_call | solution.py:628
  47.8 0.0 copy-start
  47.9 0.1 add.84.own
  47.9 2.0 %collective-permute-start.11 = (f32[568,128]{1,0:T(8,128)S(1)}, f32[568,128]{1,0:T(8,128)S(1)}, u32[]{:S(2)}, u32[]{:S(2)}) collective-permute-start(f32[568,128]{1,0:T(8,128)S(1)} %get-tuple-element.50), channel_id=1, source_target_pairs={{0,4},{4,0},{8,12},{12,8},{16,20},{20,16},{24,28},{28,24},{1,5},{5... | collective-permute-start | bytes 872456 | tf_op jit(solution)/shard_map/ppermute | solution.py:535
  50.0 1.2 %collective-permute-done.11 = f32[568,128]{1,0:T(8,128)S(1)} collective-permute-done((f32[568,128]{1,0:T(8,128)S(1)}, f32[568,128]{1,0:T(8,128)S(1)}, u32[]{:S(2)}, u32[]{:S(2)}) %collective-permute-start.11) | collective-permute-done | bytes 290848 | tf_op jit(solution)/shard_map/ppermute | solution.py:535
  51.2 0.1 add.85
  51.2 1.2 %collective-permute-start.12 = (f32[568,128]{1,0:T(8,128)S(1)}, f32[568,128]{1,0:T(8,128)S(1)}, u32[]{:S(2)}, u32[]{:S(2)}) collective-permute-start(f32[568,128]{1,0:T(8,128)S(1)} %add.85), channel_id=1, source_target_pairs={{0,8},{4,20},{8,0},{12,28},{16,24},{20,4},{24,16},{28,12},{1,9},{5... | collective-permute-start | bytes 872456 | tf_op jit(solution)/shard_map/ppermute | solution.py:545
  52.4 0.0 collective-permute-start.13
  52.4 4.7 %collective-permute-done.12 = f32[568,128]{1,0:T(8,128)S(1)} collective-permute-done((f32[568,128]{1,0:T(8,128)S(1)}, f32[568,128]{1,0:T(8,128)S(1)}, u32[]{:S(2)}, u32[]{:S(2)}) %collective-permute-start.12) | collective-permute-done | bytes 290848 | tf_op jit(solution)/shard_map/ppermute | solution.py:545
  57.1 0.1 add.86
  57.2 0.3 collective-permute-start.14
  57.5 1.9 %solve.2 = (f32[4,32,128]{2,1,0:T(8,128)S(1)}, f32[4,16,128]{2,1,0:T(8,128)S(1)}, f32[4,8,128]{2,1,0:T(8,128)S(1)}) custom-call(f32[8,128]{1,0:T(8,128)S(1)} %concatenate.8.obs, f32[32,128]{1,0:T(8,128)S(1)} %get-tuple-element.52.seen, f32[568,128]{1,0:T(8,128)S(1)} %add.84.own), custom_call_target="tpu_custom_call" | custom-call | flops 1024 | bytes 6291456 | tf_op jit(solution)/shard_map/solve/pallas_call | solution.py:682
  59.4 1.6 %finish.2.rest_0_ = f32[32,4,4,1024]{3,2,1,0:T(4,128)} custom-call(f32[64,32,128]{2,1,0:T(8,128)S(1)} %copy-done, f32[4,32,128]{2,1,0:T(8,128)S(1)} %get-tuple-element.53.factors, f32[4,16,128]{2,1,0:T(8,128)S(1)} %get-tuple-element.54.centres, f32[4,8,128]{2,1,0:T(8,128)S(1)} %get-tuple-element.55.keeps, f32[568,128]{1,0:T(8,128)S(1)} %add.84.own, ...), custom_call_target="tpu_custom_call" | custom-call | flops 1024 | bytes 16777216 | tf_op jit(solution)/shard_map/finish/pallas_call | solution.py:694
  61.0 2.1 %collective-permute-done.14 = f32[568,128]{1,0:T(8,128)S(1)} collective-permute-done((f32[568,128]{1,0:T(8,128)S(1)}, f32[568,128]{1,0:T(8,128)S(1)}, u32[]{:S(2)}, u32[]{:S(2)}) %collective-permute-start.14) | collective-permute-done | bytes 290848 | tf_op jit(solution)/shard_map/ppermute | solution.py:545
  63.1 0.1 add.87.own
  63.1 2.1 %collective-permute-start.15 = (f32[568,128]{1,0:T(8,128)S(1)}, f32[568,128]{1,0:T(8,128)S(1)}, u32[]{:S(2)}, u32[]{:S(2)}) collective-permute-start(f32[568,128]{1,0:T(8,128)S(1)} %add.87.own), channel_id=1, source_target_pairs={{0,4},{4,0},{8,12},{12,8},{16,20},{20,16},{24,28},{28,24},{1,5},{5... | collective-permute-start | bytes 872456 | tf_op jit(solution)/shard_map/ppermute | solution.py:553
  65.3 1.9 %solve.3 = (f32[4,32,128]{2,1,0:T(8,128)S(1)}, f32[4,16,128]{2,1,0:T(8,128)S(1)}, f32[4,8,128]{2,1,0:T(8,128)S(1)}) custom-call(f32[8,128]{1,0:T(8,128)S(1)} %concatenate.8.obs, f32[32,128]{1,0:T(8,128)S(1)} %get-tuple-element.47.seen, f32[568,128]{1,0:T(8,128)S(1)} %add.87.own), custom_call_target="tpu_custom_call" | custom-call | flops 1024 | bytes 6291456 | tf_op jit(solution)/shard_map/solve/pallas_call | solution.py:682
  67.2 1.6 %finish.3 = f32[32,4,4,1024]{3,2,1,0:T(4,128)} custom-call(f32[64,32,128]{2,1,0:T(8,128)S(1)} %get-tuple-element.46.ahead, f32[4,32,128]{2,1,0:T(8,128)S(1)} %get-tuple-element.57.factors, f32[4,16,128]{2,1,0:T(8,128)S(1)} %get-tuple-element.58.centres, f32[4,8,128]{2,1,0:T(8,128)S(1)} %get-tuple-element.59.keeps, ...), custom_call_target="tpu_custom_call", output_to_operand_aliasing={{}: (6, {})} | custom-call | flops 1024 | bytes 16777216 | tf_op jit(solution)/shard_map/finish/pallas_call | solution.py:694
  (9 shorter events, 0.1 us)
Async XLA Ops:
  2.9 19.1 %collective-permute-start.5 = (f32[49,32,128]{2,1,0:T(8,128)}, f32[49,32,128]{2,1,0:T(8,128)S(1)}, u32[]{:S(2)}, u32[]{:S(2)}) collective-permute-start(f32[49,32,128]{2,1,0:T(8,128)} %get-tuple-element.39), channel_id=1, source_target_pairs={{0,1},{1,0},{2,3},{3,2},{4,5},{5,4},{6,7},{7,6},{8,9},{9,8},{10,11... | collective-permute-start | bytes 2408456 | tf_op jit(solution)/shard_map/ppermute | solution.py:606
  4.3 20.6 %collective-permute-start.6 = (f32[49,32,128]{2,1,0:T(8,128)}, f32[49,32,128]{2,1,0:T(8,128)}, u32[]{:S(2)}, u32[]{:S(2)}) collective-permute-start(f32[49,32,128]{2,1,0:T(8,128)} %get-tuple-element.40), channel_id=1, source_target_pairs={{1,2},{2,1},{5,6},{6,5},{9,10},{10,9},{13,14},{14,13},{17,18},{18,... | collective-permute-start | bytes 2408456 | tf_op jit(solution)/shard_map/ppermute | solution.py:606
  6.9 1.8 %collective-permute-start.1 = (f32[1,128]{1,0:T(1,128)S(1)}, f32[1,128]{1,0:T(1,128)S(1)}, u32[]{:S(2)}, u32[]{:S(2)}) collective-permute-start(f32[1,128]{1,0:T(1,128)S(1)} %compare_select_fusion.1), channel_id=1, source_target_pairs={{0,4},{4,0},{8,12},{12,8},{16,20},{20,16},{24,28},{28,24},{1,5},{5... | collective-permute-start | bytes 1544 | tf_op jit(solution)/shard_map/ppermute | solution.py:599
  8.7 3.3 %collective-permute-start.4 = (f32[2,128]{1,0:T(2,128)S(1)}, f32[2,128]{1,0:T(2,128)S(1)}, u32[]{:S(2)}, u32[]{:S(2)}) collective-permute-start(f32[2,128]{1,0:T(2,128)S(1)} %pad_maximum_fusion), channel_id=1, source_target_pairs={{0,24},{4,28},{8,16},{12,20},{16,8},{20,12},{24,0},{28,4},{1,25},{... | collective-permute-start | bytes 3080 | tf_op jit(solution)/shard_map/ppermute | solution.py:599
  9.9 2.8 %collective-permute-start.3 = (f32[2,128]{1,0:T(2,128)S(1)}, f32[2,128]{1,0:T(2,128)S(1)}, u32[]{:S(2)}, u32[]{:S(2)}) collective-permute-start(f32[2,128]{1,0:T(2,128)S(1)} %pad_maximum_fusion), channel_id=1, source_target_pairs={{0,16},{4,20},{8,24},{12,28},{16,0},{20,4},{24,8},{28,12},{1,17},{... | collective-permute-start | bytes 3080 | tf_op jit(solution)/shard_map/ppermute | solution.py:599
  10.1 2.8 %collective-permute-start.2 = (f32[2,128]{1,0:T(2,128)S(1)}, f32[2,128]{1,0:T(2,128)S(1)}, u32[]{:S(2)}, u32[]{:S(2)}) collective-permute-start(f32[2,128]{1,0:T(2,128)S(1)} %pad_maximum_fusion), channel_id=1, source_target_pairs={{0,8},{4,12},{8,0},{12,4},{16,24},{20,28},{24,16},{28,20},{1,9},{5... | collective-permute-start | bytes 3080 | tf_op jit(solution)/shard_map/ppermute | solution.py:599
  15.9 25.8 %collective-permute-start.8 = (f32[49,32,128]{2,1,0:T(8,128)}, f32[49,32,128]{2,1,0:T(8,128)}, u32[]{:S(2)}, u32[]{:S(2)}) collective-permute-start(f32[49,32,128]{2,1,0:T(8,128)} %get-tuple-element.44), channel_id=1, source_target_pairs={{0,1},{1,0},{2,3},{3,2},{4,5},{5,4},{6,7},{7,6},{8,9},{9,8},{10,11... | collective-permute-start | bytes 2408456 | tf_op jit(solution)/shard_map/ppermute | solution.py:606
  16.0 26.2 %collective-permute-start.9 = (f32[49,32,128]{2,1,0:T(8,128)}, f32[49,32,128]{2,1,0:T(8,128)}, u32[]{:S(2)}, u32[]{:S(2)}) collective-permute-start(f32[49,32,128]{2,1,0:T(8,128)} %get-tuple-element.45), channel_id=1, source_target_pairs={{1,2},{2,1},{5,6},{6,5},{9,10},{10,9},{13,14},{14,13},{17,18},{18,... | collective-permute-start | bytes 2408456 | tf_op jit(solution)/shard_map/ppermute | solution.py:606
  30.6 4.6 %collective-permute-start.7 = (f32[568,128]{1,0:T(8,128)S(1)}, f32[568,128]{1,0:T(8,128)S(1)}, u32[]{:S(2)}, u32[]{:S(2)}) collective-permute-start(f32[568,128]{1,0:T(8,128)S(1)} %get-tuple-element.42), channel_id=1, source_target_pairs={{0,4},{4,0},{8,12},{12,8},{16,20},{20,16},{24,28},{28,24},{1,5},{5... | collective-permute-start | bytes 872456 | tf_op jit(solution)/shard_map/ppermute | solution.py:535
  35.3 6.0 %collective-permute-start = (f32[568,128]{1,0:T(8,128)S(1)}, f32[568,128]{1,0:T(8,128)S(1)}, u32[]{:S(2)}, u32[]{:S(2)}) collective-permute-start(f32[568,128]{1,0:T(8,128)S(1)} %param.1), channel_id=1, source_target_pairs={{0,8},{4,20},{8,0},{12,28},{16,24},{20,4},{24,16},{28,12},{1,9},{5... | collective-permute-start | bytes 872456 | tf_op jit(solution)/shard_map/cond/branch_1_fun/ppermute | solution.py:545
  41.4 6.5 %collective-permute-start.10 = (f32[568,128]{1,0:T(8,128)S(1)}, f32[568,128]{1,0:T(8,128)S(1)}, u32[]{:S(2)}, u32[]{:S(2)}) collective-permute-start(f32[568,128]{1,0:T(8,128)S(1)} %get-tuple-element.64), channel_id=1, source_target_pairs={{0,16},{4,12},{8,24},{12,4},{16,0},{20,28},{24,8},{28,20},{1,17},{... | collective-permute-start | bytes 872456 | tf_op jit(solution)/shard_map/ppermute | solution.py:545
  47.8 11.6 %copy-start = (f32[64,32,128]{2,1,0:T(8,128)S(1)}, f32[64,32,128]{2,1,0:T(8,128)}, u32[]{:S(2)}) copy-start(f32[64,32,128]{2,1,0:T(8,128)} %get-tuple-element.51.ahead) | copy-start | bytes 3145732
  47.9 3.2 %collective-permute-start.11 = (f32[568,128]{1,0:T(8,128)S(1)}, f32[568,128]{1,0:T(8,128)S(1)}, u32[]{:S(2)}, u32[]{:S(2)}) collective-permute-start(f32[568,128]{1,0:T(8,128)S(1)} %get-tuple-element.50), channel_id=1, source_target_pairs={{0,4},{4,0},{8,12},{12,8},{16,20},{20,16},{24,28},{28,24},{1,5},{5... | collective-permute-start | bytes 872456 | tf_op jit(solution)/shard_map/ppermute | solution.py:535
  51.2 5.9 %collective-permute-start.12 = (f32[568,128]{1,0:T(8,128)S(1)}, f32[568,128]{1,0:T(8,128)S(1)}, u32[]{:S(2)}, u32[]{:S(2)}) collective-permute-start(f32[568,128]{1,0:T(8,128)S(1)} %add.85), channel_id=1, source_target_pairs={{0,8},{4,20},{8,0},{12,28},{16,24},{20,4},{24,16},{28,12},{1,9},{5... | collective-permute-start | bytes 872456 | tf_op jit(solution)/shard_map/ppermute | solution.py:545
  52.4 7.0 %collective-permute-start.13 = (f32[568,128]{1,0:T(8,128)S(1)}, f32[568,128]{1,0:T(8,128)S(1)}, u32[]{:S(2)}, u32[]{:S(2)}) collective-permute-start(f32[568,128]{1,0:T(8,128)S(1)} %add.84.own), channel_id=1, source_target_pairs={{0,4},{4,0},{8,12},{12,8},{16,20},{20,16},{24,28},{28,24},{1,5},{5... | collective-permute-start | bytes 872456 | tf_op jit(solution)/shard_map/ppermute | solution.py:553
  57.2 5.9 %collective-permute-start.14 = (f32[568,128]{1,0:T(8,128)S(1)}, f32[568,128]{1,0:T(8,128)S(1)}, u32[]{:S(2)}, u32[]{:S(2)}) collective-permute-start(f32[568,128]{1,0:T(8,128)S(1)} %add.86), channel_id=1, source_target_pairs={{0,16},{4,12},{8,24},{12,4},{16,0},{20,28},{24,8},{28,20},{1,17},{... | collective-permute-start | bytes 872456 | tf_op jit(solution)/shard_map/ppermute | solution.py:545
  63.1 4.0 %collective-permute-start.15 = (f32[568,128]{1,0:T(8,128)S(1)}, f32[568,128]{1,0:T(8,128)S(1)}, u32[]{:S(2)}, u32[]{:S(2)}) collective-permute-start(f32[568,128]{1,0:T(8,128)S(1)} %add.87.own), channel_id=1, source_target_pairs={{0,4},{4,0},{8,12},{12,8},{16,20},{20,16},{24,28},{28,24},{1,5},{5... | collective-permute-start | bytes 872456 | tf_op jit(solution)/shard_map/ppermute | solution.py:553

commit v7 on v6

--- a/solution.py
+++ b/solution.py
@@ -494,37 +494,36 @@
         cols = pl.ds(p.first * LANES, p.nt * LANES)
         return pltpu.make_async_copy(staged.at[r, f], out.at[:, f, r, cols], sems.at[r, f])
 
-    for r in range(p.rows):
-        half, begin = divmod(r, p.hrows)
-        begin *= p.fields
+    for half in range(p.halves):
         at_own = half == core
+        lines = [(half * p.hrows + i // p.fields, i % p.fields) for i in range(p.hrf)]
         for t in range(p.nt):
             pieces = []
-            for f in range(p.fields):
-                at = t * p.block + (begin + f) * n
+            for i in range(p.hrf):
+                at = t * p.block + i * n
                 pieces.append(jnp.where(at_own, own[at : at + n, :], other[at : at + n, :]))
-            at = t * p.block + p.hrf * n + begin
-            plain = jnp.where(at_own, own[at : at + p.fields, :], other[at : at + p.fields, :])
+            at = t * p.block + p.hrf * n
+            plain = jnp.where(at_own, own[at : at + p.plain, :], other[at : at + p.plain, :])
             results = []
             for j, first, stop in p.patches_of(t):
                 mine, centre, keep0 = mixing[j]
-                centred = [pieces[f] - centre * plain[f : f + 1, :] for f in range(p.fields)]
+                centred = [pieces[i] - centre * plain[i : i + 1, :] for i in range(p.hrf)]
                 high, low_part = split(jnp.concatenate(centred, axis=1))
                 joined = jnp.concatenate([high, low_part, high], axis=0)
                 results.append((jnp.dot(mine, joined, preferred_element_type=jnp.float32), keep0, first, stop))
-            for f in range(p.fields):
+            for i, (r, f) in enumerate(lines):
                 x = ahead[(t * p.rows + r) * p.fields + f]
-                average = plain[f : f + 1, :] * (1.0 / p.total)
+                average = plain[i : i + 1, :] * (1.0 / p.total)
                 final = None
                 for update, keep0, first, stop in results:
-                    part = (1.0 - keep0) * average + keep0 * x + update[:, f * LANES : (f + 1) * LANES]
+                    part = (1.0 - keep0) * average + keep0 * x + update[:, i * LANES : (i + 1) * LANES]
                     if final is None:
                         final = part
                     else:
                         at = lane_ids(part.shape)
                         final = jnp.where((at >= first) & (at < stop), part, final)
                 staged[r, f, :, t * LANES : (t + 1) * LANES] = final
-        for f in range(p.fields):
+        for r, f in lines:
             line_copy(r, f).start()
     for r in range(p.rows):
         for f in range(p.fields):

time: 69.1 us -> 68.9 us (level)
  no operation moved by 1% of the time
where the time goes in v7:
time: 68.9 us; the launch traced here: 68.6 us
  Pallas kernels  24.4 us (35%)
  starting transfers between devices  21.4 us (31%)
  waiting for transfers between devices  21.4 us (31%)
  between operations  0.83 us (1%)
    ppermute x4, waiting for transfers between devices, sum_phase(): lax.ppermute(total, 'mem', [(i, i ^ (odd if i & 1 else even)) for i in ra...  11.6 us
    pallas_call x2, Pallas kernels, per_device(): call(functools.partial(forecast_kernel, h), [(shape if c == len(chunks) -...  11.4 us
    ppermute x4, starting transfers between devices, per_device(): lax.ppermute(messages[2 * c + i], 'lat', swaps[i])  7.01 us
    pallas_call x2, Pallas kernels, pack(): call(functools.partial(pack_kernel, h), [pltpu.VMEM((p.rows, p.fields, p....  5.8 us
    ppermute x2, starting transfers between devices, core_sums(): lax.ppermute(send, 'mem', [(i, i ^ 1) for i in range(plan.groups)])  5.43 us
    ppermute x4, waiting for transfers between devices, per_device(): lax.ppermute(messages[2 * c + i], 'lat', swaps[i])  4.95 us
    pallas_call x2, Pallas kernels, finish(): call(functools.partial(solve_kernel, h), [pltpu.VMEM((h.np, p.members, LA...  3.74 us
    ppermute x4, starting transfers between devices, per_device(): lax.ppermute(obs, 'mem', [(i, i ^ bit * b) for i in range(groups)])  3.67 us
  transfers between devices with their start and end apart: 16, of which 12 were waited for; matrix products, arithmetic and copies ran while one was open for 1% of the time, Pallas kernels for 29%

profile of v7, /device:TPU:19, one launch (start us, length us, event | category | flops | bytes accessed | tf_op | source)
XLA Modules:
  0.0 68.6 jit_solution(3941789392718972231)
XLA Ops:
  0.0 2.9 %pack.2 = (f32[4,4,32,640]{3,2,1,0:T(8,128)S(1)}, f32[49,32,128]{2,1,0:T(8,128)}, f32[49,32,128]{2,1,0:T(8,128)}, f32[1,128]{1,0:T(1,128)S(1)}) custom-call(f32[32,4,4,1024]{3,2,1,0:T(4,128)} %raw.2, f32[1,1,16]{2,1,0:T(1,128)} %rest_0_.1, f32[1,1,16]{2,1,0:T(1,128)} %rest_1_.1, s32[1,1,16]{2,1,0:T(1,128)} %rest_2_.1, s32[1,1,16]{2,1,0:T(1,128)} %rest_3_.1), custom_call_target="tpu_custom_call" | custom-call | flops 1048576 | bytes 1048576 | tf_op jit(solution)/shard_map/pack/pallas_call | solution.py:573
  2.9 1.4 %collective-permute-start.5 = (f32[49,32,128]{2,1,0:T(8,128)}, f32[49,32,128]{2,1,0:T(8,128)S(1)}, u32[]{:S(2)}, u32[]{:S(2)}) collective-permute-start(f32[49,32,128]{2,1,0:T(8,128)} %get-tuple-element.39), channel_id=1, source_target_pairs={{0,1},{1,0},{2,3},{3,2},{4,5},{5,4},{6,7},{7,6},{8,9},{9,8},{10,11... | collective-permute-start | bytes 2408456 | tf_op jit(solution)/shard_map/ppermute | solution.py:605
  4.3 1.9 %collective-permute-start.6 = (f32[49,32,128]{2,1,0:T(8,128)}, f32[49,32,128]{2,1,0:T(8,128)}, u32[]{:S(2)}, u32[]{:S(2)}) collective-permute-start(f32[49,32,128]{2,1,0:T(8,128)} %get-tuple-element.40), channel_id=1, source_target_pairs={{1,2},{2,1},{5,6},{6,5},{9,10},{10,9},{13,14},{14,13},{17,18},{18,... | collective-permute-start | bytes 2408456 | tf_op jit(solution)/shard_map/ppermute | solution.py:605
  6.9 1.0 %collective-permute-start.1 = (f32[1,128]{1,0:T(1,128)S(1)}, f32[1,128]{1,0:T(1,128)S(1)}, u32[]{:S(2)}, u32[]{:S(2)}) collective-permute-start(f32[1,128]{1,0:T(1,128)S(1)} %compare_select_fusion.1), channel_id=1, source_target_pairs={{0,4},{4,0},{8,12},{12,8},{16,20},{20,16},{24,28},{28,24},{1,5},{5... | collective-permute-start | bytes 1544 | tf_op jit(solution)/shard_map/ppermute | solution.py:598
  7.9 0.8 %collective-permute-done.1 = f32[1,128]{1,0:T(1,128)S(1)} collective-permute-done((f32[1,128]{1,0:T(1,128)S(1)}, f32[1,128]{1,0:T(1,128)S(1)}, u32[]{:S(2)}, u32[]{:S(2)}) %collective-permute-start.1) | collective-permute-done | bytes 544 | tf_op jit(solution)/shard_map/ppermute | solution.py:598
  8.7 1.2 %collective-permute-start.4 = (f32[2,128]{1,0:T(2,128)S(1)}, f32[2,128]{1,0:T(2,128)S(1)}, u32[]{:S(2)}, u32[]{:S(2)}) collective-permute-start(f32[2,128]{1,0:T(2,128)S(1)} %pad_maximum_fusion), channel_id=1, source_target_pairs={{0,24},{4,28},{8,16},{12,20},{16,8},{20,12},{24,0},{28,4},{1,25},{... | collective-permute-start | bytes 3080 | tf_op jit(solution)/shard_map/ppermute | solution.py:598
  9.9 0.2 collective-permute-start.3
  10.1 1.2 %collective-permute-start.2 = (f32[2,128]{1,0:T(2,128)S(1)}, f32[2,128]{1,0:T(2,128)S(1)}, u32[]{:S(2)}, u32[]{:S(2)}) collective-permute-start(f32[2,128]{1,0:T(2,128)S(1)} %pad_maximum_fusion), channel_id=1, source_target_pairs={{0,8},{4,12},{8,0},{12,4},{16,24},{20,28},{24,16},{28,20},{1,9},{5... | collective-permute-start | bytes 3080 | tf_op jit(solution)/shard_map/ppermute | solution.py:598
  11.4 0.7 collective-permute-done.4
  12.0 0.7 %collective-permute-done.3 = f32[2,128]{1,0:T(2,128)S(1)} collective-permute-done((f32[2,128]{1,0:T(2,128)S(1)}, f32[2,128]{1,0:T(2,128)S(1)}, u32[]{:S(2)}, u32[]{:S(2)}) %collective-permute-start.3) | collective-permute-done | bytes 1056 | tf_op jit(solution)/shard_map/ppermute | solution.py:598
  12.7 0.2 collective-permute-done.2
  13.0 2.9 %pack.3 = (f32[4,4,32,640]{3,2,1,0:T(8,128)S(1)}, f32[49,32,128]{2,1,0:T(8,128)}, f32[49,32,128]{2,1,0:T(8,128)}) custom-call(f32[32,4,4,1024]{3,2,1,0:T(4,128)} %raw.2), custom_call_target="tpu_custom_call" | custom-call | flops 1048576 | bytes 1048576 | tf_op jit(solution)/shard_map/pack/pallas_call | solution.py:573
  15.9 0.1 collective-permute-start.8
  16.0 3.7 %collective-permute-start.9 = (f32[49,32,128]{2,1,0:T(8,128)}, f32[49,32,128]{2,1,0:T(8,128)}, u32[]{:S(2)}, u32[]{:S(2)}) collective-permute-start(f32[49,32,128]{2,1,0:T(8,128)} %get-tuple-element.45), channel_id=1, source_target_pairs={{1,2},{2,1},{5,6},{6,5},{9,10},{10,9},{13,14},{14,13},{17,18},{18,... | collective-permute-start | bytes 2408456 | tf_op jit(solution)/shard_map/ppermute | solution.py:605
  19.6 0.1 fusion.5
  19.8 0.1 reshape.32.table_in
  19.8 0.6 places.1.table
  20.4 1.7 %collective-permute-done.5.first_in = f32[49,32,128]{2,1,0:T(8,128)S(1)} collective-permute-done((f32[49,32,128]{2,1,0:T(8,128)}, f32[49,32,128]{2,1,0:T(8,128)S(1)}, u32[]{:S(2)}, u32[]{:S(2)}) %collective-permute-start.5) | collective-permute-done | bytes 802848 | tf_op jit(solution)/shard_map/ppermute | solution.py:605
  22.1 2.9 %collective-permute-done.6.second_in = f32[49,32,128]{2,1,0:T(8,128)} collective-permute-done((f32[49,32,128]{2,1,0:T(8,128)}, f32[49,32,128]{2,1,0:T(8,128)}, u32[]{:S(2)}, u32[]{:S(2)}) %collective-permute-start.6) | collective-permute-done | bytes 802848 | tf_op jit(solution)/shard_map/ppermute | solution.py:605
  24.9 5.7 %forecast.2 = (f32[64,32,128]{2,1,0:T(8,128)}, f32[32,128]{1,0:T(8,128)S(1)}, f32[568,128]{1,0:T(8,128)S(1)}, f32[568,128]{1,0:T(8,128)S(1)}) custom-call(s32[256]{0:T(256)S(4)} %places.1.table, f32[4,4,32,640]{3,2,1,0:T(8,128)S(1)} %get-tuple-element.38.state, f32[49,32,128]{2,1,0:T(8,128)S(1)} %collective-permute-done.5.first_in, ...), custom_call_target="tpu_custom_call" | custom-call | flops 1024 | bytes 1024 | tf_op jit(solution)/shard_map/forecast/pallas_call | solution.py:627
  30.6 3.4 %collective-permute-start.7 = (f32[568,128]{1,0:T(8,128)S(1)}, f32[568,128]{1,0:T(8,128)S(1)}, u32[]{:S(2)}, u32[]{:S(2)}) collective-permute-start(f32[568,128]{1,0:T(8,128)S(1)} %get-tuple-element.42), channel_id=1, source_target_pairs={{0,4},{4,0},{8,12},{12,8},{16,20},{20,16},{24,28},{28,24},{1,5},{5... | collective-permute-start | bytes 872456 | tf_op jit(solution)/shard_map/ppermute | solution.py:534
  34.0 1.2 %collective-permute-done.7 = f32[568,128]{1,0:T(8,128)S(1)} collective-permute-done((f32[568,128]{1,0:T(8,128)S(1)}, f32[568,128]{1,0:T(8,128)S(1)}, u32[]{:S(2)}, u32[]{:S(2)}) %collective-permute-start.7) | collective-permute-done | bytes 290848 | tf_op jit(solution)/shard_map/ppermute | solution.py:534
  35.2 0.1 add.83
  35.3 6.1 %conditional.1 = (f32[568,128]{1,0:T(8,128)S(1)}) conditional(s32[]{:T(128)} %bitcast.3, f32[568,128]{1,0:T(8,128)S(1)} %add.83, f32[568,128]{1,0:T(8,128)S(1)} %add.83), branch_computations={%region_0.1_spmd, %region_1.2_spmd} | conditional | flops 72704 | bytes 2035760 | solution.py:652
  35.3 1.3 %collective-permute-start = (f32[568,128]{1,0:T(8,128)S(1)}, f32[568,128]{1,0:T(8,128)S(1)}, u32[]{:S(2)}, u32[]{:S(2)}) collective-permute-start(f32[568,128]{1,0:T(8,128)S(1)} %param.1), channel_id=1, source_target_pairs={{0,8},{4,20},{8,0},{12,28},{16,24},{20,4},{24,16},{28,12},{1,9},{5... | collective-permute-start | bytes 872456 | tf_op jit(solution)/shard_map/cond/branch_1_fun/ppermute | solution.py:544
  36.6 4.7 %collective-permute-done = f32[568,128]{1,0:T(8,128)S(1)} collective-permute-done((f32[568,128]{1,0:T(8,128)S(1)}, f32[568,128]{1,0:T(8,128)S(1)}, u32[]{:S(2)}, u32[]{:S(2)}) %collective-permute-start) | collective-permute-done | bytes 290848 | tf_op jit(solution)/shard_map/cond/branch_1_fun/ppermute | solution.py:544
  41.3 0.1 add.55
  41.4 0.3 collective-permute-start.10
  41.7 0.0 collective-permute-done.8.first_in
  41.7 0.4 collective-permute-done.9.second_in
  42.1 5.7 %forecast.3 = (f32[64,32,128]{2,1,0:T(8,128)S(1)}, f32[32,128]{1,0:T(8,128)S(1)}, f32[568,128]{1,0:T(8,128)S(1)}, f32[568,128]{1,0:T(8,128)S(1)}) custom-call(s32[256]{0:T(256)S(4)} %places.1.table, f32[4,4,32,640]{3,2,1,0:T(8,128)S(1)} %get-tuple-element.43.state, f32[49,32,128]{2,1,0:T(8,128)} %collective-permute-done.8.first_in, ...), custom_call_target="tpu_custom_call" | custom-call | flops 1024 | bytes 25165824 | tf_op jit(solution)/shard_map/forecast/pallas_call | solution.py:627
  47.8 0.0 copy-start
  47.9 0.1 add.84.own
  47.9 2.0 %collective-permute-start.11 = (f32[568,128]{1,0:T(8,128)S(1)}, f32[568,128]{1,0:T(8,128)S(1)}, u32[]{:S(2)}, u32[]{:S(2)}) collective-permute-start(f32[568,128]{1,0:T(8,128)S(1)} %get-tuple-element.50), channel_id=1, source_target_pairs={{0,4},{4,0},{8,12},{12,8},{16,20},{20,16},{24,28},{28,24},{1,5},{5... | collective-permute-start | bytes 872456 | tf_op jit(solution)/shard_map/ppermute | solution.py:534
  50.0 1.2 %collective-permute-done.11 = f32[568,128]{1,0:T(8,128)S(1)} collective-permute-done((f32[568,128]{1,0:T(8,128)S(1)}, f32[568,128]{1,0:T(8,128)S(1)}, u32[]{:S(2)}, u32[]{:S(2)}) %collective-permute-start.11) | collective-permute-done | bytes 290848 | tf_op jit(solution)/shard_map/ppermute | solution.py:534
  51.2 0.1 add.85
  51.2 1.2 %collective-permute-start.12 = (f32[568,128]{1,0:T(8,128)S(1)}, f32[568,128]{1,0:T(8,128)S(1)}, u32[]{:S(2)}, u32[]{:S(2)}) collective-permute-start(f32[568,128]{1,0:T(8,128)S(1)} %add.85), channel_id=1, source_target_pairs={{0,8},{4,20},{8,0},{12,28},{16,24},{20,4},{24,16},{28,12},{1,9},{5... | collective-permute-start | bytes 872456 | tf_op jit(solution)/shard_map/ppermute | solution.py:544
  52.4 0.0 collective-permute-start.13
  52.4 4.7 %collective-permute-done.12 = f32[568,128]{1,0:T(8,128)S(1)} collective-permute-done((f32[568,128]{1,0:T(8,128)S(1)}, f32[568,128]{1,0:T(8,128)S(1)}, u32[]{:S(2)}, u32[]{:S(2)}) %collective-permute-start.12) | collective-permute-done | bytes 290848 | tf_op jit(solution)/shard_map/ppermute | solution.py:544
  57.1 0.1 add.86
  57.2 0.3 collective-permute-start.14
  57.5 1.9 %solve.2 = (f32[4,32,128]{2,1,0:T(8,128)S(1)}, f32[4,16,128]{2,1,0:T(8,128)S(1)}, f32[4,8,128]{2,1,0:T(8,128)S(1)}) custom-call(f32[8,128]{1,0:T(8,128)S(1)} %concatenate.8.obs, f32[32,128]{1,0:T(8,128)S(1)} %get-tuple-element.52.seen, f32[568,128]{1,0:T(8,128)S(1)} %add.84.own), custom_call_target="tpu_custom_call" | custom-call | flops 1024 | bytes 6291456 | tf_op jit(solution)/shard_map/solve/pallas_call | solution.py:681
  59.4 1.4 %finish.2.rest_0_ = f32[32,4,4,1024]{3,2,1,0:T(4,128)} custom-call(f32[64,32,128]{2,1,0:T(8,128)S(1)} %copy-done, f32[4,32,128]{2,1,0:T(8,128)S(1)} %get-tuple-element.53.factors, f32[4,16,128]{2,1,0:T(8,128)S(1)} %get-tuple-element.54.centres, f32[4,8,128]{2,1,0:T(8,128)S(1)} %get-tuple-element.55.keeps, f32[568,128]{1,0:T(8,128)S(1)} %add.84.own, ...), custom_call_target="tpu_custom_call" | custom-call | flops 1024 | bytes 16777216 | tf_op jit(solution)/shard_map/finish/pallas_call | solution.py:693
  60.8 2.2 %collective-permute-done.14 = f32[568,128]{1,0:T(8,128)S(1)} collective-permute-done((f32[568,128]{1,0:T(8,128)S(1)}, f32[568,128]{1,0:T(8,128)S(1)}, u32[]{:S(2)}, u32[]{:S(2)}) %collective-permute-start.14) | collective-permute-done | bytes 290848 | tf_op jit(solution)/shard_map/ppermute | solution.py:544
  63.1 0.1 add.87.own
  63.1 2.1 %collective-permute-start.15 = (f32[568,128]{1,0:T(8,128)S(1)}, f32[568,128]{1,0:T(8,128)S(1)}, u32[]{:S(2)}, u32[]{:S(2)}) collective-permute-start(f32[568,128]{1,0:T(8,128)S(1)} %add.87.own), channel_id=1, source_target_pairs={{0,4},{4,0},{8,12},{12,8},{16,20},{20,16},{24,28},{28,24},{1,5},{5... | collective-permute-start | bytes 872456 | tf_op jit(solution)/shard_map/ppermute | solution.py:552
  65.3 1.9 %solve.3 = (f32[4,32,128]{2,1,0:T(8,128)S(1)}, f32[4,16,128]{2,1,0:T(8,128)S(1)}, f32[4,8,128]{2,1,0:T(8,128)S(1)}) custom-call(f32[8,128]{1,0:T(8,128)S(1)} %concatenate.8.obs, f32[32,128]{1,0:T(8,128)S(1)} %get-tuple-element.47.seen, f32[568,128]{1,0:T(8,128)S(1)} %add.87.own), custom_call_target="tpu_custom_call" | custom-call | flops 1024 | bytes 6291456 | tf_op jit(solution)/shard_map/solve/pallas_call | solution.py:681
  67.2 1.4 %finish.3 = f32[32,4,4,1024]{3,2,1,0:T(4,128)} custom-call(f32[64,32,128]{2,1,0:T(8,128)S(1)} %get-tuple-element.46.ahead, f32[4,32,128]{2,1,0:T(8,128)S(1)} %get-tuple-element.57.factors, f32[4,16,128]{2,1,0:T(8,128)S(1)} %get-tuple-element.58.centres, f32[4,8,128]{2,1,0:T(8,128)S(1)} %get-tuple-element.59.keeps, ...), custom_call_target="tpu_custom_call", output_to_operand_aliasing={{}: (6, {})} | custom-call | flops 1024 | bytes 16777216 | tf_op jit(solution)/shard_map/finish/pallas_call | solution.py:693
  (9 shorter events, 0.1 us)
Async XLA Ops:
  2.9 19.1 %collective-permute-start.5 = (f32[49,32,128]{2,1,0:T(8,128)}, f32[49,32,128]{2,1,0:T(8,128)S(1)}, u32[]{:S(2)}, u32[]{:S(2)}) collective-permute-start(f32[49,32,128]{2,1,0:T(8,128)} %get-tuple-element.39), channel_id=1, source_target_pairs={{0,1},{1,0},{2,3},{3,2},{4,5},{5,4},{6,7},{7,6},{8,9},{9,8},{10,11... | collective-permute-start | bytes 2408456 | tf_op jit(solution)/shard_map/ppermute | solution.py:605
  4.3 20.6 %collective-permute-start.6 = (f32[49,32,128]{2,1,0:T(8,128)}, f32[49,32,128]{2,1,0:T(8,128)}, u32[]{:S(2)}, u32[]{:S(2)}) collective-permute-start(f32[49,32,128]{2,1,0:T(8,128)} %get-tuple-element.40), channel_id=1, source_target_pairs={{1,2},{2,1},{5,6},{6,5},{9,10},{10,9},{13,14},{14,13},{17,18},{18,... | collective-permute-start | bytes 2408456 | tf_op jit(solution)/shard_map/ppermute | solution.py:605
  6.9 1.8 %collective-permute-start.1 = (f32[1,128]{1,0:T(1,128)S(1)}, f32[1,128]{1,0:T(1,128)S(1)}, u32[]{:S(2)}, u32[]{:S(2)}) collective-permute-start(f32[1,128]{1,0:T(1,128)S(1)} %compare_select_fusion.1), channel_id=1, source_target_pairs={{0,4},{4,0},{8,12},{12,8},{16,20},{20,16},{24,28},{28,24},{1,5},{5... | collective-permute-start | bytes 1544 | tf_op jit(solution)/shard_map/ppermute | solution.py:598
  8.7 3.3 %collective-permute-start.4 = (f32[2,128]{1,0:T(2,128)S(1)}, f32[2,128]{1,0:T(2,128)S(1)}, u32[]{:S(2)}, u32[]{:S(2)}) collective-permute-start(f32[2,128]{1,0:T(2,128)S(1)} %pad_maximum_fusion), channel_id=1, source_target_pairs={{0,24},{4,28},{8,16},{12,20},{16,8},{20,12},{24,0},{28,4},{1,25},{... | collective-permute-start | bytes 3080 | tf_op jit(solution)/shard_map/ppermute | solution.py:598
  9.9 2.8 %collective-permute-start.3 = (f32[2,128]{1,0:T(2,128)S(1)}, f32[2,128]{1,0:T(2,128)S(1)}, u32[]{:S(2)}, u32[]{:S(2)}) collective-permute-start(f32[2,128]{1,0:T(2,128)S(1)} %pad_maximum_fusion), channel_id=1, source_target_pairs={{0,16},{4,20},{8,24},{12,28},{16,0},{20,4},{24,8},{28,12},{1,17},{... | collective-permute-start | bytes 3080 | tf_op jit(solution)/shard_map/ppermute | solution.py:598
  10.1 2.8 %collective-permute-start.2 = (f32[2,128]{1,0:T(2,128)S(1)}, f32[2,128]{1,0:T(2,128)S(1)}, u32[]{:S(2)}, u32[]{:S(2)}) collective-permute-start(f32[2,128]{1,0:T(2,128)S(1)} %pad_maximum_fusion), channel_id=1, source_target_pairs={{0,8},{4,12},{8,0},{12,4},{16,24},{20,28},{24,16},{28,20},{1,9},{5... | collective-permute-start | bytes 3080 | tf_op jit(solution)/shard_map/ppermute | solution.py:598
  15.9 25.8 %collective-permute-start.8 = (f32[49,32,128]{2,1,0:T(8,128)}, f32[49,32,128]{2,1,0:T(8,128)}, u32[]{:S(2)}, u32[]{:S(2)}) collective-permute-start(f32[49,32,128]{2,1,0:T(8,128)} %get-tuple-element.44), channel_id=1, source_target_pairs={{0,1},{1,0},{2,3},{3,2},{4,5},{5,4},{6,7},{7,6},{8,9},{9,8},{10,11... | collective-permute-start | bytes 2408456 | tf_op jit(solution)/shard_map/ppermute | solution.py:605
  16.0 26.2 %collective-permute-start.9 = (f32[49,32,128]{2,1,0:T(8,128)}, f32[49,32,128]{2,1,0:T(8,128)}, u32[]{:S(2)}, u32[]{:S(2)}) collective-permute-start(f32[49,32,128]{2,1,0:T(8,128)} %get-tuple-element.45), channel_id=1, source_target_pairs={{1,2},{2,1},{5,6},{6,5},{9,10},{10,9},{13,14},{14,13},{17,18},{18,... | collective-permute-start | bytes 2408456 | tf_op jit(solution)/shard_map/ppermute | solution.py:605
  30.6 4.6 %collective-permute-start.7 = (f32[568,128]{1,0:T(8,128)S(1)}, f32[568,128]{1,0:T(8,128)S(1)}, u32[]{:S(2)}, u32[]{:S(2)}) collective-permute-start(f32[568,128]{1,0:T(8,128)S(1)} %get-tuple-element.42), channel_id=1, source_target_pairs={{0,4},{4,0},{8,12},{12,8},{16,20},{20,16},{24,28},{28,24},{1,5},{5... | collective-permute-start | bytes 872456 | tf_op jit(solution)/shard_map/ppermute | solution.py:534
  35.3 6.0 %collective-permute-start = (f32[568,128]{1,0:T(8,128)S(1)}, f32[568,128]{1,0:T(8,128)S(1)}, u32[]{:S(2)}, u32[]{:S(2)}) collective-permute-start(f32[568,128]{1,0:T(8,128)S(1)} %param.1), channel_id=1, source_target_pairs={{0,8},{4,20},{8,0},{12,28},{16,24},{20,4},{24,16},{28,12},{1,9},{5... | collective-permute-start | bytes 872456 | tf_op jit(solution)/shard_map/cond/branch_1_fun/ppermute | solution.py:544
  41.4 6.5 %collective-permute-start.10 = (f32[568,128]{1,0:T(8,128)S(1)}, f32[568,128]{1,0:T(8,128)S(1)}, u32[]{:S(2)}, u32[]{:S(2)}) collective-permute-start(f32[568,128]{1,0:T(8,128)S(1)} %get-tuple-element.64), channel_id=1, source_target_pairs={{0,16},{4,12},{8,24},{12,4},{16,0},{20,28},{24,8},{28,20},{1,17},{... | collective-permute-start | bytes 872456 | tf_op jit(solution)/shard_map/ppermute | solution.py:544
  47.8 11.6 %copy-start = (f32[64,32,128]{2,1,0:T(8,128)S(1)}, f32[64,32,128]{2,1,0:T(8,128)}, u32[]{:S(2)}) copy-start(f32[64,32,128]{2,1,0:T(8,128)} %get-tuple-element.51.ahead) | copy-start | bytes 3145732
  47.9 3.2 %collective-permute-start.11 = (f32[568,128]{1,0:T(8,128)S(1)}, f32[568,128]{1,0:T(8,128)S(1)}, u32[]{:S(2)}, u32[]{:S(2)}) collective-permute-start(f32[568,128]{1,0:T(8,128)S(1)} %get-tuple-element.50), channel_id=1, source_target_pairs={{0,4},{4,0},{8,12},{12,8},{16,20},{20,16},{24,28},{28,24},{1,5},{5... | collective-permute-start | bytes 872456 | tf_op jit(solution)/shard_map/ppermute | solution.py:534
  51.2 5.9 %collective-permute-start.12 = (f32[568,128]{1,0:T(8,128)S(1)}, f32[568,128]{1,0:T(8,128)S(1)}, u32[]{:S(2)}, u32[]{:S(2)}) collective-permute-start(f32[568,128]{1,0:T(8,128)S(1)} %add.85), channel_id=1, source_target_pairs={{0,8},{4,20},{8,0},{12,28},{16,24},{20,4},{24,16},{28,12},{1,9},{5... | collective-permute-start | bytes 872456 | tf_op jit(solution)/shard_map/ppermute | solution.py:544
  52.4 7.0 %collective-permute-start.13 = (f32[568,128]{1,0:T(8,128)S(1)}, f32[568,128]{1,0:T(8,128)S(1)}, u32[]{:S(2)}, u32[]{:S(2)}) collective-permute-start(f32[568,128]{1,0:T(8,128)S(1)} %add.84.own), channel_id=1, source_target_pairs={{0,4},{4,0},{8,12},{12,8},{16,20},{20,16},{24,28},{28,24},{1,5},{5... | collective-permute-start | bytes 872456 | tf_op jit(solution)/shard_map/ppermute | solution.py:552
  57.2 5.9 %collective-permute-start.14 = (f32[568,128]{1,0:T(8,128)S(1)}, f32[568,128]{1,0:T(8,128)S(1)}, u32[]{:S(2)}, u32[]{:S(2)}) collective-permute-start(f32[568,128]{1,0:T(8,128)S(1)} %add.86), channel_id=1, source_target_pairs={{0,16},{4,12},{8,24},{12,4},{16,0},{20,28},{24,8},{28,20},{1,17},{... | collective-permute-start | bytes 872456 | tf_op jit(solution)/shard_map/ppermute | solution.py:544
  63.1 4.0 %collective-permute-start.15 = (f32[568,128]{1,0:T(8,128)S(1)}, f32[568,128]{1,0:T(8,128)S(1)}, u32[]{:S(2)}, u32[]{:S(2)}) collective-permute-start(f32[568,128]{1,0:T(8,128)S(1)} %add.87.own), channel_id=1, source_target_pairs={{0,4},{4,0},{8,12},{12,8},{16,20},{20,16},{24,28},{28,24},{1,5},{5... | collective-permute-start | bytes 872456 | tf_op jit(solution)/shard_map/ppermute | solution.py:552

commit v8 on v7

--- a/solution.py
+++ b/solution.py
@@ -351,42 +351,44 @@
             found = jnp.where(wide == to, pltpu.roll(ahead[table[at + o]], table[every + at + o], 1), found)
     seen[...] = found
 
-    high, low_part = (a.astype(jnp.float32) for a in split(found))
+    share = 1.0 / p.members
+    average = jnp.sum(found, axis=0, keepdims=True) * share
+    high, low_part = (a.astype(jnp.float32) for a in split(found - average))
     turned = jnp.transpose(jnp.concatenate([high, high, low_part], axis=0))
-    depth = 3 * p.members
-    extra = lax.broadcasted_iota(jnp.int32, (2 * SUB, depth), 0)
-    ones = jnp.where((extra == 0) & (lane_ids((2 * SUB, depth)) < 2 * p.members), 1.0, 0.0).astype(jnp.float32)
-    sides = [
-        jnp.concatenate([turned[j * p.slots : (j + 1) * p.slots], ones], axis=0).astype(jnp.bfloat16) for j in range(p.np)
-    ]
-    lanes = lane_ids((p.slots + 2 * SUB, LANES))
-    moments = jnp.zeros((p.slots + 2 * SUB, LANES), jnp.float32)
+    weigh = jnp.transpose(jnp.broadcast_to(average * p.members, (SUB, LANES)))
+    sides = [turned[j * p.slots : (j + 1) * p.slots].astype(jnp.bfloat16) for j in range(p.np)]
+    weighs = [weigh[j * p.slots : (j + 1) * p.slots, 0:1] for j in range(p.np)]
+    lanes = lane_ids((p.slots, LANES))
+    moments = jnp.zeros((p.slots, LANES), jnp.float32)
     joined = jnp.concatenate([a.astype(jnp.bfloat16) for a in (high, low_part, high)], axis=0)
     for j in range(p.np):
-        part = jnp.dot(sides[j], joined, preferred_element_type=jnp.float32)
+        part = jnp.dot(sides[j], joined, preferred_element_type=jnp.float32) + weighs[j] * average
         moments = jnp.where((lanes >= j * p.slots) & (lanes < (j + 1) * p.slots), part, moments)
     for out in (keep, send):
-        out[pl.ds(p.cell_rows, p.slots + SUB), :] = moments[: p.slots + SUB]
+        out[pl.ds(p.cell_rows, p.slots), :] = moments
+        out[pl.ds(p.cell_rows + p.slots, SUB), :] = jnp.broadcast_to(average * p.members, (SUB, LANES))
     for side in range(p.halves):
         out = keep if side == 0 else send
         half = core if side == 0 else 1 - core
         for t in range(p.nt):
             base = t * p.block
             begin = (t * p.rows + half * p.hrows) * p.fields
-            high, low_part = split(jnp.concatenate([ahead[begin + i] for i in range(p.hrf)], axis=1))
+            tiles = [ahead[begin + i] for i in range(p.hrf)]
+            means = [jnp.sum(x, axis=0, keepdims=True) * share for x in tiles]
+            high, low_part = split(jnp.concatenate([x - m for x, m in zip(tiles, means)], axis=1))
             joined = jnp.concatenate([high, low_part, high], axis=0)
+            line = jnp.concatenate(means, axis=1)
             result = None
             for j, first, stop in p.patches_of(t):
-                part = jnp.dot(sides[j], joined, preferred_element_type=jnp.float32)
+                part = jnp.dot(sides[j], joined, preferred_element_type=jnp.float32) + weighs[j] * line
                 if result is None:
                     result = part
                 else:
                     at = lane_ids(part.shape) % LANES
                     result = jnp.where((at >= first) & (at < stop), part, result)
             for i in range(p.hrf):
-                piece = result[:, i * LANES : (i + 1) * LANES]
-                out[pl.ds(base + i * p.slots, p.slots), :] = piece[: p.slots]
-                out[pl.ds(base + p.hrf * p.slots + i, 1), :] = piece[p.slots : p.slots + 1]
+                out[pl.ds(base + i * p.slots, p.slots), :] = result[:, i * LANES : (i + 1) * LANES]
+                out[pl.ds(base + p.hrf * p.slots + i, 1), :] = means[i] * p.members
             for i in range(p.hrf, p.plain):
                 out[pl.ds(base + p.hrf * p.slots + i, 1), :] = jnp.zeros((1, LANES), jnp.float32)
     if rest:

time: 68.9 us -> 69 us (level)
  no operation moved by 1% of the time
where the time goes in v8:
time: 69 us; the launch traced here: 68.7 us
  Pallas kernels  24.5 us (36%)
  starting transfers between devices  21.4 us (31%)
  waiting for transfers between devices  21.4 us (31%)
  between operations  0.83 us (1%)
    ppermute x4, waiting for transfers between devices, sum_phase(): lax.ppermute(total, 'mem', [(i, i ^ (odd if i & 1 else even)) for i in ra...  11.7 us
    pallas_call x2, Pallas kernels, per_device(): call(functools.partial(forecast_kernel, h), [(shape if c == len(chunks) -...  11.5 us
    ppermute x4, starting transfers between devices, per_device(): lax.ppermute(messages[2 * c + i], 'lat', swaps[i])  7.01 us
    pallas_call x2, Pallas kernels, pack(): call(functools.partial(pack_kernel, h), [pltpu.VMEM((p.rows, p.fields, p....  5.8 us
    ppermute x2, starting transfers between devices, core_sums(): lax.ppermute(send, 'mem', [(i, i ^ 1) for i in range(plan.groups)])  5.48 us
    ppermute x4, waiting for transfers between devices, per_device(): lax.ppermute(messages[2 * c + i], 'lat', swaps[i])  4.9 us
    pallas_call x2, Pallas kernels, finish(): call(functools.partial(solve_kernel, h), [pltpu.VMEM((h.np, p.members, LA...  3.74 us
    ppermute x4, starting transfers between devices, per_device(): lax.ppermute(obs, 'mem', [(i, i ^ bit * b) for i in range(groups)])  3.67 us
  transfers between devices with their start and end apart: 16, of which 12 were waited for; matrix products, arithmetic and copies ran while one was open for 1% of the time, Pallas kernels for 29%

profile of v8, /device:TPU:19, one launch (start us, length us, event | category | flops | bytes accessed | tf_op | source)
XLA Modules:
  0.0 68.7 jit_solution(13372995053329615562)
XLA Ops:
  0.0 2.9 %pack.2 = (f32[4,4,32,640]{3,2,1,0:T(8,128)S(1)}, f32[49,32,128]{2,1,0:T(8,128)}, f32[49,32,128]{2,1,0:T(8,128)}, f32[1,128]{1,0:T(1,128)S(1)}) custom-call(f32[32,4,4,1024]{3,2,1,0:T(4,128)} %raw.2, f32[1,1,16]{2,1,0:T(1,128)} %rest_0_.1, f32[1,1,16]{2,1,0:T(1,128)} %rest_1_.1, s32[1,1,16]{2,1,0:T(1,128)} %rest_2_.1, s32[1,1,16]{2,1,0:T(1,128)} %rest_3_.1), custom_call_target="tpu_custom_call" | custom-call | flops 1048576 | bytes 1048576 | tf_op jit(solution)/shard_map/pack/pallas_call | solution.py:575
  2.9 1.4 %collective-permute-start.5 = (f32[49,32,128]{2,1,0:T(8,128)}, f32[49,32,128]{2,1,0:T(8,128)S(1)}, u32[]{:S(2)}, u32[]{:S(2)}) collective-permute-start(f32[49,32,128]{2,1,0:T(8,128)} %get-tuple-element.39), channel_id=1, source_target_pairs={{0,1},{1,0},{2,3},{3,2},{4,5},{5,4},{6,7},{7,6},{8,9},{9,8},{10,11... | collective-permute-start | bytes 2408456 | tf_op jit(solution)/shard_map/ppermute | solution.py:607
  4.3 1.9 %collective-permute-start.6 = (f32[49,32,128]{2,1,0:T(8,128)}, f32[49,32,128]{2,1,0:T(8,128)}, u32[]{:S(2)}, u32[]{:S(2)}) collective-permute-start(f32[49,32,128]{2,1,0:T(8,128)} %get-tuple-element.40), channel_id=1, source_target_pairs={{1,2},{2,1},{5,6},{6,5},{9,10},{10,9},{13,14},{14,13},{17,18},{18,... | collective-permute-start | bytes 2408456 | tf_op jit(solution)/shard_map/ppermute | solution.py:607
  6.9 1.0 %collective-permute-start.1 = (f32[1,128]{1,0:T(1,128)S(1)}, f32[1,128]{1,0:T(1,128)S(1)}, u32[]{:S(2)}, u32[]{:S(2)}) collective-permute-start(f32[1,128]{1,0:T(1,128)S(1)} %compare_select_fusion.1), channel_id=1, source_target_pairs={{0,4},{4,0},{8,12},{12,8},{16,20},{20,16},{24,28},{28,24},{1,5},{5... | collective-permute-start | bytes 1544 | tf_op jit(solution)/shard_map/ppermute | solution.py:600
  7.9 0.8 %collective-permute-done.1 = f32[1,128]{1,0:T(1,128)S(1)} collective-permute-done((f32[1,128]{1,0:T(1,128)S(1)}, f32[1,128]{1,0:T(1,128)S(1)}, u32[]{:S(2)}, u32[]{:S(2)}) %collective-permute-start.1) | collective-permute-done | bytes 544 | tf_op jit(solution)/shard_map/ppermute | solution.py:600
  8.7 1.2 %collective-permute-start.4 = (f32[2,128]{1,0:T(2,128)S(1)}, f32[2,128]{1,0:T(2,128)S(1)}, u32[]{:S(2)}, u32[]{:S(2)}) collective-permute-start(f32[2,128]{1,0:T(2,128)S(1)} %pad_maximum_fusion), channel_id=1, source_target_pairs={{0,24},{4,28},{8,16},{12,20},{16,8},{20,12},{24,0},{28,4},{1,25},{... | collective-permute-start | bytes 3080 | tf_op jit(solution)/shard_map/ppermute | solution.py:600
  9.9 0.2 collective-permute-start.3
  10.1 1.2 %collective-permute-start.2 = (f32[2,128]{1,0:T(2,128)S(1)}, f32[2,128]{1,0:T(2,128)S(1)}, u32[]{:S(2)}, u32[]{:S(2)}) collective-permute-start(f32[2,128]{1,0:T(2,128)S(1)} %pad_maximum_fusion), channel_id=1, source_target_pairs={{0,8},{4,12},{8,0},{12,4},{16,24},{20,28},{24,16},{28,20},{1,9},{5... | collective-permute-start | bytes 3080 | tf_op jit(solution)/shard_map/ppermute | solution.py:600
  11.4 0.7 collective-permute-done.4
  12.0 0.7 %collective-permute-done.3 = f32[2,128]{1,0:T(2,128)S(1)} collective-permute-done((f32[2,128]{1,0:T(2,128)S(1)}, f32[2,128]{1,0:T(2,128)S(1)}, u32[]{:S(2)}, u32[]{:S(2)}) %collective-permute-start.3) | collective-permute-done | bytes 1056 | tf_op jit(solution)/shard_map/ppermute | solution.py:600
  12.7 0.2 collective-permute-done.2
  13.0 2.9 %pack.3 = (f32[4,4,32,640]{3,2,1,0:T(8,128)S(1)}, f32[49,32,128]{2,1,0:T(8,128)}, f32[49,32,128]{2,1,0:T(8,128)}) custom-call(f32[32,4,4,1024]{3,2,1,0:T(4,128)} %raw.2), custom_call_target="tpu_custom_call" | custom-call | flops 1048576 | bytes 1048576 | tf_op jit(solution)/shard_map/pack/pallas_call | solution.py:575
  15.9 0.1 collective-permute-start.8
  16.0 3.7 %collective-permute-start.9 = (f32[49,32,128]{2,1,0:T(8,128)}, f32[49,32,128]{2,1,0:T(8,128)}, u32[]{:S(2)}, u32[]{:S(2)}) collective-permute-start(f32[49,32,128]{2,1,0:T(8,128)} %get-tuple-element.45), channel_id=1, source_target_pairs={{1,2},{2,1},{5,6},{6,5},{9,10},{10,9},{13,14},{14,13},{17,18},{18,... | collective-permute-start | bytes 2408456 | tf_op jit(solution)/shard_map/ppermute | solution.py:607
  19.6 0.1 fusion.5
  19.8 0.1 reshape.32.table_in
  19.8 0.6 places.1.table
  20.4 1.7 %collective-permute-done.5.first_in = f32[49,32,128]{2,1,0:T(8,128)S(1)} collective-permute-done((f32[49,32,128]{2,1,0:T(8,128)}, f32[49,32,128]{2,1,0:T(8,128)S(1)}, u32[]{:S(2)}, u32[]{:S(2)}) %collective-permute-start.5) | collective-permute-done | bytes 802848 | tf_op jit(solution)/shard_map/ppermute | solution.py:607
  22.1 2.9 %collective-permute-done.6.second_in = f32[49,32,128]{2,1,0:T(8,128)} collective-permute-done((f32[49,32,128]{2,1,0:T(8,128)}, f32[49,32,128]{2,1,0:T(8,128)}, u32[]{:S(2)}, u32[]{:S(2)}) %collective-permute-start.6) | collective-permute-done | bytes 802848 | tf_op jit(solution)/shard_map/ppermute | solution.py:607
  24.9 5.8 %forecast.2 = (f32[64,32,128]{2,1,0:T(8,128)}, f32[32,128]{1,0:T(8,128)S(1)}, f32[568,128]{1,0:T(8,128)S(1)}, f32[568,128]{1,0:T(8,128)S(1)}) custom-call(s32[256]{0:T(256)S(4)} %places.1.table, f32[4,4,32,640]{3,2,1,0:T(8,128)S(1)} %get-tuple-element.38.state, f32[49,32,128]{2,1,0:T(8,128)S(1)} %collective-permute-done.5.first_in, ...), custom_call_target="tpu_custom_call" | custom-call | flops 1024 | bytes 1024 | tf_op jit(solution)/shard_map/forecast/pallas_call | solution.py:629
  30.7 3.4 %collective-permute-start.7 = (f32[568,128]{1,0:T(8,128)S(1)}, f32[568,128]{1,0:T(8,128)S(1)}, u32[]{:S(2)}, u32[]{:S(2)}) collective-permute-start(f32[568,128]{1,0:T(8,128)S(1)} %get-tuple-element.42), channel_id=1, source_target_pairs={{0,4},{4,0},{8,12},{12,8},{16,20},{20,16},{24,28},{28,24},{1,5},{5... | collective-permute-start | bytes 872456 | tf_op jit(solution)/shard_map/ppermute | solution.py:536
  34.1 1.2 %collective-permute-done.7 = f32[568,128]{1,0:T(8,128)S(1)} collective-permute-done((f32[568,128]{1,0:T(8,128)S(1)}, f32[568,128]{1,0:T(8,128)S(1)}, u32[]{:S(2)}, u32[]{:S(2)}) %collective-permute-start.7) | collective-permute-done | bytes 290848 | tf_op jit(solution)/shard_map/ppermute | solution.py:536
  35.3 0.1 add.83
  35.4 6.1 %conditional.1 = (f32[568,128]{1,0:T(8,128)S(1)}) conditional(s32[]{:T(128)} %bitcast.3, f32[568,128]{1,0:T(8,128)S(1)} %add.83, f32[568,128]{1,0:T(8,128)S(1)} %add.83), branch_computations={%region_0.1_spmd, %region_1.2_spmd} | conditional | flops 72704 | bytes 2035760 | solution.py:654
  35.4 1.3 %collective-permute-start = (f32[568,128]{1,0:T(8,128)S(1)}, f32[568,128]{1,0:T(8,128)S(1)}, u32[]{:S(2)}, u32[]{:S(2)}) collective-permute-start(f32[568,128]{1,0:T(8,128)S(1)} %param.1), channel_id=1, source_target_pairs={{0,8},{4,20},{8,0},{12,28},{16,24},{20,4},{24,16},{28,12},{1,9},{5... | collective-permute-start | bytes 872456 | tf_op jit(solution)/shard_map/cond/branch_1_fun/ppermute | solution.py:546
  36.7 4.7 %collective-permute-done = f32[568,128]{1,0:T(8,128)S(1)} collective-permute-done((f32[568,128]{1,0:T(8,128)S(1)}, f32[568,128]{1,0:T(8,128)S(1)}, u32[]{:S(2)}, u32[]{:S(2)}) %collective-permute-start) | collective-permute-done | bytes 290848 | tf_op jit(solution)/shard_map/cond/branch_1_fun/ppermute | solution.py:546
  41.4 0.1 add.55
  41.4 0.3 collective-permute-start.10
  41.8 0.0 collective-permute-done.8.first_in
  41.8 0.4 collective-permute-done.9.second_in
  42.1 5.8 %forecast.3 = (f32[64,32,128]{2,1,0:T(8,128)S(1)}, f32[32,128]{1,0:T(8,128)S(1)}, f32[568,128]{1,0:T(8,128)S(1)}, f32[568,128]{1,0:T(8,128)S(1)}) custom-call(s32[256]{0:T(256)S(4)} %places.1.table, f32[4,4,32,640]{3,2,1,0:T(8,128)S(1)} %get-tuple-element.43.state, f32[49,32,128]{2,1,0:T(8,128)} %collective-permute-done.8.first_in, ...), custom_call_target="tpu_custom_call" | custom-call | flops 1024 | bytes 25165824 | tf_op jit(solution)/shard_map/forecast/pallas_call | solution.py:629
  47.9 0.0 copy-start
  47.9 0.1 add.84.own
  48.0 2.1 %collective-permute-start.11 = (f32[568,128]{1,0:T(8,128)S(1)}, f32[568,128]{1,0:T(8,128)S(1)}, u32[]{:S(2)}, u32[]{:S(2)}) collective-permute-start(f32[568,128]{1,0:T(8,128)S(1)} %get-tuple-element.50), channel_id=1, source_target_pairs={{0,4},{4,0},{8,12},{12,8},{16,20},{20,16},{24,28},{28,24},{1,5},{5... | collective-permute-start | bytes 872456 | tf_op jit(solution)/shard_map/ppermute | solution.py:536
  50.1 1.2 %collective-permute-done.11 = f32[568,128]{1,0:T(8,128)S(1)} collective-permute-done((f32[568,128]{1,0:T(8,128)S(1)}, f32[568,128]{1,0:T(8,128)S(1)}, u32[]{:S(2)}, u32[]{:S(2)}) %collective-permute-start.11) | collective-permute-done | bytes 290848 | tf_op jit(solution)/shard_map/ppermute | solution.py:536
  51.3 0.1 add.85
  51.3 1.1 %collective-permute-start.12 = (f32[568,128]{1,0:T(8,128)S(1)}, f32[568,128]{1,0:T(8,128)S(1)}, u32[]{:S(2)}, u32[]{:S(2)}) collective-permute-start(f32[568,128]{1,0:T(8,128)S(1)} %add.85), channel_id=1, source_target_pairs={{0,8},{4,20},{8,0},{12,28},{16,24},{20,4},{24,16},{28,12},{1,9},{5... | collective-permute-start | bytes 872456 | tf_op jit(solution)/shard_map/ppermute | solution.py:546
  52.5 4.7 %collective-permute-done.12 = f32[568,128]{1,0:T(8,128)S(1)} collective-permute-done((f32[568,128]{1,0:T(8,128)S(1)}, f32[568,128]{1,0:T(8,128)S(1)}, u32[]{:S(2)}, u32[]{:S(2)}) %collective-permute-start.12) | collective-permute-done | bytes 290848 | tf_op jit(solution)/shard_map/ppermute | solution.py:546
  57.2 0.1 add.86
  57.3 0.3 collective-permute-start.14
  57.6 1.9 %solve.2 = (f32[4,32,128]{2,1,0:T(8,128)S(1)}, f32[4,16,128]{2,1,0:T(8,128)S(1)}, f32[4,8,128]{2,1,0:T(8,128)S(1)}) custom-call(f32[8,128]{1,0:T(8,128)S(1)} %concatenate.8.obs, f32[32,128]{1,0:T(8,128)S(1)} %get-tuple-element.52.seen, f32[568,128]{1,0:T(8,128)S(1)} %add.84.own), custom_call_target="tpu_custom_call" | custom-call | flops 1024 | bytes 6291456 | tf_op jit(solution)/shard_map/solve/pallas_call | solution.py:683
  59.5 1.4 %finish.2.rest_0_ = f32[32,4,4,1024]{3,2,1,0:T(4,128)} custom-call(f32[64,32,128]{2,1,0:T(8,128)S(1)} %copy-done, f32[4,32,128]{2,1,0:T(8,128)S(1)} %get-tuple-element.53.factors, f32[4,16,128]{2,1,0:T(8,128)S(1)} %get-tuple-element.54.centres, f32[4,8,128]{2,1,0:T(8,128)S(1)} %get-tuple-element.55.keeps, f32[568,128]{1,0:T(8,128)S(1)} %add.84.own, ...), custom_call_target="tpu_custom_call" | custom-call | flops 1024 | bytes 16777216 | tf_op jit(solution)/shard_map/finish/pallas_call | solution.py:695
  60.9 2.2 %collective-permute-done.14 = f32[568,128]{1,0:T(8,128)S(1)} collective-permute-done((f32[568,128]{1,0:T(8,128)S(1)}, f32[568,128]{1,0:T(8,128)S(1)}, u32[]{:S(2)}, u32[]{:S(2)}) %collective-permute-start.14) | collective-permute-done | bytes 290848 | tf_op jit(solution)/shard_map/ppermute | solution.py:546
  63.2 0.1 add.87.own
  63.3 2.1 %collective-permute-start.15 = (f32[568,128]{1,0:T(8,128)S(1)}, f32[568,128]{1,0:T(8,128)S(1)}, u32[]{:S(2)}, u32[]{:S(2)}) collective-permute-start(f32[568,128]{1,0:T(8,128)S(1)} %add.87.own), channel_id=1, source_target_pairs={{0,4},{4,0},{8,12},{12,8},{16,20},{20,16},{24,28},{28,24},{1,5},{5... | collective-permute-start | bytes 872456 | tf_op jit(solution)/shard_map/ppermute | solution.py:554
  65.4 1.9 %solve.3 = (f32[4,32,128]{2,1,0:T(8,128)S(1)}, f32[4,16,128]{2,1,0:T(8,128)S(1)}, f32[4,8,128]{2,1,0:T(8,128)S(1)}) custom-call(f32[8,128]{1,0:T(8,128)S(1)} %concatenate.8.obs, f32[32,128]{1,0:T(8,128)S(1)} %get-tuple-element.47.seen, f32[568,128]{1,0:T(8,128)S(1)} %add.87.own), custom_call_target="tpu_custom_call" | custom-call | flops 1024 | bytes 6291456 | tf_op jit(solution)/shard_map/solve/pallas_call | solution.py:683
  67.3 0.0 collective-permute-done.15.other
  67.3 1.4 %finish.3 = f32[32,4,4,1024]{3,2,1,0:T(4,128)} custom-call(f32[64,32,128]{2,1,0:T(8,128)S(1)} %get-tuple-element.46.ahead, f32[4,32,128]{2,1,0:T(8,128)S(1)} %get-tuple-element.57.factors, f32[4,16,128]{2,1,0:T(8,128)S(1)} %get-tuple-element.58.centres, f32[4,8,128]{2,1,0:T(8,128)S(1)} %get-tuple-element.59.keeps, ...), custom_call_target="tpu_custom_call", output_to_operand_aliasing={{}: (6, {})} | custom-call | flops 1024 | bytes 16777216 | tf_op jit(solution)/shard_map/finish/pallas_call | solution.py:695
  (9 shorter events, 0.1 us)
Async XLA Ops:
  2.9 19.1 %collective-permute-start.5 = (f32[49,32,128]{2,1,0:T(8,128)}, f32[49,32,128]{2,1,0:T(8,128)S(1)}, u32[]{:S(2)}, u32[]{:S(2)}) collective-permute-start(f32[49,32,128]{2,1,0:T(8,128)} %get-tuple-element.39), channel_id=1, source_target_pairs={{0,1},{1,0},{2,3},{3,2},{4,5},{5,4},{6,7},{7,6},{8,9},{9,8},{10,11... | collective-permute-start | bytes 2408456 | tf_op jit(solution)/shard_map/ppermute | solution.py:607
  4.3 20.6 %collective-permute-start.6 = (f32[49,32,128]{2,1,0:T(8,128)}, f32[49,32,128]{2,1,0:T(8,128)}, u32[]{:S(2)}, u32[]{:S(2)}) collective-permute-start(f32[49,32,128]{2,1,0:T(8,128)} %get-tuple-element.40), channel_id=1, source_target_pairs={{1,2},{2,1},{5,6},{6,5},{9,10},{10,9},{13,14},{14,13},{17,18},{18,... | collective-permute-start | bytes 2408456 | tf_op jit(solution)/shard_map/ppermute | solution.py:607
  6.9 1.8 %collective-permute-start.1 = (f32[1,128]{1,0:T(1,128)S(1)}, f32[1,128]{1,0:T(1,128)S(1)}, u32[]{:S(2)}, u32[]{:S(2)}) collective-permute-start(f32[1,128]{1,0:T(1,128)S(1)} %compare_select_fusion.1), channel_id=1, source_target_pairs={{0,4},{4,0},{8,12},{12,8},{16,20},{20,16},{24,28},{28,24},{1,5},{5... | collective-permute-start | bytes 1544 | tf_op jit(solution)/shard_map/ppermute | solution.py:600
  8.7 3.3 %collective-permute-start.4 = (f32[2,128]{1,0:T(2,128)S(1)}, f32[2,128]{1,0:T(2,128)S(1)}, u32[]{:S(2)}, u32[]{:S(2)}) collective-permute-start(f32[2,128]{1,0:T(2,128)S(1)} %pad_maximum_fusion), channel_id=1, source_target_pairs={{0,24},{4,28},{8,16},{12,20},{16,8},{20,12},{24,0},{28,4},{1,25},{... | collective-permute-start | bytes 3080 | tf_op jit(solution)/shard_map/ppermute | solution.py:600
  9.9 2.8 %collective-permute-start.3 = (f32[2,128]{1,0:T(2,128)S(1)}, f32[2,128]{1,0:T(2,128)S(1)}, u32[]{:S(2)}, u32[]{:S(2)}) collective-permute-start(f32[2,128]{1,0:T(2,128)S(1)} %pad_maximum_fusion), channel_id=1, source_target_pairs={{0,16},{4,20},{8,24},{12,28},{16,0},{20,4},{24,8},{28,12},{1,17},{... | collective-permute-start | bytes 3080 | tf_op jit(solution)/shard_map/ppermute | solution.py:600
  10.1 2.8 %collective-permute-start.2 = (f32[2,128]{1,0:T(2,128)S(1)}, f32[2,128]{1,0:T(2,128)S(1)}, u32[]{:S(2)}, u32[]{:S(2)}) collective-permute-start(f32[2,128]{1,0:T(2,128)S(1)} %pad_maximum_fusion), channel_id=1, source_target_pairs={{0,8},{4,12},{8,0},{12,4},{16,24},{20,28},{24,16},{28,20},{1,9},{5... | collective-permute-start | bytes 3080 | tf_op jit(solution)/shard_map/ppermute | solution.py:600
  15.9 25.9 %collective-permute-start.8 = (f32[49,32,128]{2,1,0:T(8,128)}, f32[49,32,128]{2,1,0:T(8,128)}, u32[]{:S(2)}, u32[]{:S(2)}) collective-permute-start(f32[49,32,128]{2,1,0:T(8,128)} %get-tuple-element.44), channel_id=1, source_target_pairs={{0,1},{1,0},{2,3},{3,2},{4,5},{5,4},{6,7},{7,6},{8,9},{9,8},{10,11... | collective-permute-start | bytes 2408456 | tf_op jit(solution)/shard_map/ppermute | solution.py:607
  16.0 26.2 %collective-permute-start.9 = (f32[49,32,128]{2,1,0:T(8,128)}, f32[49,32,128]{2,1,0:T(8,128)}, u32[]{:S(2)}, u32[]{:S(2)}) collective-permute-start(f32[49,32,128]{2,1,0:T(8,128)} %get-tuple-element.45), channel_id=1, source_target_pairs={{1,2},{2,1},{5,6},{6,5},{9,10},{10,9},{13,14},{14,13},{17,18},{18,... | collective-permute-start | bytes 2408456 | tf_op jit(solution)/shard_map/ppermute | solution.py:607
  30.7 4.6 %collective-permute-start.7 = (f32[568,128]{1,0:T(8,128)S(1)}, f32[568,128]{1,0:T(8,128)S(1)}, u32[]{:S(2)}, u32[]{:S(2)}) collective-permute-start(f32[568,128]{1,0:T(8,128)S(1)} %get-tuple-element.42), channel_id=1, source_target_pairs={{0,4},{4,0},{8,12},{12,8},{16,20},{20,16},{24,28},{28,24},{1,5},{5... | collective-permute-start | bytes 872456 | tf_op jit(solution)/shard_map/ppermute | solution.py:536
  35.4 6.0 %collective-permute-start = (f32[568,128]{1,0:T(8,128)S(1)}, f32[568,128]{1,0:T(8,128)S(1)}, u32[]{:S(2)}, u32[]{:S(2)}) collective-permute-start(f32[568,128]{1,0:T(8,128)S(1)} %param.1), channel_id=1, source_target_pairs={{0,8},{4,20},{8,0},{12,28},{16,24},{20,4},{24,16},{28,12},{1,9},{5... | collective-permute-start | bytes 872456 | tf_op jit(solution)/shard_map/cond/branch_1_fun/ppermute | solution.py:546
  41.4 6.5 %collective-permute-start.10 = (f32[568,128]{1,0:T(8,128)S(1)}, f32[568,128]{1,0:T(8,128)S(1)}, u32[]{:S(2)}, u32[]{:S(2)}) collective-permute-start(f32[568,128]{1,0:T(8,128)S(1)} %get-tuple-element.64), channel_id=1, source_target_pairs={{0,16},{4,12},{8,24},{12,4},{16,0},{20,28},{24,8},{28,20},{1,17},{... | collective-permute-start | bytes 872456 | tf_op jit(solution)/shard_map/ppermute | solution.py:546
  47.9 11.6 %copy-start = (f32[64,32,128]{2,1,0:T(8,128)S(1)}, f32[64,32,128]{2,1,0:T(8,128)}, u32[]{:S(2)}) copy-start(f32[64,32,128]{2,1,0:T(8,128)} %get-tuple-element.51.ahead) | copy-start | bytes 3145732
  48.0 3.3 %collective-permute-start.11 = (f32[568,128]{1,0:T(8,128)S(1)}, f32[568,128]{1,0:T(8,128)S(1)}, u32[]{:S(2)}, u32[]{:S(2)}) collective-permute-start(f32[568,128]{1,0:T(8,128)S(1)} %get-tuple-element.50), channel_id=1, source_target_pairs={{0,4},{4,0},{8,12},{12,8},{16,20},{20,16},{24,28},{28,24},{1,5},{5... | collective-permute-start | bytes 872456 | tf_op jit(solution)/shard_map/ppermute | solution.py:536
  51.3 5.9 %collective-permute-start.12 = (f32[568,128]{1,0:T(8,128)S(1)}, f32[568,128]{1,0:T(8,128)S(1)}, u32[]{:S(2)}, u32[]{:S(2)}) collective-permute-start(f32[568,128]{1,0:T(8,128)S(1)} %add.85), channel_id=1, source_target_pairs={{0,8},{4,20},{8,0},{12,28},{16,24},{20,4},{24,16},{28,12},{1,9},{5... | collective-permute-start | bytes 872456 | tf_op jit(solution)/shard_map/ppermute | solution.py:546
  52.5 7.0 %collective-permute-start.13 = (f32[568,128]{1,0:T(8,128)S(1)}, f32[568,128]{1,0:T(8,128)S(1)}, u32[]{:S(2)}, u32[]{:S(2)}) collective-permute-start(f32[568,128]{1,0:T(8,128)S(1)} %add.84.own), channel_id=1, source_target_pairs={{0,4},{4,0},{8,12},{12,8},{16,20},{20,16},{24,28},{28,24},{1,5},{5... | collective-permute-start | bytes 872456 | tf_op jit(solution)/shard_map/ppermute | solution.py:554
  57.3 5.9 %collective-permute-start.14 = (f32[568,128]{1,0:T(8,128)S(1)}, f32[568,128]{1,0:T(8,128)S(1)}, u32[]{:S(2)}, u32[]{:S(2)}) collective-permute-start(f32[568,128]{1,0:T(8,128)S(1)} %add.86), channel_id=1, source_target_pairs={{0,16},{4,12},{8,24},{12,4},{16,0},{20,28},{24,8},{28,20},{1,17},{... | collective-permute-start | bytes 872456 | tf_op jit(solution)/shard_map/ppermute | solution.py:546
  63.3 4.0 %collective-permute-start.15 = (f32[568,128]{1,0:T(8,128)S(1)}, f32[568,128]{1,0:T(8,128)S(1)}, u32[]{:S(2)}, u32[]{:S(2)}) collective-permute-start(f32[568,128]{1,0:T(8,128)S(1)} %add.87.own), channel_id=1, source_target_pairs={{0,4},{4,0},{8,12},{12,8},{16,20},{20,16},{24,28},{28,24},{1,5},{5... | collective-permute-start | bytes 872456 | tf_op jit(solution)/shard_map/ppermute | solution.py:554
